TPU v7x, 128 devices: a whole 4x4x4 slice. The times are simulated.
128 devices in a mesh: shard: 2 (over x_lo), context: 16 (over z, y), tensor: 4 (over x_hi, core).
Axes of the slice: x: 4 (x_hi: 2, x_lo: 2; x = x_hi * 2 + x_lo), y: 4, z: 4, core: 2. Of those that a mesh axis runs over, the one named last changes fastest.
Arguments:
- tokens: bfloat16 [4096, 1024], P(('shard', 'context')), may hold values from -6 to 6
- segment_ids: int32 [4096], P('shard'), may hold values from 0 to 4, as said below
- w_qkv: bfloat16 [1, 1024, 3, 1024], P(None, 'shard', None, 'tensor'), may hold values from -0.1875 to 0.1875
- b_qv: bfloat16 [1, 2, 1024], P(None, None, 'tensor'), may hold values from -0.75 to 0.75
- w_out: bfloat16 [1, 1024, 1024], P(None, 'tensor', 'shard'), may hold values from -4 to 4
- w_up: bfloat16 [1, 1024, 4096], P(None, 'shard', 'tensor'), may hold values from -0.1875 to 0.1875
- b_up: bfloat16 [1, 4096], P(None, 'tensor'), may hold values from -6 to 6
- w_down: bfloat16 [1, 4096, 1024], P(None, 'tensor', 'shard'), may hold values from -0.09375 to 0.09375
- out_bias: bfloat16 [1, 2, 1024], replicated, may hold values from -6 to 6
- ln_gain: bfloat16 [1, 2, 1024], replicated, may hold values from 0.25 to 1.75
- ln_bias: bfloat16 [1, 2, 1024], replicated, may hold values from -6 to 6
- cotangent: float32 [4096, 1024], P(('shard', 'context')), may hold values from -6 to 6
Outputs:
- hidden_out: float32 [4096, 1024], P(('shard', 'context', 'tensor'))
- grad_tokens: float32 [4096, 1024], P(('shard', 'context', 'tensor'))
- grad_w_qkv: float32 [1, 1024, 3, 1024], P(None, 'shard', None, 'tensor')
- grad_w_out: float32 [1, 1024, 1024], P(None, 'tensor', 'shard')
- grad_w_up: float32 [1, 1024, 4096], P(None, 'shard', 'tensor')
- grad_w_down: float32 [1, 4096, 1024], P(None, 'tensor', 'shard')
- grad_b_qv: float32 [1, 2, 1024], P(None, None, 'tensor')
- grad_b_up: float32 [1, 4096], P(None, 'tensor')
- grad_out_bias: float32 [1, 2, 1024], P(None, None, 'tensor')
- grad_ln_gain: float32 [1, 2, 1024], P(None, None, 'tensor')
- grad_ln_bias: float32 [1, 2, 1024], P(None, None, 'tensor')
Inputs may be any that keep to these rules, and one draw needn't show every extreme that they name: `segment_ids`: within each sequence the ids never fall; they begin at 0 and end at 4; one document starts in the first block of 128 tokens and ends in the last.
All inputs are finite; a program needn't handle non-finite values.
Results may differ from a plain program's by a relative error of at most 0.023.
Values may be sent and summed in bfloat16 or wider, within the bound.
No kernel may reach another device: no remote copies, remote signals or barrier semaphores. Data moves between devices by JAX's collectives and lax.ppermute only.
A program may use at most 64 MiB of HBM per device.

v0:
```python
import math

import jax
import jax.numpy as jnp
from jax import lax
from jax.sharding import PartitionSpec as P

HD = 64
LAYERS = 1


EPSILON = 1e-05
NEGATIVE = -1e30
ROOT_HALF = 0.7071067811865476
DENSITY = 0.3989422804014327


def norm_rows(summed, gain, shift):
    centred = summed - jnp.mean(summed, axis=-1, keepdims=True)
    factor = lax.rsqrt(jnp.mean(centred * centred, axis=-1, keepdims=True) + EPSILON)
    normed = centred * factor
    return (normed * gain + shift, normed, factor)


def norm_back(incoming, normed, factor, gain):
    scaled = incoming * gain
    centre = jnp.mean(scaled, axis=-1, keepdims=True)
    along = jnp.mean(scaled * normed, axis=-1, keepdims=True)
    return factor * (scaled - centre - normed * along)


def gelu(value):
    return 0.5 * value * (1.0 + lax.erf(value * ROOT_HALF))


def gelu_slope(value):
    return 0.5 * (1.0 + lax.erf(value * ROOT_HALF)) + value * DENSITY * jnp.exp(
        -0.5 * value * value
    )


def head_scores(queries, keys):
    return jnp.einsum("qhd,khd->hqk", queries, keys, preferred_element_type=jnp.float32) * HD ** (
        -0.5
    )


def pair_grads(queries, query_ids, d_out, logsum, delta, key_rows, value_rows, key_ids):
    allowed = query_ids[:, None] == key_ids[None, :]
    probs = jnp.where(allowed, jnp.exp(head_scores(queries, key_rows) - logsum[:, :, None]), 0.0)
    d_probs = jnp.einsum("qhd,khd->hqk", d_out, value_rows, preferred_element_type=jnp.float32)
    d_scores = (probs * (d_probs - delta[:, :, None])).astype(jnp.bfloat16)
    return (probs, d_scores)


def attend(queries, query_ids, sequence_ids, block, carry, piece):
    keys, values = piece
    width = math.gcd(keys.shape[0], block)

    def step(index, inner):
        highest, totals, running = inner
        offset = index * width
        key_rows = lax.dynamic_slice_in_dim(keys, offset, width, 0).reshape(width, -1, HD)
        value_rows = lax.dynamic_slice_in_dim(values, offset, width, 0).reshape(width, -1, HD)
        key_ids = lax.dynamic_slice_in_dim(sequence_ids, offset, width, 0)
        allowed = query_ids[:, None] == key_ids[None, :]
        scores = head_scores(queries, key_rows)
        raised = jnp.maximum(highest, jnp.max(jnp.where(allowed, scores, NEGATIVE), axis=-1))
        weights = jnp.where(allowed, jnp.exp(scores - raised[:, :, None]), 0.0)
        factor = jnp.exp(highest - raised)
        totals = totals * factor + jnp.sum(weights, axis=-1)
        running = running * factor[:, :, None] + jnp.einsum(
            "hqk,khd->hqd", weights, value_rows.astype(jnp.float32)
        )
        return (raised, totals, running)

    return lax.fori_loop(0, keys.shape[0] // width, step, carry)


def spread_out(partial_value):
    result = lax.psum(partial_value.astype(jnp.bfloat16), "tensor").astype(jnp.float32)
    return result


def grad_spread(partial_value):
    result = lax.psum(partial_value.astype(jnp.bfloat16), "tensor").astype(jnp.float32)
    return result


def end_rows(rows, row_at, share):
    result = lax.dynamic_slice_in_dim(rows, row_at, share, 0)
    return result


def own_columns(stacked, columns):
    result = lax.dynamic_slice_in_dim(stacked, lax.axis_index("tensor") * columns, columns, 2)
    return result


def shards(
    tokens,
    segment_ids,
    w_qkv,
    b_qv,
    w_out,
    w_up,
    b_up,
    w_down,
    out_bias,
    ln_gain,
    ln_bias,
    cotangent,
):
    tensor_count = lax.axis_size("tensor")
    block = tokens.shape[0]
    share = block // tensor_count
    columns = tokens.shape[1] // tensor_count
    row_at = lax.axis_index("tensor") * share
    query_ids = lax.dynamic_slice_in_dim(segment_ids, lax.axis_index("context") * block, block, 0)
    length = segment_ids.shape[0]
    stream = tokens.astype(jnp.float32)
    wide = tokens
    layer = 0
    weight_in = lax.all_gather(w_qkv[layer], "shard", axis=0, tiled=True)
    weight_out = lax.all_gather(w_out[layer], "shard", axis=1, tiled=True)
    weight_up = lax.all_gather(w_up[layer], "shard", axis=0, tiled=True)
    weight_down = lax.all_gather(w_down[layer], "shard", axis=1, tiled=True)
    mixed = jnp.einsum("td,dcj->tcj", wide, weight_in, preferred_element_type=jnp.float32)
    biases = b_qv[layer].astype(jnp.float32)
    queries = (mixed[:, 0] + biases[0]).astype(jnp.bfloat16)
    keys = mixed[:, 1].astype(jnp.bfloat16)
    values = (mixed[:, 2] + biases[1]).astype(jnp.bfloat16)
    heads_q = queries.reshape(block, -1, HD)
    heads = heads_q.shape[1]
    start_carry = (
        jnp.full((heads, block), NEGATIVE, jnp.float32),
        jnp.zeros((heads, block), jnp.float32),
        jnp.zeros((heads, block, HD), jnp.float32),
    )
    highest, totals, running = attend(
        heads_q,
        query_ids,
        segment_ids,
        block,
        start_carry,
        (
            lax.all_gather(keys, "context", axis=0, tiled=True),
            lax.all_gather(values, "context", axis=0, tiled=True),
        ),
    )
    context = running / totals[:, :, None]
    logsum = highest + jnp.log(totals)
    context_low = jnp.transpose(context, (1, 0, 2)).reshape(block, -1).astype(jnp.bfloat16)
    partial_value = jnp.dot(context_low, weight_out, preferred_element_type=jnp.float32)
    gains = ln_gain[layer].astype(jnp.float32)
    shifts = ln_bias[layer].astype(jnp.float32)
    extra = out_bias[layer].astype(jnp.float32)
    middle, normed_a, factor_a = norm_rows(
        stream + (spread_out(partial_value) + extra[0]), gains[0], shifts[0]
    )
    wide_mid = middle.astype(jnp.bfloat16)
    before = jnp.dot(wide_mid, weight_up, preferred_element_type=jnp.float32) + b_up[layer].astype(
        jnp.float32
    )
    after = gelu(before).astype(jnp.bfloat16)
    second = jnp.dot(after, weight_down, preferred_element_type=jnp.float32)
    stream, normed_b, factor_b = norm_rows(
        middle + (spread_out(second) + extra[1]), gains[1], shifts[1]
    )
    saved = [
        (
            wide,
            weight_in,
            weight_out,
            weight_up,
            weight_down,
            heads_q,
            keys,
            values,
            context,
            logsum,
            context_low,
            normed_a,
            factor_a,
            wide_mid,
            before,
            after,
            normed_b,
            factor_b,
        )
    ]
    hidden_out = end_rows(stream, row_at, share)
    grad = cotangent
    grads_in, grads_out, grads_up, grads_down, grads_qv, grads_bup, grads_norm = (
        [],
        [],
        [],
        [],
        [],
        [],
        [],
    )
    for layer in reversed(range(LAYERS)):
        (
            wide,
            weight_in,
            weight_out,
            weight_up,
            weight_down,
            heads_q,
            keys,
            values,
            context,
            logsum,
            context_low,
            normed_a,
            factor_a,
            wide_mid,
            before,
            after,
            normed_b,
            factor_b,
        ) = saved[layer]
        gains = ln_gain[layer].astype(jnp.float32)
        gain_second = jnp.sum(grad * normed_b, axis=0)
        shift_second = jnp.sum(grad, axis=0)
        d_second = norm_back(grad, normed_b, factor_b, gains[1])
        low_second = d_second.astype(jnp.bfloat16)
        bias_second = jnp.sum(low_second.astype(jnp.float32), axis=0)
        grads_down.append(
            jnp.einsum("tf,td->fd", after, low_second, preferred_element_type=jnp.float32)
        )
        d_after = jnp.einsum(
            "td,fd->tf", low_second, weight_down, preferred_element_type=jnp.float32
        )
        d_before = (d_after * gelu_slope(before)).astype(jnp.bfloat16)
        grads_bup.append(jnp.sum(d_before.astype(jnp.float32), axis=0))
        grads_up.append(
            jnp.einsum("td,tf->df", wide_mid, d_before, preferred_element_type=jnp.float32)
        )
        d_middle = d_second + grad_spread(
            jnp.einsum("tf,df->td", d_before, weight_up, preferred_element_type=jnp.float32)
        )
        gain_first = jnp.sum(d_middle * normed_a, axis=0)
        shift_first = jnp.sum(d_middle, axis=0)
        d_first = norm_back(d_middle, normed_a, factor_a, gains[0])
        low_first = d_first.astype(jnp.bfloat16)
        bias_first = jnp.sum(low_first.astype(jnp.float32), axis=0)
        grads_out.append(
            jnp.einsum("tj,td->jd", context_low, low_first, preferred_element_type=jnp.float32)
        )
        d_context = (
            jnp.einsum("td,jd->tj", low_first, weight_out, preferred_element_type=jnp.float32)
            .astype(jnp.bfloat16)
            .reshape(block, -1, HD)
        )
        d_context_wide = d_context.astype(jnp.float32)
        delta = jnp.einsum("qhd,hqd->hq", d_context_wide, context)
        all_keys, all_values = (
            lax.all_gather(keys, "context", axis=0, tiled=True),
            lax.all_gather(values, "context", axis=0, tiled=True),
        )

        def query_step(index, total_grad):
            offset = index * block
            key_rows = lax.dynamic_slice_in_dim(all_keys, offset, block, 0).reshape(block, -1, HD)
            value_rows = lax.dynamic_slice_in_dim(all_values, offset, block, 0).reshape(
                block, -1, HD
            )
            key_ids = lax.dynamic_slice_in_dim(segment_ids, offset, block, 0)
            probs, d_scores = pair_grads(
                heads_q, query_ids, d_context, logsum, delta, key_rows, value_rows, key_ids
            )
            term = jnp.einsum(
                "hqk,khd->qhd", d_scores, key_rows, preferred_element_type=jnp.float32
            )
            return total_grad + term * HD ** (-0.5)

        d_query = lax.fori_loop(
            0, length // block, query_step, jnp.zeros(heads_q.shape, jnp.float32)
        )
        width = math.gcd(block * lax.axis_size("context"), block)

        def one_block(index):
            offset = index * width
            key_rows = lax.dynamic_slice_in_dim(all_keys, offset, width, 0).reshape(width, -1, HD)
            value_rows = lax.dynamic_slice_in_dim(all_values, offset, width, 0).reshape(
                width, -1, HD
            )
            key_ids = lax.dynamic_slice_in_dim(segment_ids, offset, width, 0)
            probs, d_scores = pair_grads(
                heads_q, query_ids, d_context, logsum, delta, key_rows, value_rows, key_ids
            )
            d_key = jnp.einsum(
                "hqk,qhd->khd", d_scores, heads_q, preferred_element_type=jnp.float32
            ) * HD ** (-0.5)
            d_value = jnp.einsum("hqk,qhd->khd", probs, d_context_wide)
            return jnp.stack([d_key.reshape(width, -1), d_value.reshape(width, -1)], axis=1)

        terms = lax.map(
            one_block, jnp.arange(block * lax.axis_size("context") // width, dtype=jnp.int32)
        )
        d_pairs = lax.psum_scatter(
            terms.reshape(block * lax.axis_size("context"), 2, -1).astype(jnp.bfloat16),
            "context",
            scatter_dimension=0,
            tiled=True,
        ).astype(jnp.float32)
        d_mixed = jnp.stack(
            [d_query.reshape(block, -1), d_pairs[:, 0], d_pairs[:, 1]], axis=1
        ).astype(jnp.bfloat16)
        d_mixed_wide = d_mixed.astype(jnp.float32)
        grads_qv.append(
            jnp.stack([jnp.sum(d_mixed_wide[:, 0], axis=0), jnp.sum(d_mixed_wide[:, 2], axis=0)])
        )
        grads_in.append(
            jnp.einsum("td,tcj->dcj", wide, d_mixed, preferred_element_type=jnp.float32)
        )
        grads_norm.append(
            jnp.stack([bias_first, bias_second, gain_first, gain_second, shift_first, shift_second])
        )
        grad = d_first + grad_spread(
            jnp.einsum("tcj,dcj->td", d_mixed, weight_in, preferred_element_type=jnp.float32)
        )
    grad_tokens = end_rows(grad, row_at, share)
    stacked_in = jnp.stack(grads_in[::-1])
    stacked_out = jnp.stack(grads_out[::-1])
    stacked_up = jnp.stack(grads_up[::-1])
    stacked_down = jnp.stack(grads_down[::-1])
    shard_in, shard_out, shard_up, shard_down = (
        lax.psum_scatter(
            stacked_in.astype(jnp.bfloat16), "shard", scatter_dimension=1, tiled=True
        ).astype(jnp.float32),
        lax.psum_scatter(
            stacked_out.astype(jnp.bfloat16), "shard", scatter_dimension=2, tiled=True
        ).astype(jnp.float32),
        lax.psum_scatter(
            stacked_up.astype(jnp.bfloat16), "shard", scatter_dimension=1, tiled=True
        ).astype(jnp.float32),
        lax.psum_scatter(
            stacked_down.astype(jnp.bfloat16), "shard", scatter_dimension=2, tiled=True
        ).astype(jnp.float32),
    )
    grad_w_qkv, grad_w_out, grad_w_up, grad_w_down = (
        lax.psum(shard_in.astype(jnp.bfloat16), "context").astype(jnp.float32),
        lax.psum(shard_out.astype(jnp.bfloat16), "context").astype(jnp.float32),
        lax.psum(shard_up.astype(jnp.bfloat16), "context").astype(jnp.float32),
        lax.psum(shard_down.astype(jnp.bfloat16), "context").astype(jnp.float32),
    )
    norm_columns = own_columns(jnp.stack(grads_norm[::-1]), columns)
    grad_b_qv, grad_b_up, norm_totals = lax.psum(
        (jnp.stack(grads_qv[::-1]), jnp.stack(grads_bup[::-1]), norm_columns), ("shard", "context")
    )
    return (
        hidden_out,
        grad_tokens,
        grad_w_qkv,
        grad_w_out,
        grad_w_up,
        grad_w_down,
        grad_b_qv,
        grad_b_up,
        norm_totals[:, 0:2],
        norm_totals[:, 2:4],
        norm_totals[:, 4:6],
    )


def solution(mesh):
    in_specs = (
        P(("shard", "context"), None),
        P("shard"),
        P(None, "shard", None, "tensor"),
        P(None, None, "tensor"),
        P(None, "tensor", "shard"),
        P(None, "shard", "tensor"),
        P(None, "tensor"),
        P(None, "tensor", "shard"),
        P(),
        P(),
        P(),
        P(("shard", "context"), None),
    )
    out_specs = (
        P(("shard", "context", "tensor"), None),
        P(("shard", "context", "tensor"), None),
        P(None, "shard", None, "tensor"),
        P(None, "tensor", "shard"),
        P(None, "shard", "tensor"),
        P(None, "tensor", "shard"),
        P(None, None, "tensor"),
        P(None, "tensor"),
        P(None, None, "tensor"),
        P(None, None, "tensor"),
        P(None, None, "tensor"),
    )
    return jax.shard_map(shards, mesh=mesh, in_specs=in_specs, out_specs=out_specs, check_vma=False)
```

profile of v0, /device:TPU:0, one launch (start us, length us, event | category | flops | bytes accessed | tf_op | source)
XLA Modules:
  0.0 871.2 jit_solution(14308619757996558183)
XLA Ops:
  8.0 33.9 %all-gather.13.cloned.1.call-done = bf16[1,1024,3,256]{3,1,2,0:T(8,128)(2,1)} async-done(((bf16[1,512,3,256]{3,1,2,0:T(8,128)(2,1)}), bf16[1,1024,3,256]{3,1,2,0:T(8,128)(2,1)}) %all-gather.13.cloned.1.call-update) | async-done | bytes 1572880 | tf_op jit(solution)/shard_map/all_gather | solution.py:124
  41.9 1.9 fusion.45
  45.4 1.3 dynamic_slice.67
  46.7 8.7 all-gather.2
  55.6 32.9 %all-gather.15.cloned.1.call-done = bf16[2048,1,256]{2,0,1:T(8,128)(2,1)} async-done(((bf16[128,1,256]{2,0,1:T(8,128)(2,1)}), bf16[2048,1,256]{2,0,1:T(8,128)(2,1)}) %all-gather.15.cloned.1.call-update) | async-done | bytes 1048592 | tf_op jit(solution)/shard_map/all_gather | solution.py:147
  88.5 1.5 copy.41
  90.0 43.4 %all-gather.11.cloned.1.call-done = bf16[2048,256]{1,0:T(8,128)(2,1)} async-done(((bf16[128,256]{1,0:T(8,128)(2,1)}), bf16[2048,256]{1,0:T(8,128)(2,1)}) %all-gather.11.cloned.1.call-update) | async-done | bytes 1048592 | tf_op jit(solution)/shard_map/all_gather | solution.py:148
  133.4 2.3 copy.42
  135.6 47.5 %while.43 = (s32[]{:T(128)}, f32[4,128]{1,0:T(4,128)S(1)}, f32[4,128]{1,0:T(4,128)S(1)}, f32[4,128,64]{1,2,0:T(8,128)S(1)}, s32[128]{0:T(128)}, /*index=5*/s32[2...) while((s32[]{:T(128)}, f32[4,128]{1,0:T(4,128)S(1)}, ...), condition=%wide.region_3.4_spmd.clone, body=%wide.region_0.3_spmd.clone.sunk | while | flops 17418760 | bytes 1607879 | solution.py:77
  183.2 1.0 convolution_convert_fusion.2
  186.1 37.9 %all-reduce.8.cloned.1.call-done = bf16[128,1024]{1,0:T(8,128)(2,1)} async-done(((bf16[128,1024]{1,0:T(8,128)(2,1)}), bf16[128,1024]{1,0:T(8,128)(2,1)}) %all-reduce.8.cloned.1.call-update) | async-done | bytes 262160 | tf_op jit(solution)/shard_map/psum | solution.py:81
  224.1 1.1 fusion.76
  225.2 1.2 multiply_reduce_fusion.5
  226.4 34.4 %all-gather.17.cloned.1.call-done = bf16[1,1024,1024]{2,1,0:T(8,128)(2,1)} async-done(((bf16[1,512,1024]{2,1,0:T(8,128)(2,1)}), bf16[1,1024,1024]{2,1,0:T(8,128)(2,1)}) %all-gather.17.cloned.1.call-update) | async-done | bytes 2097168 | tf_op jit(solution)/shard_map/all_gather | solution.py:126
  260.8 2.2 fusion.52
  263.1 36.0 %all-gather.19.cloned.1.call-done = bf16[1,1024,1024]{2,1,0:T(8,128)(2,1)} async-done(((bf16[1,1024,512]{2,1,0:T(8,128)(2,1)}), bf16[1,1024,1024]{2,1,0:T(8,128)(2,1)}) %all-gather.19.cloned.1.call-update) | async-done | bytes 2097168 | tf_op jit(solution)/shard_map/all_gather | solution.py:127
  299.1 2.8 fusion.64
  301.9 41.9 %all-reduce.10.cloned.1.call-done = bf16[128,1024]{1,0:T(8,128)(2,1)} async-done(((bf16[128,1024]{1,0:T(8,128)(2,1)}), bf16[128,1024]{1,0:T(8,128)(2,1)}) %all-reduce.10.cloned.1.call-update) | async-done | bytes 262160 | tf_op jit(solution)/shard_map/psum | solution.py:81
  343.8 1.3 fusion.87
  345.0 1.4 multiply_reduce_fusion.4
  346.5 2.0 multiply_reduce_fusion
  348.5 1.4 subtract_multiply_fusion.1
  349.9 1.5 convert_reduce_fusion.2
  351.5 1.6 fusion.61
  353.8 39.4 %all-reduce.12.cloned.1.call-done = bf16[128,1024]{1,0:T(8,128)(2,1)} async-done(((bf16[128,1024]{1,0:T(8,128)(2,1)}), bf16[128,1024]{1,0:T(8,128)(2,1)}) %all-reduce.12.cloned.1.call-update) | async-done | bytes 262160 | tf_op jit(solution)/shard_map/psum | solution.py:86
  393.2 1.9 multiply_reduce_fusion.1
  395.1 1.8 convert_reduce_fusion.1
  397.6 93.5 %while.42 = (s32[]{:T(128)}, bf16[16,128,2,256]{1,3,2,0:T(8,128)(2,1)}, s32[128]{0:T(128)}, s32[16]{0:T(128)S(1)}, s32[2048]{0:T(1024)}, /*index=5*/bf16[2048,25...) while((s32[]{:T(128)}, ...), condition=%wide.region_18.19_spmd, body=%wide.region_17.18_spmd.sunk | while | flops 34291716 | bytes 1874147 | solution.py:300
  401.2 0.9 fusion.146
  407.1 0.9 fusion.146
  412.9 0.9 fusion.146
  418.7 0.9 fusion.146
  424.6 0.9 fusion.146
  430.4 0.9 fusion.146
  436.3 0.9 fusion.146
  442.1 0.9 fusion.146
  448.0 0.9 fusion.146
  453.8 0.9 fusion.146
  459.6 0.9 fusion.146
  465.5 0.9 fusion.146
  471.3 0.9 fusion.146
  477.2 0.9 fusion.146
  483.0 0.9 fusion.146
  488.9 0.9 fusion.146
  491.1 3.9 copy.51
  495.8 1.1 fusion.48
  497.0 2.1 convert_bitcast_fusion.1
  499.4 2.1 convert_bitcast_fusion
  501.5 58.6 %while.44 = (s32[]{:T(128)}, f32[128,4,64]{0,2,1:T(8,128)S(1)}, bf16[2048,256]{0,1:T(8,128)(2,1)}, s32[128]{0:T(128)}, s32[2048]{0:T(1024)}, /*index=5*/bf16[128...) while((s32[]{:T(128)}, f32[128,4,64]{0,2,1:T(8,128)S(1)}, ...), condition=%wide.region_16.17_spmd.clone, body=%wide.region_15.16_spmd.clone.sunk | while | flops 25673736 | bytes 1415373 | solution.py:279
  516.2 0.9 constant_dynamic-slice_fusion.11
  538.1 0.9 constant_dynamic-slice_fusion.11
  560.2 9.0 %reduce-scatter.6.cloned.1.call-done = bf16[128,2,256]{2,0,1:T(8,128)(2,1)} async-done(((bf16[2048,2,256]{2,0,1:T(8,128)(2,1)}), bf16[128,2,256]{2,0,1:T(8,128)(2,1)}) %reduce-scatter.6.cloned.1.call-update) | async-done | bytes 131088 | tf_op jit(solution)/shard_map/reduce_scatter | solution.py:303
  569.2 2.7 fusion.47
  572.0 1.3 fusion.58
  573.5 14.1 %reduce-scatter.10.cloned.1.call-done = bf16[1,256,512]{2,1,0:T(8,128)(2,1)} async-done(((bf16[1,256,1024]{2,1,0:T(8,128)(2,1)}), bf16[1,256,512]{2,1,0:T(8,128)(2,1)}) %reduce-scatter.10.cloned.1.call-update) | async-done | bytes 262160 | tf_op jit(solution)/shard_map/reduce_scatter | solution.py:334
  587.6 38.4 %reduce-scatter.12.cloned.1.call-done = bf16[1,512,1024]{2,1,0:T(8,128)(2,1)} async-done(((bf16[1,1024,1024]{2,1,0:T(8,128)(2,1)}), bf16[1,512,1024]{2,1,0:T(8,128)(2,1)}) %reduce-scatter.12.cloned.1.call-update) | async-done | bytes 1048592 | tf_op jit(solution)/shard_map/reduce_scatter | solution.py:337
  626.0 37.6 %reduce-scatter.14.cloned.1.call-done = bf16[1,1024,512]{2,1,0:T(8,128)(2,1)} async-done(((bf16[1,1024,1024]{2,1,0:T(8,128)(2,1)}), bf16[1,1024,512]{2,1,0:T(8,128)(2,1)}) %reduce-scatter.14.cloned.1.call-update) | async-done | bytes 1048592 | tf_op jit(solution)/shard_map/reduce_scatter | solution.py:340
  663.6 32.7 %reduce-scatter.8.cloned.1.call-done = bf16[1,512,3,256]{1,3,2,0:T(8,128)(2,1)} async-done(((bf16[1,1024,3,256]{1,3,2,0:T(8,128)(2,1)}), bf16[1,512,3,256]{1,3,2,0:T(8,128)(2,1)}) %reduce-scatter.8.cloned.1.call-update) | async-done | bytes 786448 | tf_op jit(solution)/shard_map/reduce_scatter | solution.py:331
  696.3 1.6 fusion.79
  698.0 157.9 %all-reduce = (f32[1,2,256]{2,1,0:T(2,128)}, f32[1,1024]{1,0:T(1,128)}, f32[1,6,256]{2,1,0:T(8,128)S(1)}) all-reduce(f32[1,2,256]{2,1,0:T(2,128)S(1)} %maximum_bitcast_fusion.1, f32[1,1024]{1,0:T(1,128)S(1)} %bitcast.270, ...), channel_id=1, replica_groups=mesh['shard'=2,'context'=16,'tensor'=4] {'shard','context'}, use_global_device_ids=true, to_apply=%region_31.32 | all-reduce | flops 3072 | bytes 24576 | tf_op jit(solution)/shard_map/psum | solution.py:351
  856.5 1.5 dynamic-slice_add_fusion
  858.0 2.7 copy.54
  861.5 1.6 convert_element_type.204
  863.1 1.6 convert_element_type.207
  (476 shorter events, 179.0 us)
Async XLA Ops:
  7.2 37.3 %copy-start.32 = (bf16[1,2,256]{2,1,0:T(2,128)(2,1)S(1)}, bf16[1,2,256]{2,1,0:T(2,128)(2,1)}, u32[]{:S(2)}) copy-start(bf16[1,2,256]{2,1,0:T(2,128)(2,1)} %param.21) | copy-start | bytes 3076
  7.2 39.5 %copy-start.13 = (bf16[1,256,512]{2,1,0:T(8,128)(2,1)S(1)}, bf16[1,256,512]{2,1,0:T(8,128)(2,1)}, u32[]{:S(2)}) copy-start(bf16[1,256,512]{2,1,0:T(8,128)(2,1)} %param.22) | copy-start | bytes 786436
  7.2 34.7 %all-gather.13.cloned.1.call-start = ((), (), s32[]{:S(2)}) async-start(), calls=%async_computation.15 | async-start | bytes 2359296 | tf_op jit(solution)/shard_map/all_gather | solution.py:124
  7.9 80.6 %all-gather.15.cloned.1.call-start = ((), (), s32[]{:S(2)}) async-start(), calls=%async_computation.16 | async-start | bytes 1114112 | tf_op jit(solution)/shard_map/all_gather | solution.py:147
  44.4 88.9 %all-gather.11.cloned.1.call-start = ((), (), s32[]{:S(2)}) async-start(), calls=%async_computation.5 | async-start | bytes 1114112 | tf_op jit(solution)/shard_map/all_gather | solution.py:148
  45.2 178.9 %all-reduce.8.cloned.1.call-start = ((), (), s32[]{:S(2)}) async-start(), calls=%async_computation.6 | async-start | bytes 524288 | tf_op jit(solution)/shard_map/psum | solution.py:81
  183.1 77.7 %copy-start.5 = (bf16[2048,256]{0,1:T(8,128)(2,1)}, bf16[2048,256]{0,1:T(8,128)(2,1)S(1)}, u32[]{:S(2)}) copy-start(bf16[2048,256]{0,1:T(8,128)(2,1)S(1)} %get-tuple-element.1031) | copy-start | bytes 3145732
  183.1 2.3 copy-start.33
  183.2 2.3 copy-start.29
  183.2 2.3 copy-start.30
  183.2 2.4 copy-start.31
  183.2 40.9 %copy-start = (bf16[128,1024]{1,0:T(8,128)(2,1)S(1)}, bf16[128,1024]{1,0:T(8,128)(2,1)}, u32[]{:S(2)}) copy-start(bf16[128,1024]{1,0:T(8,128)(2,1)} %param.18) | copy-start | bytes 786436
  183.2 43.1 %copy-start.11 = (bf16[4,128,64]{1,2,0:T(8,128)(2,1)}, bf16[4,128,64]{1,2,0:T(8,128)(2,1)S(1)}, u32[]{:S(2)}) copy-start(bf16[4,128,64]{1,2,0:T(8,128)(2,1)S(1)} %fusion.86) | copy-start | bytes 196612
  184.2 76.6 %all-gather.17.cloned.1.call-start = ((), (), s32[]{:S(2)}) async-start(), calls=%async_computation.17 | async-start | bytes 3145728 | tf_op jit(solution)/shard_map/all_gather | solution.py:126
  184.8 114.2 %all-gather.19.cloned.1.call-start = ((), (), s32[]{:S(2)}) async-start(), calls=%async_computation.18 | async-start | bytes 3145728 | tf_op jit(solution)/shard_map/all_gather | solution.py:127
  185.4 158.4 %all-reduce.10.cloned.1.call-start = ((), (), s32[]{:S(2)}) async-start(), calls=%async_computation.7 | async-start | bytes 524288 | tf_op jit(solution)/shard_map/psum | solution.py:81
  185.5 163.0 %copy-start.15 = (f32[1,1,1024]{2,1,0:T(1,128)}, f32[1,1,1024]{2,1,0:T(1,128)S(1)}, u32[]{:S(2)}) copy-start(f32[1,1,1024]{2,1,0:T(1,128)S(1)} %get-tuple-element.651) | copy-start | bytes 12292
  225.2 168.0 %copy-start.17 = (f32[128]{0:T(128)}, f32[128]{0:T(128)S(1)}, u32[]{:S(2)}) copy-start(f32[128]{0:T(128)S(1)} %broadcast_multiply_fusion.5) | copy-start | bytes 1540
  226.4 166.8 %copy-start.19 = (f32[128]{0:T(128)}, f32[128]{0:T(128)S(1)}, u32[]{:S(2)}) copy-start(f32[128]{0:T(128)S(1)} %add_rsqrt_fusion.1) | copy-start | bytes 1540
  263.1 80.7 %copy-start.1 = (bf16[128,1024]{1,0:T(8,128)(2,1)S(1)}, bf16[128,1024]{1,0:T(8,128)(2,1)}, u32[]{:S(2)}) copy-start(bf16[128,1024]{1,0:T(8,128)(2,1)} %all-reduce.8.cloned.1.call-done) | copy-start | bytes 786436
  263.1 83.4 %copy-start.7 = (f32[128,1024]{1,0:T(8,128)S(1)}, f32[128,1024]{1,0:T(8,128)}, u32[]{:S(2)}) copy-start(f32[128,1024]{1,0:T(8,128)} %param.29) | copy-start | bytes 1572868
  301.8 91.4 %all-reduce.12.cloned.1.call-start = ((), (), s32[]{:S(2)}) async-start(), calls=%async_computation.8 | async-start | bytes 524288 | tf_op jit(solution)/shard_map/psum | solution.py:86
  345.0 4.9 copy-start.3
  348.5 2.9 copy-start.6
  349.9 1.6 copy-start.2
  353.1 216.1 %reduce-scatter.6.cloned.1.call-start = ((), (), s32[]{:S(2)}) async-start(), calls=%async_computation.9 | async-start | bytes 2228224 | tf_op jit(solution)/shard_map/reduce_scatter | solution.py:303
  495.0 0.8 copy-start.12
  495.0 2.0 copy-start.18
  495.0 2.0 copy-start.20
  495.0 92.6 %reduce-scatter.10.cloned.1.call-start = ((), (), s32[]{:S(2)}) async-start(), calls=%async_computation.12 | async-start | bytes 786432 | tf_op jit(solution)/shard_map/reduce_scatter | solution.py:334
  496.9 129.1 %reduce-scatter.12.cloned.1.call-start = ((), (), s32[]{:S(2)}) async-start(), calls=%async_computation.13 | async-start | bytes 3145728 | tf_op jit(solution)/shard_map/reduce_scatter | solution.py:337
  499.2 164.4 %reduce-scatter.14.cloned.1.call-start = ((), (), s32[]{:S(2)}) async-start(), calls=%async_computation.14 | async-start | bytes 3145728 | tf_op jit(solution)/shard_map/reduce_scatter | solution.py:340
  501.5 194.7 %reduce-scatter.8.cloned.1.call-start = ((), (), s32[]{:S(2)}) async-start(), calls=%async_computation.11 | async-start | bytes 2359296 | tf_op jit(solution)/shard_map/reduce_scatter | solution.py:331
  560.1 11.9 %copy-start.4 = (bf16[1,1024,3,256]{3,1,2,0:T(8,128)(2,1)S(1)}, bf16[1,1024,3,256]{3,1,2,0:T(8,128)(2,1)}, u32[]{:S(2)}) copy-start(bf16[1,1024,3,256]{3,1,2,0:T(8,128)(2,1)} %all-gather.13.cloned.1.call-done) | copy-start | bytes 4718596
  569.2 2.8 copy-start.8
  572.0 284.5 %all-reduce.14.cloned.1.call-start = ((), (), s32[]{:S(2)}) async-start(), calls=%async_computation.10 | async-start | bytes 524288 | tf_op jit(solution)/shard_map/psum | solution.py:86
  573.4 122.9 %copy-start.16 = (f32[1,1,1024]{2,1,0:T(1,128)S(1)}, f32[1,1,1024]{2,1,0:T(1,128)}, u32[]{:S(2)}) copy-start(f32[1,1,1024]{2,1,0:T(1,128)} %copy-done.15) | copy-start | bytes 12292
  573.4 122.9 %copy-start.28 = (f32[1,1,1024]{2,1,0:T(1,128)S(1)}, f32[1,1,1024]{2,1,0:T(1,128)}, u32[]{:S(2)}) copy-start(f32[1,1,1024]{2,1,0:T(1,128)} %get-tuple-element.646) | copy-start | bytes 12292
  573.4 124.5 %copy-start.21 = (f32[1024]{0:T(1024)S(1)}, f32[1024]{0:T(1024)}, u32[]{:S(2)}) copy-start(f32[1024]{0:T(1024)} %get-tuple-element.552) | copy-start | bytes 12292
  573.4 124.5 %copy-start.22 = (f32[1024]{0:T(1024)S(1)}, f32[1024]{0:T(1024)}, u32[]{:S(2)}) copy-start(f32[1024]{0:T(1024)} %get-tuple-element.557) | copy-start | bytes 12292
  573.4 124.5 %copy-start.23 = (f32[1024]{0:T(1024)S(1)}, f32[1024]{0:T(1024)}, u32[]{:S(2)}) copy-start(f32[1024]{0:T(1024)} %get-tuple-element.550) | copy-start | bytes 12292
  573.4 124.5 %copy-start.24 = (f32[1024]{0:T(1024)S(1)}, f32[1024]{0:T(1024)}, u32[]{:S(2)}) copy-start(f32[1024]{0:T(1024)} %get-tuple-element.555) | copy-start | bytes 12292
  573.4 124.5 %copy-start.25 = (f32[1024]{0:T(1024)S(1)}, f32[1024]{0:T(1024)}, u32[]{:S(2)}) copy-start(f32[1024]{0:T(1024)} %get-tuple-element.558) | copy-start | bytes 12292
  573.4 124.5 %copy-start.26 = (f32[1024]{0:T(1024)S(1)}, f32[1024]{0:T(1024)}, u32[]{:S(2)}) copy-start(f32[1024]{0:T(1024)} %get-tuple-element.632) | copy-start | bytes 12292
  573.4 284.6 %all-reduce.16.cloned.1.call-start = ((), (), s32[]{:S(2)}) async-start(), calls=%async_computation.19 | async-start | bytes 6291456 | tf_op jit(solution)/shard_map/psum | solution.py:345
  696.2 1.8 copy-start.27
  858.0 2.7 copy-start.14
  858.0 3.5 copy-start.10
  860.7 2.4 copy-start.9
Sparse Core Ops, SparseCore 0:
  9.7 32.1 all-gather.12
  44.6 43.8 all-gather.14
  91.2 42.0 all-gather.10
  184.3 39.6 all-reduce.7
  225.7 35.0 all-gather.16
  262.4 36.5 all-gather.18
  302.3 41.4 all-reduce.9
  353.2 39.9 all-reduce.11
  495.1 74.0 reduce-scatter.5
  571.4 16.1 reduce-scatter.9
  590.7 35.2 reduce-scatter.11
  628.2 35.3 reduce-scatter.13
  666.6 29.5 reduce-scatter.7
  699.1 41.4 all-reduce.13
  744.8 95.9 all-reduce.15
where the time goes:
time: 878 us; the launch traced here: 871 us
  waiting for transfers between devices  433 us (49%)
  blocking collectives  167 us (19%)
  local copies, waits for them, and re-layouts  104 us (12%)
  matrix products  70.9 us (8%)
  other arithmetic  68.7 us (8%)
  between operations  14.5 us (2%)
  loops' own time  12.7 us (1%)
    psum x1, blocking collectives, shards(): lax.psum((jnp.stack(grads_qv[::-1]), jnp.stack(grads_bup[::-1]), norm_col...  158 us
    psum x2, waiting for transfers between devices, spread_out(): lax.psum(partial_value.astype(jnp.bfloat16), 'tensor').astype(jnp.float32)  79.8 us
    all_gather x1, waiting for transfers between devices, shards(): lax.all_gather(values, 'context', axis=0, tiled=True)  43.4 us
    psum x2, waiting for transfers between devices, grad_spread(): lax.psum(partial_value.astype(jnp.bfloat16), 'tensor').astype(jnp.float32)  39.4 us
    reduce_scatter x1, waiting for transfers between devices, shards(): lax.psum_scatter(stacked_up.astype(jnp.bfloat16), 'shard', scatter_dimens...  38.4 us
    reduce_scatter x1, waiting for transfers between devices, shards(): lax.psum_scatter(stacked_down.astype(jnp.bfloat16), 'shard', scatter_dime...  37.6 us
    all_gather x1, waiting for transfers between devices, shards(): weight_down = lax.all_gather(w_down[layer], 'shard', axis=1, tiled=True)  36 us
    all_gather x1, waiting for transfers between devices, shards(): weight_up = lax.all_gather(w_up[layer], 'shard', axis=0, tiled=True)  34.4 us
  transfers between devices with their start and end apart: 15, of which 13 were waited for; matrix products, arithmetic and copies ran while one was open for 9% of the time, Pallas kernels for 0%

commit v1 on v0

v1 whole, which is shorter than its diff:
```python
import functools

import jax
import jax.numpy as jnp
from jax import lax
from jax.experimental import pallas as pl
from jax.experimental.pallas import tpu as pltpu
from jax.sharding import PartitionSpec as P

HD = 64
HEADS = 4
BLK = 128
LEN = 2048
D = 1024
HALF = 512
COLS = 256
UNITS = 1024
RING = 16
EPSILON = 1e-05
NEGATIVE = -1e30
ROOT_HALF = 0.7071067811865476
DENSITY = 0.3989422804014327
BF = jnp.bfloat16
F32 = jnp.float32

NN = (((1,), (0,)), ((), ()))
NT = (((1,), (1,)), ((), ()))
TN = (((0,), (0,)), ((), ()))


def mm(a, b, dims=NN):
    return lax.dot_general(a, b, dims, preferred_element_type=F32)


def call(kernel, outs, scalars, *args, scratch=(), vmem=40):
    specs = [pl.BlockSpec(memory_space=pltpu.SMEM)]
    specs += [pl.BlockSpec(memory_space=pltpu.VMEM)] * len(args)
    return pl.pallas_call(
        kernel,
        out_shape=[jax.ShapeDtypeStruct(shape, dtype) for shape, dtype in outs],
        in_specs=specs,
        out_specs=[pl.BlockSpec(memory_space=pltpu.VMEM)] * len(outs),
        scratch_shapes=list(scratch),
        compiler_params=pltpu.CompilerParams(vmem_limit_bytes=vmem << 20),
    )(scalars, *args)


def half_at(shard, own):
    return pl.ds(pl.multiple_of((shard if own else 1 - shard) * HALF, HALF), HALF)


def by_head(rows):
    lane = lax.broadcasted_iota(jnp.int32, rows.shape, 1) // HD
    return jnp.concatenate(
        [jnp.where(lane == head, rows, jnp.zeros_like(rows)) for head in range(HEADS)], axis=0
    )


def norm_rows(summed, gain, shift):
    centred = summed - jnp.mean(summed, axis=-1, keepdims=True)
    factor = lax.rsqrt(jnp.mean(centred * centred, axis=-1, keepdims=True) + EPSILON)
    normed = centred * factor
    return normed * gain + shift, normed, factor


def norm_back(incoming, normed, factor, gain):
    scaled = incoming * gain
    centre = jnp.mean(scaled, axis=-1, keepdims=True)
    along = jnp.mean(scaled * normed, axis=-1, keepdims=True)
    return factor * (scaled - centre - normed * along)


def split_rows(place, rows_ref, mine_ref, theirs_ref):
    core = place[2]
    for part in range(2):
        mine = pl.multiple_of(part * 64 + core * 32, 32)
        theirs = pl.multiple_of(part * 64 + (1 - core) * 32, 32)
        mine_ref[pl.ds(part * 32, 32), :] = rows_ref[pl.ds(mine, 32), :]
        theirs_ref[pl.ds(part * 32, 32), :] = rows_ref[pl.ds(theirs, 32), :].astype(BF)


def attend_kernel(
    place, x, w_own, w_oth, b_qv, id_q, id_k, wo_own, wo_oth,
    q_ref, k_ref, v_ref, o_ref, ob_ref, lse_ref, mine_ref, theirs_ref, part_ref,
):
    shard, block = place[0], place[1]
    biases = b_qv[...].astype(F32)

    @pl.loop(0, LEN // 256)
    def _(step):
        rows = pl.ds(pl.multiple_of(step * 256, 256), 256)
        x_own, x_oth = x[shard, rows, :], x[1 - shard, rows, :]
        k_ref[rows, :] = (mm(x_own, w_own[1]) + mm(x_oth, w_oth[1])).astype(BF)
        v_ref[rows, :] = (mm(x_own, w_own[2]) + mm(x_oth, w_oth[2]) + biases[1:2]).astype(BF)

    rows = pl.ds(pl.multiple_of(block * BLK, BLK), BLK)
    q = (mm(x[shard, rows, :], w_own[0]) + mm(x[1 - shard, rows, :], w_oth[0]) + biases[0:1]).astype(BF)
    q_ref[...] = q
    q_heads = by_head(q * BF(HD ** -0.5))
    allowed = id_q[...] == id_k[...]
    lane = lax.broadcasted_iota(jnp.int32, (BLK, COLS), 1) // HD
    out = jnp.zeros((BLK, COLS), F32)
    lse_ref[...] = jnp.zeros((1, HEADS * BLK), F32)
    for head in range(HEADS):
        scores = mm(q_heads[head * BLK : (head + 1) * BLK], k_ref[...], NT)
        scores = jnp.where(allowed, scores, NEGATIVE)
        highest = jnp.max(scores, axis=-1, keepdims=True)
        weights = jnp.exp(scores - highest)
        total = jnp.sum(weights, axis=-1, keepdims=True)
        mixed = mm(weights.astype(BF), v_ref[...]) / total
        out = jnp.where(lane == head, mixed, out)
        column = jnp.broadcast_to(highest + jnp.log(total), (BLK, BLK))
        lse_ref[:, head * BLK : (head + 1) * BLK] = column.T[0:1, :]
    o_ref[...] = out
    low = out.astype(BF)
    ob_ref[...] = low
    part_ref[:, half_at(shard, True)] = mm(low, wo_own[...])
    part_ref[:, half_at(shard, False)] = mm(low, wo_oth[...])
    split_rows(place, part_ref, mine_ref, theirs_ref)


def first_norm_kernel(place, tokens, chip, recv, extra, gain, shift, h_ref, n_ref, f_ref, hb_ref):
    core = place[2]
    for part in range(2):
        rows = pl.ds(part * 32, 32)
        here = tokens[pl.ds(pl.multiple_of(part * 64 + core * 32, 32), 32), :].astype(F32)
        summed = here + (chip[rows, :] + recv[rows, :].astype(F32) + extra[0:1, :].astype(F32))
        middle, normed, factor = norm_rows(
            summed, gain[0:1, :].astype(F32), shift[0:1, :].astype(F32)
        )
        h_ref[rows, :] = middle
        n_ref[rows, :] = normed
        f_ref[rows, :] = jnp.broadcast_to(factor, (32, 128))
        hb_ref[rows, :] = middle.astype(BF)


def up_down_kernel(
    place, hb, up_own, down_own, other, b_up, ub_ref, slope_ref, mine_ref, theirs_ref, part_ref
):
    shard, core = place[0], place[2]
    own, oth = hb[:, half_at(shard, True)], hb[:, half_at(shard, False)]
    for side in range(2):
        cols = pl.ds(side * HALF, HALF)
        weight = other[:, side * 32 : side * 32 + 32, :].reshape(HALF, HALF)
        before = mm(own, up_own[:, cols]) + mm(oth, weight) + b_up[:, cols].astype(F32)
        bell = 0.5 * (1.0 + lax.erf(before * ROOT_HALF))
        ub_ref[:, cols] = (before * bell).astype(BF)
        slope_ref[:, cols] = bell + before * DENSITY * jnp.exp(-0.5 * before * before)
    after = ub_ref[...]
    part_ref[:, half_at(shard, True)] = mm(after, down_own[...])
    part_ref[:, half_at(shard, False)] = mm(after, other[:, 64:128, :].reshape(UNITS, HALF))
    mine_ref[...] = part_ref[pl.ds(pl.multiple_of(core * 64, 64), 64), :]
    theirs_ref[...] = part_ref[pl.ds(pl.multiple_of((1 - core) * 64, 64), 64), :].astype(BF)


def second_norm_kernel(
    place, middle, chip, recv, extra, gain, shift, cot, out_ref, dx_ref, dz_ref, sums_ref, keep
):
    core, far = place[2], place[3]
    gains = gain[1:2, :].astype(F32)
    summed = middle[...] + (chip[...] + recv[...].astype(F32) + extra[1:2, :].astype(F32))
    hidden, normed, factor = norm_rows(summed, gains, shift[1:2, :].astype(F32))
    keep[...] = hidden
    out_ref[...] = keep[pl.ds(pl.multiple_of(far * 32, 32), 32), :]
    grad = jnp.concatenate(
        [cot[pl.ds(pl.multiple_of(part * 64 + core * 32, 32), 32), :] for part in range(2)], axis=0
    )
    back = norm_back(grad, normed, factor, gains)
    dx_ref[...] = back
    low = back.astype(BF)
    dz_ref[...] = low
    sums_ref[0:1, :] = jnp.sum(low.astype(F32), axis=0, keepdims=True)
    sums_ref[1:2, :] = jnp.sum(grad * normed, axis=0, keepdims=True)
    sums_ref[2:3, :] = jnp.sum(grad, axis=0, keepdims=True)
    sums_ref[3:8, :] = jnp.zeros((5, D), F32)


def down_up_kernel(
    place, dz, slope, up_own, down_own, other, da_ref, mine_ref, theirs_ref, part_ref
):
    shard, core = place[0], place[2]
    own, oth = dz[:, half_at(shard, True)], dz[:, half_at(shard, False)]
    after = mm(own, down_own[...], NT) + mm(oth, other[:, 64:128, :].reshape(UNITS, HALF), NT)
    da_ref[...] = (after * slope[...]).astype(BF)
    before = da_ref[...]
    part_ref[:, half_at(shard, True)] = mm(before, up_own[...], NT)
    part_ref[:, half_at(shard, False)] = mm(
        before[:, 0:HALF], other[:, 0:32, :].reshape(HALF, HALF), NT
    ) + mm(before[:, HALF:UNITS], other[:, 32:64, :].reshape(HALF, HALF), NT)
    mine_ref[...] = part_ref[pl.ds(pl.multiple_of(core * 64, 64), 64), :]
    theirs_ref[...] = part_ref[pl.ds(pl.multiple_of((1 - core) * 64, 64), 64), :].astype(BF)


def unit_grads_kernel(place, hb, da, ub, dz, pair_fwd, pair_bwd, out_ref):
    shard = place[0]
    rows = jnp.concatenate([hb[:, half_at(shard, True)], pair_fwd[:, 256:768]], axis=0)
    units = jnp.concatenate([da[...], pair_bwd[:, 512:1536]], axis=0)
    out_ref[0:512, :] = mm(rows, units, TN).astype(BF)
    total = jnp.sum(units.astype(F32), axis=0, keepdims=True)
    out_ref[1024:1040, :] = jnp.broadcast_to(total, (16, UNITS)).astype(BF)
    after = jnp.concatenate([ub[...], pair_fwd[:, 768:1792]], axis=0)
    grads = jnp.concatenate([dz[:, half_at(shard, True)], pair_bwd[:, 0:512]], axis=0)
    for side in range(2):
        cols = slice(side * HALF, side * HALF + HALF)
        out_ref[512:1024, cols] = mm(after[:, cols], grads, TN).astype(BF)


def first_back_kernel(
    place, dx, chip, recv, normed, factor, gain, sums_in, d_ref, low_ref, sums_ref
):
    grad = dx[...] + (chip[...] + recv[...].astype(F32))
    back = norm_back(grad, normed[...], factor[:, 0:1], gain[0:1, :].astype(F32))
    d_ref[...] = back
    low = back.astype(BF)
    low_ref[...] = low
    sums_ref[...] = sums_in[...]
    sums_ref[3:4, :] = jnp.sum(low.astype(F32), axis=0, keepdims=True)
    sums_ref[4:5, :] = jnp.sum(grad * normed[...], axis=0, keepdims=True)
    sums_ref[5:6, :] = jnp.sum(grad, axis=0, keepdims=True)


def attend_back_kernel(
    place, q, k, v, o, lse, low, wo_own, wo_oth, id_q, id_k, dq_ref, dkv_ref, nat_ref, acc_ref
):
    shard = place[0]
    nat_ref[0:32, :] = low[0, 0:32, :]
    nat_ref[32:64, :] = low[1, 0:32, :]
    nat_ref[64:96, :] = low[0, 32:64, :]
    nat_ref[96:128, :] = low[1, 32:64, :]
    d_out = (
        mm(nat_ref[:, half_at(shard, True)], wo_own[...], NT)
        + mm(nat_ref[:, half_at(shard, False)], wo_oth[...], NT)
    ).astype(BF)
    turned = (d_out.astype(F32) * o[...]).T
    delta = jnp.concatenate(
        [
            jnp.sum(turned[head * HD : (head + 1) * HD], axis=0, keepdims=True)
            for head in range(HEADS)
        ],
        axis=1,
    )
    q_heads = by_head(q[...] * BF(HD ** -0.5))
    d_heads = by_head(d_out)
    acc_ref[...] = jnp.zeros_like(acc_ref)

    @pl.loop(0, LEN // 256)
    def _(step):
        rows = pl.ds(pl.multiple_of(step * 256, 256), 256)
        keys, values = k[rows, :], v[rows, :]
        allowed = id_k[rows, :] == id_q[...]
        probs = jnp.where(allowed, jnp.exp(mm(keys, q_heads, NT) - lse[...]), 0.0)
        d_scores = (probs * (mm(values, d_heads, NT) - delta)).astype(BF)
        dkv_ref[rows, 0:COLS] = mm(d_scores, q_heads).astype(BF)
        dkv_ref[rows, COLS : 2 * COLS] = mm(probs.astype(BF), d_heads).astype(BF)
        acc_ref[...] += mm(d_scores, keys, TN)

    lane = lax.broadcasted_iota(jnp.int32, (BLK, COLS), 1) // HD
    total = jnp.zeros((BLK, COLS), F32)
    for head in range(HEADS):
        total = jnp.where(lane == head, acc_ref[head * BLK : (head + 1) * BLK, :], total)
    dq_ref[...] = (total * HD ** -0.5).astype(BF)


def token_grad_kernel(place, dq, recv, w_own, w_oth, d_ref, mine_ref, theirs_ref, part_ref):
    shard = place[0]
    total = recv[0].astype(F32)
    for index in range(1, RING):
        total = total + recv[index].astype(F32)
    d_ref[:, 0:COLS] = dq[...]
    d_ref[:, COLS : 3 * COLS] = total.astype(BF)
    for own, weight in ((True, w_own), (False, w_oth)):
        part_ref[:, half_at(shard, own)] = (
            mm(d_ref[:, 0:COLS], weight[0], NT)
            + mm(d_ref[:, COLS : 2 * COLS], weight[1], NT)
            + mm(d_ref[:, 2 * COLS : 3 * COLS], weight[2], NT)
        )
    split_rows(place, part_ref, mine_ref, theirs_ref)


def in_grads_kernel(place, tokens, d, d_pair, pair_fwd, ob, low, low_pair, sums, out_ref):
    shard = place[0]
    rows = jnp.concatenate([tokens[:, half_at(shard, True)], pair_fwd[:, 1792:2304]], axis=0)
    grads = jnp.concatenate([d[...], d_pair[...]], axis=0)
    for part in range(3):
        term = mm(rows, grads[:, part * COLS : (part + 1) * COLS], TN).astype(BF)
        out_ref[:, part * 32 : part * 32 + 32, :] = term.reshape(RING, 32, COLS)
    heads = jnp.concatenate([ob[...], pair_fwd[:, 0:256]], axis=0)
    outs = jnp.concatenate([low[...], low_pair[...]], axis=0)
    for side in range(2):
        term = mm(heads, outs[:, side * COLS : (side + 1) * COLS], TN).astype(BF)
        out_ref[:, 96 + side * 16 : 112 + side * 16, :] = term.reshape(RING, 16, COLS)
    wide = grads.astype(F32)
    small = jnp.concatenate(
        [
            sums[0:6, :],
            jnp.sum(wide[:, 0:COLS], axis=0, keepdims=True),
            jnp.sum(wide[:, 2 * COLS : 3 * COLS], axis=0, keepdims=True),
            jnp.zeros((8, COLS), F32),
        ],
        axis=0,
    ).astype(BF)
    for index in range(RING):
        out_ref[index, 128:144, :] = small


def total_kernel(place, recv, small_ref, out_ref):
    total = recv[0].astype(F32)
    for index in range(1, RING):
        total = total + recv[index].astype(F32)
    small_ref[...] = total[128:144]
    low = total[0:128].astype(BF)
    for index in range(RING):
        out_ref[index] = low


def unpack_kernel(place, recv, in_ref, out_ref):
    for part in range(3):
        in_ref[part] = recv[:, part * 32 : part * 32 + 32, :].reshape(HALF, COLS).astype(F32)
    for side in range(2):
        out_ref[:, side * COLS : (side + 1) * COLS] = (
            recv[:, 96 + side * 16 : 112 + side * 16, :].reshape(COLS, COLS).astype(F32)
        )


def swap(value, axis, bit):
    size = lax.axis_size(axis)
    return lax.ppermute(value, axis, [(index, index ^ bit) for index in range(size)])


def pair_gather(value):
    return lax.all_gather(value, "tensor", axis=0, axis_index_groups=[[0, 1], [2, 3]])


def tensor_sum(mine, theirs):
    chip = mine + swap(theirs, "tensor", 1).astype(F32)
    return chip, swap(chip.astype(BF), "tensor", 2)


def shards(
    tokens, segment_ids, w_qkv, b_qv, w_out, w_up, b_up, w_down, out_bias, ln_gain, ln_bias, cotangent
):
    shard, block, tensor = (lax.axis_index(name) for name in ("shard", "context", "tensor"))
    core, far = tensor % 2, tensor // 2
    place = jnp.stack([shard, block, core, far]).astype(jnp.int32)
    w_in = jnp.transpose(w_qkv[0], (1, 0, 2))
    w_out, w_up, w_down = w_out[0], w_up[0], w_down[0]
    extra, gain, shift = out_bias[0], ln_gain[0], ln_bias[0]

    in_oth = swap(w_in, "shard", 1)
    out_oth = swap(w_out, "shard", 1)
    up_rows = lax.dynamic_slice_in_dim(w_up, block * 32, 32, 0)
    down_rows = lax.dynamic_slice_in_dim(w_down, block * 64, 64, 0)
    packed = jnp.concatenate([up_rows[:, :HALF], up_rows[:, HALF:], down_rows], axis=0)
    ff_oth = lax.all_gather(swap(packed, "shard", 1), "context", axis=0)

    mine = lax.dynamic_slice_in_dim(tokens, core * HALF, HALF, 1)
    spread = lax.all_to_all(
        jnp.broadcast_to(mine[None], (RING, BLK, HALF)), "context", 0, 0, tiled=True
    )
    x = pair_gather(spread.reshape(LEN, HALF))

    id_q = lax.dynamic_slice_in_dim(segment_ids, block * BLK, BLK, 0)
    q, k, v, o, ob, lse, mine, theirs = call(
        attend_kernel,
        [
            ((BLK, COLS), BF), ((LEN, COLS), BF), ((LEN, COLS), BF), ((BLK, COLS), F32),
            ((BLK, COLS), BF), ((1, HEADS * BLK), F32), ((64, D), F32), ((64, D), BF),
        ],
        place, x, w_in, in_oth, b_qv[0], id_q[:, None], segment_ids[None, :], w_out, out_oth,
        scratch=[pltpu.VMEM((BLK, D), F32)], vmem=48,
    )
    chip, recv = tensor_sum(mine, theirs)
    middle, normed, factor, low_mid = call(
        first_norm_kernel,
        [((64, D), F32), ((64, D), F32), ((64, 128), F32), ((64, D), BF)],
        place, tokens, chip, recv, extra, gain, shift,
    )
    hb = pair_gather(low_mid).reshape(BLK, D)
    ub, slope, mine, theirs = call(
        up_down_kernel,
        [((BLK, UNITS), BF), ((BLK, UNITS), F32), ((64, D), F32), ((64, D), BF)],
        place, hb, w_up, w_down, ff_oth, b_up,
        scratch=[pltpu.VMEM((BLK, D), F32)],
    )
    away = (1 - shard) * HALF
    pair_fwd = swap(
        jnp.concatenate(
            [
                ob,
                lax.dynamic_slice_in_dim(hb, away, HALF, 1),
                ub,
                lax.dynamic_slice_in_dim(tokens, away, HALF, 1),
            ],
            axis=1,
        ),
        "shard", 1,
    )
    chip, recv = tensor_sum(mine, theirs)
    hidden_out, dx, low_second, sums = call(
        second_norm_kernel,
        [((32, D), F32), ((64, D), F32), ((64, D), BF), ((8, D), F32)],
        place, middle, chip, recv, extra, gain, shift, cotangent,
        scratch=[pltpu.VMEM((64, D), F32)],
    )
    dz = pair_gather(low_second).reshape(BLK, D)
    da, mine, theirs = call(
        down_up_kernel,
        [((BLK, UNITS), BF), ((64, D), F32), ((64, D), BF)],
        place, dz, slope, w_up, w_down, ff_oth,
        scratch=[pltpu.VMEM((BLK, D), F32)],
    )
    pair_bwd = swap(
        jnp.concatenate([lax.dynamic_slice_in_dim(dz, away, HALF, 1), da], axis=1), "shard", 1
    )
    chip, recv = tensor_sum(mine, theirs)
    (unit_grads,) = call(
        unit_grads_kernel, [((1040, UNITS), BF)], place, hb, da, ub, dz, pair_fwd, pair_bwd
    )
    unit_total = lax.psum(unit_grads, "context")
    d_first, low_first, sums = call(
        first_back_kernel,
        [((64, D), F32), ((64, D), BF), ((8, D), F32)],
        place, dx, chip, recv, normed, factor, gain, sums,
    )
    low_pairs = pair_gather(low_first)
    dq, dkv = call(
        attend_back_kernel,
        [((BLK, COLS), BF), ((LEN, 2 * COLS), BF)],
        place, q, k, v, o, lse, low_pairs, w_out, out_oth,
        jnp.tile(id_q[None, :], (1, HEADS)), segment_ids[:, None],
        scratch=[pltpu.VMEM((BLK, D), BF), pltpu.VMEM((HEADS * BLK, COLS), F32)], vmem=48,
    )
    sums = sums + swap(sums, "tensor", 1)
    sums = lax.dynamic_slice_in_dim(sums, tensor * COLS, COLS, 1)
    sums = sums + swap(sums, "shard", 1)
    low_rows = low_pairs.reshape(2, 2, 32, D).transpose(1, 0, 2, 3).reshape(BLK, D)
    low_pair = swap(lax.dynamic_slice_in_dim(low_rows, away, HALF, 1), "shard", 1)
    low_own = lax.dynamic_slice_in_dim(low_rows, shard * HALF, HALF, 1)
    recv = lax.all_to_all(dkv, "context", 0, 0, tiled=True).reshape(RING, BLK, 2 * COLS)
    d_mixed, mine, theirs = call(
        token_grad_kernel,
        [((BLK, 3 * COLS), BF), ((64, D), F32), ((64, D), BF)],
        place, dq, recv, w_in, in_oth,
        scratch=[pltpu.VMEM((BLK, D), F32)],
    )
    d_pair = swap(d_mixed, "shard", 1)
    chip = mine + swap(theirs, "tensor", 1).astype(F32)
    chip_far = lax.dynamic_slice_in_dim(chip, (1 - far) * 32, 32, 0).astype(BF)
    grad_tokens = (
        lax.dynamic_slice_in_dim(d_first + chip, far * 32, 32, 0)
        + swap(chip_far, "tensor", 2).astype(F32)
    )
    (in_grads,) = call(
        in_grads_kernel, [((RING, 144, COLS), BF)],
        place, tokens, d_mixed, d_pair, pair_fwd, ob, low_own, low_pair, sums,
    )
    recv = lax.all_to_all(in_grads, "context", 0, 0, tiled=True)
    small, totals = call(
        total_kernel, [((16, COLS), F32), ((RING, 128, COLS), BF)], place, recv
    )
    recv = lax.all_to_all(totals, "context", 0, 0, tiled=True)
    grad_in, grad_w_out = call(
        unpack_kernel, [((3, HALF, COLS), F32), ((COLS, HALF), F32)], place, recv
    )
    unit_total = unit_total.astype(F32)
    grad_w_down = jnp.concatenate([unit_total[512:1024, :HALF], unit_total[512:1024, HALF:]], axis=0)
    return (
        hidden_out,
        grad_tokens,
        jnp.transpose(grad_in, (1, 0, 2))[None],
        grad_w_out[None],
        unit_total[0:512][None],
        grad_w_down[None],
        small[6:8][None],
        unit_total[1024:1025],
        jnp.stack([small[3], small[0]])[None],
        jnp.stack([small[4], small[1]])[None],
        jnp.stack([small[5], small[2]])[None],
    )


def solution(mesh):
    rows = P(("shard", "context"), None)
    own_rows = P(("shard", "context", "tensor"), None)
    by_column = P(None, None, "tensor")
    in_specs = (
        rows,
        P("shard"),
        P(None, "shard", None, "tensor"),
        by_column,
        P(None, "tensor", "shard"),
        P(None, "shard", "tensor"),
        P(None, "tensor"),
        P(None, "tensor", "shard"),
        P(),
        P(),
        P(),
        rows,
    )
    out_specs = (
        own_rows,
        own_rows,
        P(None, "shard", None, "tensor"),
        P(None, "tensor", "shard"),
        P(None, "shard", "tensor"),
        P(None, "tensor", "shard"),
        by_column,
        P(None, "tensor"),
        by_column,
        by_column,
        by_column,
    )
    return jax.shard_map(shards, mesh=mesh, in_specs=in_specs, out_specs=out_specs, check_vma=False)
```

time: 878 us -> 326 us (0.37)
  waiting for transfers between devices: 433 us -> 151 us
  blocking collectives: 167 us -> 42.5 us
  local copies, waits for them, and re-layouts: 104 us -> 31.2 us
  matrix products: 70.9 us -> 0 us
  other arithmetic: 68.7 us -> 12.7 us
  starting transfers between devices: 0.61 us -> 37.6 us
  Pallas kernels: 0 us -> 35.6 us
  loops' own time: 12.7 us -> 0 us
    all_gather x5 -> x2, waiting for transfers between devices: 181 us -> 7.88 us  [the longest x1 7.88 us: shards(): ff_oth = lax.all_gather(swap(packed, 'shard', 1), 'context', axis=0)]
    psum x1 -> x0, blocking collectives: 158 us -> none  [shards(): lax.psum((jnp.stack(grads_qv[::-1]), jnp.stack(grads_bup[::-1]), norm_col...]
    reduce_scatter x5 -> x0, waiting for transfers between devices: 132 us -> none  [the longest x1 38.4 us: shards(): lax.psum_scatter(stacked_up.astype(jnp.bfloat16), 'shard', scatter_dimens...]
    dynamic_slice x114 -> x7, local copies, waits for them, and re-layouts: 89.7 us -> 2.94 us  [the longest x1 1.65 us: shards(): lax.dynamic_slice_in_dim(tokens, away, HALF, 1)]
    dot_general x124 -> x0, matrix products: 70.9 us -> none  [the longest x48 32.9 us: head_scores(): jnp.einsum('qhd,khd->hqk', queries, keys, preferred_element_type=jnp.floa...]
    ppermute x0 -> x17, waiting for transfers between devices: none -> 67.5 us  [swap(): lax.ppermute(value, axis, [(index, index ^ bit) for index in range(size)])]
    psum x5 -> x1, waiting for transfers between devices: 119 us -> 63.7 us  [shards(): unit_total = lax.psum(unit_grads, 'context')]
    all_to_all x0 -> x1, blocking collectives: none -> 36.6 us  [shards(): lax.all_to_all(jnp.broadcast_to(mine[None], (RING, BLK, HALF)), 'context'...]
  transfers between devices with their start and end apart: 15 -> 23, of which waited for: 13 -> 17; matrix products, arithmetic and copies ran while one was open for 9% -> 6% of each run, Pallas kernels for 0% -> 5%
where the time goes in v1:
time: 326 us; the launch traced here: 325 us
  waiting for transfers between devices  151 us (46%)
  blocking collectives  42.5 us (13%)
  starting transfers between devices  37.6 us (12%)
  Pallas kernels  35.6 us (11%)
  local copies, waits for them, and re-layouts  31.2 us (10%)
  between operations  14.2 us (4%)
  other arithmetic  12.7 us (4%)
    ppermute x17, waiting for transfers between devices, swap(): lax.ppermute(value, axis, [(index, index ^ bit) for index in range(size)])  67.5 us
    psum x1, waiting for transfers between devices, shards(): unit_total = lax.psum(unit_grads, 'context')  63.7 us
    all_to_all x1, blocking collectives, shards(): lax.all_to_all(jnp.broadcast_to(mine[None], (RING, BLK, HALF)), 'context'...  36.6 us
    pallas_call x12, Pallas kernels, call(): pl.pallas_call(kernel, out_shape=[jax.ShapeDtypeStruct(shape, dtype) for...  35.6 us
    ppermute x17, starting transfers between devices, swap(): lax.ppermute(value, axis, [(index, index ^ bit) for index in range(size)])  22.1 us
    unnamed x114, local copies, waits for them, and re-layouts  21.1 us
    all_to_all x1, waiting for transfers between devices, shards(): recv = lax.all_to_all(totals, 'context', 0, 0, tiled=True)  9.22 us
    all_gather x1, waiting for transfers between devices, shards(): ff_oth = lax.all_gather(swap(packed, 'shard', 1), 'context', axis=0)  7.88 us
  transfers between devices with their start and end apart: 23, of which 17 were waited for; matrix products, arithmetic and copies ran while one was open for 6% of the time, Pallas kernels for 5%

profile of v1, /device:TPU:0, one launch (start us, length us, event | category | flops | bytes accessed | tf_op | source)
XLA Modules:
  0.0 325.1 jit_solution(1616069103960842465)
XLA Ops:
  7.2 1.6 constant_dynamic-slice_fusion.3
  9.1 36.6 %all_to_all.24 = bf16[16,128,512]{2,1,0:T(8,128)(2,1)} all-to-all(bf16[16,128,512]{2,1,0:T(8,128)(2,1)S(1)} %broadcast_in_dim.39), channel_id=1, replica_groups=mesh['shard'=2,'context'=16,'tensor'=4] {'context'}, dimensions={0} | all-to-all | bytes 4194304 | tf_op jit(solution)/shard_map/all_to_all | solution.py:357
  45.8 1.1 copy-done.3
  47.3 1.6 collective-permute-start.4
  48.8 3.5 %collective-permute-done.4 = bf16[128,512]{1,0:T(8,128)(2,1)S(1)} collective-permute-done((bf16[128,512]{1,0:T(8,128)(2,1)S(1)}, bf16[128,512]{1,0:T(8,128)(2,1)S(1)}, u32[]{:S(2)}, u32[]{:S(2)}) %collective-permute-start.4) | collective-permute-done | bytes 131104 | tf_op jit(solution)/shard_map/ppermute | solution.py:327
  53.0 1.6 collective-permute-start
  55.4 20.1 %collective-permute-done.1.wo_oth = bf16[256,512]{1,0:T(8,128)(2,1)S(1)} collective-permute-done((bf16[256,512]{1,0:T(8,128)(2,1)S(1)}, bf16[256,512]{1,0:T(8,128)(2,1)S(1)}, u32[]{:S(2)}, u32[]{:S(2)}) %collective-permute-start.1) | collective-permute-done | bytes 262176 | tf_op jit(solution)/shard_map/ppermute | solution.py:327
  76.2 0.9 copy-done.18
  77.8 9.6 %shard_map.203 = (bf16[128,256]{1,0:T(8,128)(2,1)S(1)}, bf16[2048,256]{1,0:T(8,128)(2,1)S(1)}, bf16[2048,256]{1,0:T(8,128)(2,1)S(1)}, f32[128,256]{1,0:T(8,128)S...) custom-call(s32[4]{0:T(128)S(1)} %pad_add_fusion.place, ...), custom_call_target="tpu_custom_call" | custom-call | tf_op jit(solution)/shard_map/pallas_call | solution.py:38
  87.5 1.0 copy-done.13
  88.5 1.3 collective-permute-done.2
  89.9 3.1 collective-permute-start.3
  93.0 4.0 %collective-permute-done.3.recv = bf16[64,1024]{1,0:T(8,128)(2,1)S(1)} collective-permute-done((bf16[64,1024]{1,0:T(8,128)(2,1)S(1)}, bf16[64,1024]{1,0:T(8,128)(2,1)S(1)}, u32[]{:S(2)}, u32[]{:S(2)}) %collective-permute-start.3) | collective-permute-done | bytes 131104 | tf_op jit(solution)/shard_map/ppermute | solution.py:327
  99.2 2.0 all-gather.hb
  101.2 7.9 %all-gather.9.cloned.1.call-done = bf16[2048,512]{1,0:T(8,128)(2,1)} async-done(((bf16[128,512]{1,0:T(8,128)(2,1)}), bf16[2048,512]{1,0:T(8,128)(2,1)}) %all-gather.9.cloned.1.call-update) | async-done | bytes 2097168 | tf_op jit(solution)/shard_map/all_gather | solution.py:354
  109.1 1.6 copy-done
  111.4 1.5 shard_map.205
  113.6 1.3 collective-permute-done.5
  115.0 3.1 collective-permute-start.6
  118.0 4.1 %collective-permute-done.6.recv = bf16[64,1024]{1,0:T(8,128)(2,1)S(1)} collective-permute-done((bf16[64,1024]{1,0:T(8,128)(2,1)S(1)}, bf16[64,1024]{1,0:T(8,128)(2,1)S(1)}, u32[]{:S(2)}, u32[]{:S(2)}) %collective-permute-start.6) | collective-permute-done | bytes 131104 | tf_op jit(solution)/shard_map/ppermute | solution.py:327
  122.1 1.4 shard_map.206
  123.6 2.0 all-gather.2.dz
  125.6 2.1 shard_map.207
  127.9 1.2 collective-permute-done.7
  129.9 3.0 collective-permute-start.8
  134.5 2.8 collective-permute-done.8.recv
  137.3 0.9 copy-done.22
  138.2 0.9 copy-done.27
  139.2 0.9 copy-done.29
  141.6 1.8 shard_map.208
  143.4 2.0 all-gather.3
  146.1 0.9 copy-done.16
  147.1 0.9 copy-done.19
  148.0 0.9 copy-done.31
  149.6 7.5 %shard_map.209 = (bf16[128,256]{1,0:T(8,128)(2,1)S(1)}, bf16[2048,512]{1,0:T(8,128)(2,1)}) custom-call(s32[4]{0:T(128)S(1)} %pad_add_fusion.place, bf16[128,256]{1,0:T(8,128)(2,1)S(1)} %copy-done.33, bf16[2048,256]{1,0:T(8,128)(2,1)S(1)} %copy-done.12, bf16[2048,256]{1,0:T(8,128)(2,1)S(1)} %copy-done.14, f32[128,256]{1,0:T(8,128)S(1)} %copy-done.31, ...), custom_call_target="tpu_custom_call" | custom-call | tf_op jit(solution)/shard_map/pallas_call | solution.py:38
  157.7 4.9 %all-to-all-start.1 = ((bf16[16,128,512]{2,1,0:T(8,128)(2,1)}), bf16[16,128,512]{2,1,0:T(8,128)(2,1)S(1)}, u32[]{:S(2)}, u32[]{:S(2)}) async-start(bf16[16,128,512]{2,1,0:T(8,128)(2,1)} %bitcast.73), calls=%async_computation.1 | async-start | bytes 4194304 | tf_op jit(solution)/shard_map/all_to_all | solution.py:439
  162.7 1.1 pad_maximum_fusion
  163.8 1.5 collective-permute-start.12
  165.4 1.0 pad_maximum_fusion.1
  166.3 0.9 collective-permute-start.16
  167.2 12.9 %collective-permute-done.12.pair_fwd = bf16[128,2304]{1,0:T(8,128)(2,1)S(1)} collective-permute-done((bf16[128,2304]{1,0:T(8,128)(2,1)S(1)}, bf16[128,2304]{1,0:T(8,128)(2,1)S(1)}, u32[]{:S(2)}, u32[]{:S(2)}) %collective-permute-start.12) | collective-permute-done | bytes 589856 | tf_op jit(solution)/shard_map/ppermute | solution.py:327
  180.1 7.3 %collective-permute-done.16.pair_bwd = bf16[128,1536]{1,0:T(8,128)(2,1)S(1)} collective-permute-done((bf16[128,1536]{1,0:T(8,128)(2,1)S(1)}, bf16[128,1536]{1,0:T(8,128)(2,1)S(1)}, u32[]{:S(2)}, u32[]{:S(2)}) %collective-permute-start.16) | collective-permute-done | bytes 393248 | tf_op jit(solution)/shard_map/ppermute | solution.py:327
  187.5 2.6 shard_map.214
  190.9 0.9 copy-done.10
  192.6 3.0 all-to-all-done.1.recv
  195.6 2.2 shard_map.210
  197.8 1.4 collective-permute-start.11
  200.7 1.4 collective-permute-start.15
  202.1 4.7 %collective-permute-done.15 = f32[8,256]{1,0:T(8,128)S(1)} collective-permute-done((f32[8,256]{1,0:T(8,128)S(1)}, f32[8,256]{1,0:T(8,128)S(1)}, u32[]{:S(2)}, u32[]{:S(2)}) %collective-permute-start.15) | collective-permute-done | bytes 8224 | tf_op jit(solution)/shard_map/ppermute | solution.py:327
  206.9 1.1 copy-done.6
  207.9 2.5 shard_map.211
  210.4 5.5 %all-to-all-start.2 = ((bf16[16,144,256]{2,1,0:T(8,128)(2,1)}), bf16[16,144,256]{2,1,0:T(8,128)(2,1)S(1)}, u32[]{:S(2)}, u32[]{:S(2)}) async-start(bf16[16,144,256]{2,1,0:T(8,128)(2,1)} %shard_map.211), calls=%async_computation.2 | async-start | bytes 2359296 | tf_op jit(solution)/shard_map/all_to_all | solution.py:457
  216.1 1.3 collective-permute-done.9
  217.4 3.1 collective-permute-start.10
  220.5 2.8 collective-permute-done.10
  224.0 63.7 %all-reduce.2.cloned.1.call-done = bf16[1040,1024]{1,0:T(8,128)(2,1)} async-done(((bf16[1040,1024]{1,0:T(8,128)(2,1)}), bf16[1040,1024]{1,0:T(8,128)(2,1)}) %all-reduce.2.cloned.1.call-update) | async-done | bytes 2129936 | tf_op jit(solution)/shard_map/psum | solution.py:419
  287.7 4.3 %convert_element_type.39 = f32[1040,1024]{1,0:T(8,128)} convert(bf16[1040,1024]{1,0:T(8,128)(2,1)} %all-reduce.2.cloned.1.call-done) | non-fusion elementwise | flops 1064960 | bytes 6389760 | tf_op jit(solution)/shard_map/convert_element_type | solution.py:465
  292.5 1.2 fusion.4
  293.8 1.7 shard_map.212
  295.5 4.9 %all-to-all-start.3 = ((bf16[16,128,256]{2,1,0:T(8,128)(2,1)}), bf16[16,128,256]{2,1,0:T(8,128)(2,1)S(1)}, u32[]{:S(2)}, u32[]{:S(2)}) async-start(bf16[16,128,256]{2,1,0:T(8,128)(2,1)} %get-tuple-element.76), calls=%async_computation.3 | async-start | bytes 2097152 | tf_op jit(solution)/shard_map/all_to_all | solution.py:461
  300.3 2.7 maximum_bitcast_fusion
  303.0 3.2 slice_bitcast_fusion
  307.4 9.2 %all-to-all-done.3.recv = bf16[16,128,256]{2,1,0:T(8,128)(2,1)S(1)} async-done(((bf16[16,128,256]{2,1,0:T(8,128)(2,1)}), bf16[16,128,256]{2,1,0:T(8,128)(2,1)S(1)}, u32[]{:S(2)}, u32[]{:S(2)}) %all-to-all-start.3) | async-done | bytes 1048608 | tf_op jit(solution)/shard_map/all_to_all | solution.py:461
  316.6 2.0 shard_map.213
  (149 shorter events, 19.1 us)
Async XLA Ops:
  7.2 69.0 %all-gather.7.cloned.1.call-start = ((), (), s32[]{:S(2)}) async-start(), calls=%async_computation.4 | async-start | bytes 6291456 | tf_op jit(solution)/shard_map/all_gather | solution.py:331
  9.1 45.5 %copy-start.15 = (bf16[1,256,512]{2,1,0:T(8,128)(2,1)S(1)}, bf16[1,256,512]{2,1,0:T(8,128)(2,1)}, u32[]{:S(2)}) copy-start(bf16[1,256,512]{2,1,0:T(8,128)(2,1)} %param.16) | copy-start | bytes 786436
  45.7 1.2 copy-start.3
  45.7 1.5 copy-start.2
  45.7 7.3 %copy-start.4 = (bf16[1,512,3,256]{3,1,2,0:T(8,128)(2,1)S(1)}, bf16[1,512,3,256]{3,1,2,0:T(8,128)(2,1)}, u32[]{:S(2)}) copy-start(bf16[1,512,3,256]{3,1,2,0:T(8,128)(2,1)} %param.14) | copy-start | bytes 2359300
  45.7 9.4 %copy-start.39 = (s32[2048]{0:T(1024)S(1)}, s32[2048]{0:T(1024)}, u32[]{:S(2)}) copy-start(s32[2048]{0:T(1024)} %param.13) | copy-start | bytes 24580
  45.7 63.4 %all-gather.9.cloned.1.call-start = ((), (), s32[]{:S(2)}) async-start(), calls=%async_computation.6 | async-start | bytes 2228224 | tf_op jit(solution)/shard_map/all_gather | solution.py:354
  47.3 5.0 %collective-permute-start.4 = (bf16[128,512]{1,0:T(8,128)(2,1)S(1)}, bf16[128,512]{1,0:T(8,128)(2,1)S(1)}, u32[]{:S(2)}, u32[]{:S(2)}) collective-permute-start(bf16[128,512]{1,0:T(8,128)(2,1)S(1)} %pad_maximum_fusion.2), channel_id=1, source_target_pairs={{0,64},{64,0},{1,65},{65,1},{2,66},{66,2},{3,67},{67,3},{4,68},{68... | collective-permute-start | bytes 393224 | tf_op jit(solution)/shard_map/ppermute | solution.py:327
  53.0 23.2 %collective-permute-start = (bf16[3,512,256]{2,1,0:T(8,128)(2,1)S(1)}, bf16[3,512,256]{2,1,0:T(8,128)(2,1)}, u32[]{:S(2)}, u32[]{:S(2)}) collective-permute-start(bf16[3,512,256]{2,1,0:T(8,128)(2,1)S(1)} %bitcast.53), channel_id=1, source_target_pairs={{0,64},{64,0},{1,65},{65,1},{2,66},{66,2},{3,67},{67,3},{4,68},{68... | collective-permute-start | bytes 2359304 | tf_op jit(solution)/shard_map/ppermute | solution.py:327
  54.6 20.9 %collective-permute-start.1 = (bf16[256,512]{1,0:T(8,128)(2,1)S(1)}, bf16[256,512]{1,0:T(8,128)(2,1)S(1)}, u32[]{:S(2)}, u32[]{:S(2)}) collective-permute-start(bf16[256,512]{1,0:T(8,128)(2,1)S(1)} %bitcast.58), channel_id=1, source_target_pairs={{0,64},{64,0},{1,65},{65,1},{2,66},{66,2},{3,67},{67,3},{4,68},{68... | collective-permute-start | bytes 786440 | tf_op jit(solution)/shard_map/ppermute | solution.py:327
  76.2 1.0 copy-start.18
  77.8 19.2 %copy-start.7 = (bf16[128,1024]{1,0:T(8,128)(2,1)S(1)}, bf16[128,1024]{1,0:T(8,128)(2,1)}, u32[]{:S(2)}) copy-start(bf16[128,1024]{1,0:T(8,128)(2,1)} %tokens.3) | copy-start | bytes 786436
  77.8 19.2 %copy-start.38 = (bf16[1,2,1024]{2,1,0:T(2,128)(2,1)S(1)}, bf16[1,2,1024]{2,1,0:T(2,128)(2,1)}, u32[]{:S(2)}) copy-start(bf16[1,2,1024]{2,1,0:T(2,128)(2,1)} %param.21) | copy-start | bytes 12292
  77.8 19.2 %copy-start.44 = (bf16[1,2,1024]{2,1,0:T(2,128)(2,1)S(1)}, bf16[1,2,1024]{2,1,0:T(2,128)(2,1)}, u32[]{:S(2)}) copy-start(bf16[1,2,1024]{2,1,0:T(2,128)(2,1)} %param.20) | copy-start | bytes 12292
  77.8 19.2 %copy-start.46 = (bf16[1,2,1024]{2,1,0:T(2,128)(2,1)S(1)}, bf16[1,2,1024]{2,1,0:T(2,128)(2,1)}, u32[]{:S(2)}) copy-start(bf16[1,2,1024]{2,1,0:T(2,128)(2,1)} %param.22) | copy-start | bytes 12292
  87.5 1.0 copy-start.13
  88.4 9.4 %copy-start.11 = (bf16[2048,256]{1,0:T(8,128)(2,1)}, bf16[2048,256]{1,0:T(8,128)(2,1)S(1)}, u32[]{:S(2)}) copy-start(bf16[2048,256]{1,0:T(8,128)(2,1)S(1)} %get-tuple-element.63.k) | copy-start | bytes 3145732
  88.4 10.8 %copy-start.30 = (f32[128,256]{1,0:T(8,128)}, f32[128,256]{1,0:T(8,128)S(1)}, u32[]{:S(2)}) copy-start(f32[128,256]{1,0:T(8,128)S(1)} %get-tuple-element.65.o) | copy-start | bytes 393220
  88.4 10.8 %copy-start.32 = (bf16[128,256]{1,0:T(8,128)(2,1)}, bf16[128,256]{1,0:T(8,128)(2,1)S(1)}, u32[]{:S(2)}) copy-start(bf16[128,256]{1,0:T(8,128)(2,1)S(1)} %get-tuple-element.62.q) | copy-start | bytes 196612
  88.5 10.8 %copy-start.49 = (f32[1,512]{1,0:T(1,128)}, f32[1,512]{1,0:T(1,128)S(1)}, u32[]{:S(2)}) copy-start(f32[1,512]{1,0:T(1,128)S(1)} %get-tuple-element.66.lse) | copy-start | bytes 6148
  88.5 1.4 collective-permute-start.2
  89.9 7.1 %collective-permute-start.3 = (bf16[64,1024]{1,0:T(8,128)(2,1)S(1)}, bf16[64,1024]{1,0:T(8,128)(2,1)S(1)}, u32[]{:S(2)}, u32[]{:S(2)}) collective-permute-start(bf16[64,1024]{1,0:T(8,128)(2,1)S(1)} %get-tuple-element.85), channel_id=1, source_target_pairs={{0,2},{1,3},{2,0},{3,1},{4,6},{5,7},{6,4},{7,5},{8,10},{9,11},{10,... | collective-permute-start | bytes 393224 | tf_op jit(solution)/shard_map/ppermute | solution.py:327
  109.1 1.6 copy-start
  111.4 10.7 %copy-start.25 = (f32[128,1024]{1,0:T(8,128)S(1)}, f32[128,1024]{1,0:T(8,128)}, u32[]{:S(2)}) copy-start(f32[128,1024]{1,0:T(8,128)} %cot.1) | copy-start | bytes 1572868
  111.4 10.7 %copy-start.45 = (bf16[1,2,1024]{2,1,0:T(2,128)(2,1)S(1)}, bf16[1,2,1024]{2,1,0:T(2,128)(2,1)}, u32[]{:S(2)}) copy-start(bf16[1,2,1024]{2,1,0:T(2,128)(2,1)} %param.20) | copy-start | bytes 12292
  111.4 10.7 %copy-start.47 = (bf16[1,2,1024]{2,1,0:T(2,128)(2,1)S(1)}, bf16[1,2,1024]{2,1,0:T(2,128)(2,1)}, u32[]{:S(2)}) copy-start(bf16[1,2,1024]{2,1,0:T(2,128)(2,1)} %param.22) | copy-start | bytes 12292
  113.6 12.0 %copy-start.1 = (bf16[2048,512]{1,0:T(8,128)(2,1)S(1)}, bf16[2048,512]{1,0:T(8,128)(2,1)}, u32[]{:S(2)}) copy-start(bf16[2048,512]{1,0:T(8,128)(2,1)} %all-gather.9.cloned.1.call-done) | copy-start | bytes 6291460
  113.6 1.3 collective-permute-start.5
  115.0 7.1 %collective-permute-start.6 = (bf16[64,1024]{1,0:T(8,128)(2,1)S(1)}, bf16[64,1024]{1,0:T(8,128)(2,1)S(1)}, u32[]{:S(2)}, u32[]{:S(2)}) collective-permute-start(bf16[64,1024]{1,0:T(8,128)(2,1)S(1)} %get-tuple-element.83), channel_id=1, source_target_pairs={{0,2},{1,3},{2,0},{3,1},{4,6},{5,7},{6,4},{7,5},{8,10},{9,11},{10,... | collective-permute-start | bytes 393224 | tf_op jit(solution)/shard_map/ppermute | solution.py:327
  123.6 2.0 copy-start.28
  123.6 2.0 copy-start.42
  127.6 5.8 %copy-start.20 = (bf16[128,1024]{1,0:T(8,128)(2,1)}, bf16[128,1024]{1,0:T(8,128)(2,1)S(1)}, u32[]{:S(2)}) copy-start(bf16[128,1024]{1,0:T(8,128)(2,1)S(1)} %get-tuple-element.79.da) | copy-start | bytes 786436
  127.6 18.4 %copy-start.12 = (bf16[2048,256]{1,0:T(8,128)(2,1)S(1)}, bf16[2048,256]{1,0:T(8,128)(2,1)}, u32[]{:S(2)}) copy-start(bf16[2048,256]{1,0:T(8,128)(2,1)} %copy-done.11) | copy-start | bytes 3145732
  127.7 18.4 %copy-start.33 = (bf16[128,256]{1,0:T(8,128)(2,1)S(1)}, bf16[128,256]{1,0:T(8,128)(2,1)}, u32[]{:S(2)}) copy-start(bf16[128,256]{1,0:T(8,128)(2,1)} %copy-done.32) | copy-start | bytes 196612
  127.7 1.4 collective-permute-start.7
  129.9 7.4 %collective-permute-start.8 = (bf16[64,1024]{1,0:T(8,128)(2,1)}, bf16[64,1024]{1,0:T(8,128)(2,1)}, u32[]{:S(2)}, u32[]{:S(2)}) collective-permute-start(bf16[64,1024]{1,0:T(8,128)(2,1)} %get-tuple-element.81), channel_id=1, source_target_pairs={{0,2},{1,3},{2,0},{3,1},{4,6},{5,7},{6,4},{7,5},{8,10},{9,11},{10,... | collective-permute-start | bytes 393224 | tf_op jit(solution)/shard_map/ppermute | solution.py:327
  133.8 12.3 %copy-start.14 = (bf16[2048,256]{1,0:T(8,128)(2,1)S(1)}, bf16[2048,256]{1,0:T(8,128)(2,1)}, u32[]{:S(2)}) copy-start(bf16[2048,256]{1,0:T(8,128)(2,1)} %copy-done.13) | copy-start | bytes 3145732
  137.3 1.0 copy-start.22
  138.2 0.9 copy-start.27
  143.4 2.6 copy-start.36
  145.4 11.6 %copy-start.9 = (bf16[128,1024]{1,0:T(8,128)(2,1)}, bf16[128,1024]{1,0:T(8,128)(2,1)S(1)}, u32[]{:S(2)}) copy-start(bf16[128,1024]{1,0:T(8,128)(2,1)S(1)} %all-gather.3) | copy-start | bytes 786436
  146.1 1.0 copy-start.16
  157.7 37.9 %all-to-all-start.1 = ((bf16[16,128,512]{2,1,0:T(8,128)(2,1)}), bf16[16,128,512]{2,1,0:T(8,128)(2,1)S(1)}, u32[]{:S(2)}, u32[]{:S(2)}) async-start(bf16[16,128,512]{2,1,0:T(8,128)(2,1)} %bitcast.73), calls=%async_computation.1 | async-start | bytes 4194304 | tf_op jit(solution)/shard_map/all_to_all | solution.py:439
  162.6 125.0 %all-reduce.2.cloned.1.call-start = ((), (), s32[]{:S(2)}) async-start(), calls=%async_computation.5 | async-start | bytes 4259840 | tf_op jit(solution)/shard_map/psum | solution.py:419
  162.7 24.8 %copy-start.21 = (bf16[128,1024]{1,0:T(8,128)(2,1)S(1)}, bf16[128,1024]{1,0:T(8,128)(2,1)}, u32[]{:S(2)}) copy-start(bf16[128,1024]{1,0:T(8,128)(2,1)} %copy-done.20) | copy-start | bytes 786436
  162.7 24.8 %copy-start.24 = (bf16[128,1024]{1,0:T(8,128)(2,1)S(1)}, bf16[128,1024]{1,0:T(8,128)(2,1)}, u32[]{:S(2)}) copy-start(bf16[128,1024]{1,0:T(8,128)(2,1)} %copy-done.23) | copy-start | bytes 786436
  163.8 16.3 %collective-permute-start.12 = (bf16[128,2304]{1,0:T(8,128)(2,1)S(1)}, bf16[128,2304]{1,0:T(8,128)(2,1)S(1)}, u32[]{:S(2)}, u32[]{:S(2)}) collective-permute-start(bf16[128,2304]{1,0:T(8,128)(2,1)S(1)} %pad_maximum_fusion), channel_id=1, source_target_pairs={{0,64},{64,0},{1,65},{65,1},{2,66},{66,2},{3,67},{67,3},{4,68},{68... | collective-permute-start | bytes 1769480 | tf_op jit(solution)/shard_map/ppermute | solution.py:327
  166.3 21.1 %collective-permute-start.16 = (bf16[128,1536]{1,0:T(8,128)(2,1)S(1)}, bf16[128,1536]{1,0:T(8,128)(2,1)S(1)}, u32[]{:S(2)}, u32[]{:S(2)}) collective-permute-start(bf16[128,1536]{1,0:T(8,128)(2,1)S(1)} %pad_maximum_fusion.1), channel_id=1, source_target_pairs={{0,64},{64,0},{1,65},{65,1},{2,66},{66,2},{3,67},{67,3},{4,68},{68... | collective-permute-start | bytes 1179656 | tf_op jit(solution)/shard_map/ppermute | solution.py:327
  190.9 4.7 %copy-start.35 = (bf16[128,256]{1,0:T(8,128)(2,1)S(1)}, bf16[128,256]{1,0:T(8,128)(2,1)}, u32[]{:S(2)}) copy-start(bf16[128,256]{1,0:T(8,128)(2,1)} %copy-done.34) | copy-start | bytes 196612
  192.6 7.4 %collective-permute-start.14 = (f32[8,1024]{1,0:T(8,128)}, f32[8,1024]{1,0:T(8,128)}, u32[]{:S(2)}, u32[]{:S(2)}) collective-permute-start(f32[8,1024]{1,0:T(8,128)} %get-tuple-element.75), channel_id=1, source_target_pairs={{0,1},{1,0},{2,3},{3,2},{4,5},{5,4},{6,7},{7,6},{8,9},{9,8},{10,11... | collective-permute-start | bytes 98312 | tf_op jit(solution)/shard_map/ppermute | solution.py:327
  195.6 3.7 %copy-start.55 = (bf16[2,2,32,1024]{3,2,0,1:T(8,128)(2,1)S(1)}, bf16[2,2,32,1024]{3,2,0,1:T(8,128)(2,1)}, u32[]{:S(2)}) copy-start(bf16[2,2,32,1024]{3,2,0,1:T(8,128)(2,1)} %copy.30) | copy-start | bytes 786436
  195.6 11.3 %copy-start.8 = (bf16[128,1024]{1,0:T(8,128)(2,1)S(1)}, bf16[128,1024]{1,0:T(8,128)(2,1)}, u32[]{:S(2)}) copy-start(bf16[128,1024]{1,0:T(8,128)(2,1)} %tokens.3) | copy-start | bytes 786436
  197.8 1.5 copy-start.52
  197.8 9.1 %collective-permute-start.11 = (bf16[128,768]{1,0:T(8,128)(2,1)}, bf16[128,768]{1,0:T(8,128)(2,1)S(1)}, u32[]{:S(2)}, u32[]{:S(2)}) collective-permute-start(bf16[128,768]{1,0:T(8,128)(2,1)} %get-tuple-element.72.d), channel_id=1, source_target_pairs={{0,64},{64,0},{1,65},{65,1},{2,66},{66,2},{3,67},{67,3},{4,68},{68... | collective-permute-start | bytes 589832 | tf_op jit(solution)/shard_map/ppermute | solution.py:327
  199.3 7.6 %collective-permute-start.13 = (bf16[128,512]{1,0:T(8,128)(2,1)S(1)}, bf16[128,512]{1,0:T(8,128)(2,1)S(1)}, u32[]{:S(2)}, u32[]{:S(2)}) collective-permute-start(bf16[128,512]{1,0:T(8,128)(2,1)S(1)} %get-tuple-element.89), channel_id=1, source_target_pairs={{0,64},{64,0},{1,65},{65,1},{2,66},{66,2},{3,67},{67,3},{4,68},{68... | collective-permute-start | bytes 393224 | tf_op jit(solution)/shard_map/ppermute | solution.py:327
  200.7 6.2 %collective-permute-start.15 = (f32[8,256]{1,0:T(8,128)S(1)}, f32[8,256]{1,0:T(8,128)S(1)}, u32[]{:S(2)}, u32[]{:S(2)}) collective-permute-start(f32[8,256]{1,0:T(8,128)S(1)} %dynamic-slice_add_fusion.1), channel_id=1, source_target_pairs={{0,64},{64,0},{1,65},{65,1},{2,66},{66,2},{3,67},{67,3},{4,68},{68... | collective-permute-start | bytes 24584 | tf_op jit(solution)/shard_map/ppermute | solution.py:327
  206.9 1.1 copy-start.6
  207.9 8.0 %copy-start.53 = (bf16[64,1024]{1,0:T(8,128)(2,1)S(1)}, bf16[64,1024]{1,0:T(8,128)(2,1)}, u32[]{:S(2)}) copy-start(bf16[64,1024]{1,0:T(8,128)(2,1)} %copy-done.52) | copy-start | bytes 393220
  210.4 12.9 %copy-start.37 = (f32[64,1024]{1,0:T(8,128)S(1)}, f32[64,1024]{1,0:T(8,128)}, u32[]{:S(2)}) copy-start(f32[64,1024]{1,0:T(8,128)} %copy-done.36) | copy-start | bytes 786436
  210.4 83.4 %all-to-all-start.2 = ((bf16[16,144,256]{2,1,0:T(8,128)(2,1)}), bf16[16,144,256]{2,1,0:T(8,128)(2,1)S(1)}, u32[]{:S(2)}, u32[]{:S(2)}) async-start(bf16[16,144,256]{2,1,0:T(8,128)(2,1)} %shard_map.211), calls=%async_computation.2 | async-start | bytes 2359296 | tf_op jit(solution)/shard_map/all_to_all | solution.py:457
  215.9 1.4 collective-permute-start.9
  217.4 5.8 %collective-permute-start.10 = (bf16[32,1024]{1,0:T(8,128)(2,1)S(1)}, bf16[32,1024]{1,0:T(8,128)(2,1)S(1)}, u32[]{:S(2)}, u32[]{:S(2)}) collective-permute-start(bf16[32,1024]{1,0:T(8,128)(2,1)S(1)} %dynamic-slice_convert_fusion), channel_id=1, source_target_pairs={{0,2},{1,3},{2,0},{3,1},{4,6},{5,7},{6,4},{7,5},{8,10},{9,11},{10,... | collective-permute-start | bytes 196616 | tf_op jit(solution)/shard_map/ppermute | solution.py:327
  287.7 4.3 %copy-start.54 = (bf16[1040,1024]{1,0:T(8,128)(2,1)S(1)}, bf16[1040,1024]{1,0:T(8,128)(2,1)}, u32[]{:S(2)}) copy-start(bf16[1040,1024]{1,0:T(8,128)(2,1)} %all-reduce.2.cloned.1.call-done) | copy-start | bytes 6389764
  295.5 21.2 %all-to-all-start.3 = ((bf16[16,128,256]{2,1,0:T(8,128)(2,1)}), bf16[16,128,256]{2,1,0:T(8,128)(2,1)S(1)}, u32[]{:S(2)}, u32[]{:S(2)}) async-start(bf16[16,128,256]{2,1,0:T(8,128)(2,1)} %get-tuple-element.76), calls=%async_computation.3 | async-start | bytes 2097152 | tf_op jit(solution)/shard_map/all_to_all | solution.py:461
  (16 other events, 12.2 us)
Sparse Core Ops, SparseCore 0:
  45.8 13.8 all-gather.6
  62.4 46.6 all-gather.8
  191.0 96.5 all-reduce.1

commit v2 on v1

v2 whole, which is shorter than its diff:
```python
import functools

import jax
import jax.numpy as jnp
from jax import lax
from jax.experimental import pallas as pl
from jax.experimental.pallas import tpu as pltpu
from jax.sharding import PartitionSpec as P

HD = 64
HEADS = 4
BLK = 128
LEN = 2048
D = 1024
HALF = 512
COLS = 256
UNITS = 1024
RING = 16
EPSILON = 1e-05
NEGATIVE = -1e30
ROOT_HALF = 0.7071067811865476
DENSITY = 0.3989422804014327
BF = jnp.bfloat16
F32 = jnp.float32

NN = (((1,), (0,)), ((), ()))
NT = (((1,), (1,)), ((), ()))
TN = (((0,), (0,)), ((), ()))


def mm(a, b, dims=NN):
    return lax.dot_general(a, b, dims, preferred_element_type=F32)


def call(kernel, micros, outs, scalars, *args, scratch=(), vmem=20):
    specs = [pl.BlockSpec(memory_space=pltpu.SMEM)]
    specs += [pl.BlockSpec(memory_space=pltpu.VMEM)] * len(args)
    return pl.pallas_call(
        kernel,
        out_shape=[jax.ShapeDtypeStruct(shape, dtype) for shape, dtype in outs],
        in_specs=specs,
        out_specs=[pl.BlockSpec(memory_space=pltpu.VMEM)] * len(outs),
        scratch_shapes=list(scratch),
        compiler_params=pltpu.CompilerParams(vmem_limit_bytes=vmem << 20),
        cost_estimate=pl.CostEstimate(
            flops=int(micros * 1.1e9), bytes_accessed=int(micros * 3e6), transcendentals=0
        ),
    )(scalars, *args)


def half_at(shard, own):
    return pl.ds(pl.multiple_of((shard if own else 1 - shard) * HALF, HALF), HALF)


def by_head(rows):
    lane = lax.broadcasted_iota(jnp.int32, rows.shape, 1) // HD
    return jnp.concatenate(
        [jnp.where(lane == head, rows, jnp.zeros_like(rows)) for head in range(HEADS)], axis=0
    )


def norm_rows(summed, gain, shift):
    centred = summed - jnp.mean(summed, axis=-1, keepdims=True)
    factor = lax.rsqrt(jnp.mean(centred * centred, axis=-1, keepdims=True) + EPSILON)
    normed = centred * factor
    return normed * gain + shift, normed, factor


def norm_back(incoming, normed, factor, gain):
    scaled = incoming * gain
    centre = jnp.mean(scaled, axis=-1, keepdims=True)
    along = jnp.mean(scaled * normed, axis=-1, keepdims=True)
    return factor * (scaled - centre - normed * along)


def split_rows(place, rows_ref, mine_ref, theirs_ref):
    core = place[2]
    for part in range(2):
        mine = pl.multiple_of(part * 64 + core * 32, 32)
        theirs = pl.multiple_of(part * 64 + (1 - core) * 32, 32)
        mine_ref[pl.ds(part * 32, 32), :] = rows_ref[pl.ds(mine, 32), :].astype(BF)
        theirs_ref[pl.ds(part * 32, 32), :] = rows_ref[pl.ds(theirs, 32), :].astype(BF)


def split_halves(place, rows_ref, mine_ref, theirs_ref):
    core = place[2]
    mine_ref[...] = rows_ref[pl.ds(pl.multiple_of(core * 64, 64), 64), :].astype(BF)
    theirs_ref[...] = rows_ref[pl.ds(pl.multiple_of((1 - core) * 64, 64), 64), :].astype(BF)


def core_rows(place, ref):
    core = place[2]
    return jnp.concatenate(
        [ref[pl.ds(pl.multiple_of(part * 64 + core * 32, 32), 32), :] for part in range(2)], axis=0
    )


def attend_kernel(
    place, x_mine, x_sib, w_own, w_oth, b_qv, id_q, id_k, wo_own, wo_oth,
    q_ref, k_ref, v_ref, o_ref, ob_ref, lse_ref, mine_ref, theirs_ref, part_ref,
):
    shard, block, core = place[0], place[1], place[2]
    biases = b_qv[...].astype(F32)
    own, oth = half_at(shard, True), half_at(shard, False)

    @pl.loop(0, RING // 4)
    def _(step):
        blocks = pl.ds(step * 4, 4)
        for x, side in ((x_mine, core), (x_sib, 1 - core)):
            x_own = x[blocks, :, own].reshape(256, HALF)
            x_oth = x[blocks, :, oth].reshape(256, HALF)
            queries = mm(x_own, w_own[0]) + mm(x_oth, w_oth[0]) + biases[0:1]
            keys = mm(x_own, w_own[1]) + mm(x_oth, w_oth[1])
            values = mm(x_own, w_own[2]) + mm(x_oth, w_oth[2]) + biases[1:2]
            q_ref[blocks, side] = queries.astype(BF).reshape(4, 64, COLS)
            k_ref[blocks, side] = keys.astype(BF).reshape(4, 64, COLS)
            v_ref[blocks, side] = values.astype(BF).reshape(4, 64, COLS)

    keys, values = k_ref[...].reshape(LEN, COLS), v_ref[...].reshape(LEN, COLS)
    q_heads = by_head(q_ref[block].reshape(BLK, COLS) * BF(HD ** -0.5))
    allowed = id_q[...] == id_k[...]
    lane = lax.broadcasted_iota(jnp.int32, (BLK, COLS), 1) // HD
    out = jnp.zeros((BLK, COLS), F32)
    for head in range(HEADS):
        scores = mm(q_heads[head * BLK : (head + 1) * BLK], keys, NT)
        scores = jnp.where(allowed, scores, NEGATIVE)
        highest = jnp.max(scores, axis=-1, keepdims=True)
        weights = jnp.exp(scores - highest)
        total = jnp.sum(weights, axis=-1, keepdims=True)
        mixed = mm(weights.astype(BF), values) / total
        out = jnp.where(lane == head, mixed, out)
        column = jnp.broadcast_to(highest + jnp.log(total), (BLK, BLK))
        lse_ref[:, head * BLK : (head + 1) * BLK] = column.T[0:1, :]
    o_ref[...] = out
    low = out.astype(BF)
    ob_ref[...] = low
    part_ref[:, own] = mm(low, wo_own[...])
    part_ref[:, oth] = mm(low, wo_oth[...])
    split_rows(place, part_ref, mine_ref, theirs_ref)


def first_norm(summed, gain, shift):
    return norm_rows(summed[...], gain[0:1, :].astype(F32), shift[0:1, :].astype(F32))


def first_norm_kernel(place, tokens, chip, recv, extra, gain, shift, s_ref, hb_ref):
    branch = chip[...].astype(F32) + recv[...].astype(F32) + extra[0:1, :].astype(F32)
    s_ref[...] = core_rows(place, tokens).astype(F32) + branch
    hb_ref[...] = first_norm(s_ref, gain, shift)[0].astype(BF)


def other_up(other, side):
    return other[:, side * 32 : side * 32 + 32, :].reshape(HALF, HALF)


def other_down(other):
    return other[:, 64:128, :].reshape(UNITS, HALF)


def up_down_kernel(
    place, hb, up_own, down_own, other, b_up,
    ub_ref, slope_ref, mine_ref, theirs_ref, part_ref,
):
    shard = place[0]
    own, oth = hb[:, half_at(shard, True)], hb[:, half_at(shard, False)]
    for side in range(2):
        cols = pl.ds(side * HALF, HALF)
        before = mm(own, up_own[:, cols]) + mm(oth, other_up(other, side)) + b_up[:, cols].astype(F32)
        bell = 0.5 * (1.0 + lax.erf(before * ROOT_HALF))
        ub_ref[:, cols] = (before * bell).astype(BF)
        slope_ref[:, cols] = bell + before * DENSITY * jnp.exp(-0.5 * before * before)
    after = ub_ref[...]
    part_ref[:, half_at(shard, True)] = mm(after, down_own[...])
    part_ref[:, half_at(shard, False)] = mm(after, other_down(other))
    split_halves(place, part_ref, mine_ref, theirs_ref)


def second_norm_kernel(
    place, first, chip, recv, extra, gain, shift, cot, out_ref, dx_ref, dz_ref, sums_ref, keep
):
    far = place[3]
    middle = first_norm(first, gain, shift)[0]
    gains = gain[1:2, :].astype(F32)
    branch = chip[...].astype(F32) + recv[...].astype(F32) + extra[1:2, :].astype(F32)
    hidden, normed, factor = norm_rows(middle + branch, gains, shift[1:2, :].astype(F32))
    keep[...] = hidden
    out_ref[...] = keep[pl.ds(pl.multiple_of(far * 32, 32), 32), :]
    grad = core_rows(place, cot)
    back = norm_back(grad, normed, factor, gains)
    dx_ref[...] = back
    low = back.astype(BF)
    dz_ref[...] = low
    sums_ref[0:1, :] = jnp.sum(low.astype(F32), axis=0, keepdims=True)
    sums_ref[1:2, :] = jnp.sum(grad * normed, axis=0, keepdims=True)
    sums_ref[2:3, :] = jnp.sum(grad, axis=0, keepdims=True)
    sums_ref[3:8, :] = jnp.zeros((5, D), F32)


def down_up_kernel(
    place, dz, slope, up_own, down_own, other, da_ref, mine_ref, theirs_ref, part_ref
):
    shard = place[0]
    own, oth = dz[:, half_at(shard, True)], dz[:, half_at(shard, False)]
    after = mm(own, down_own[...], NT) + mm(oth, other_down(other), NT)
    da_ref[...] = (after * slope[...]).astype(BF)
    before = da_ref[...]
    part_ref[:, half_at(shard, True)] = mm(before, up_own[...], NT)
    part_ref[:, half_at(shard, False)] = sum(
        mm(before[:, side * HALF : (side + 1) * HALF], other_up(other, side), NT) for side in range(2)
    )
    split_halves(place, part_ref, mine_ref, theirs_ref)


def unit_grads_kernel(place, hb, da, ub, dz, pair_fwd, pair_dz, pair_da, out_ref):
    shard = place[0]
    rows = jnp.concatenate([hb[:, half_at(shard, True)], pair_fwd[:, 0:512]], axis=0)
    units = jnp.concatenate([da[...], pair_da[...]], axis=0)
    after = jnp.concatenate([ub[...], pair_fwd[:, 512:1536]], axis=0)
    grads = jnp.concatenate([dz[:, half_at(shard, True)], pair_dz[...]], axis=0)
    for part in range(4):
        cols = slice(part * COLS, (part + 1) * COLS)
        term = mm(rows, units[:, cols], TN).astype(BF)
        out_ref[:, part * 32 : part * 32 + 32, :] = term.reshape(RING, 32, COLS)
    for side in range(2):
        cols = slice(side * COLS, (side + 1) * COLS)
        term = mm(after, grads[:, cols], TN).astype(BF)
        out_ref[:, 128 + side * 64 : 192 + side * 64, :] = term.reshape(RING, 64, COLS)
    total = jnp.sum(units.astype(F32), axis=0, keepdims=True)
    small = jnp.concatenate(
        [total[:, part * COLS : (part + 1) * COLS] for part in range(4)]
        + [jnp.zeros((12, COLS), F32)],
        axis=0,
    ).astype(BF)
    for index in range(RING):
        out_ref[index, 256:272, :] = small


def first_back_kernel(
    place, first, dx, chip, recv, gain, shift, sums_in, d_ref, low_ref, sums_ref, keep
):
    far = place[3]
    _, normed, factor = first_norm(first, gain, shift)
    grad = dx[...] + (chip[...].astype(F32) + recv[...].astype(F32))
    back = norm_back(grad, normed, factor, gain[0:1, :].astype(F32))
    keep[...] = back
    d_ref[...] = keep[pl.ds(pl.multiple_of(far * 32, 32), 32), :]
    low = back.astype(BF)
    low_ref[...] = low
    sums_ref[...] = sums_in[...]
    sums_ref[3:4, :] = jnp.sum(low.astype(F32), axis=0, keepdims=True)
    sums_ref[4:5, :] = jnp.sum(grad * normed, axis=0, keepdims=True)
    sums_ref[5:6, :] = jnp.sum(grad, axis=0, keepdims=True)


def parts(row):
    high = row.astype(BF)
    rest = row - high.astype(F32)
    middle = rest.astype(BF)
    return (high, middle, (rest - middle.astype(F32)).astype(BF))


def out_back_kernel(
    place, low, o, lse, wo_own, wo_oth, own_ref, oth_ref, d_ref, delta_ref, pack_ref, nat_ref
):
    shard = place[0]
    nat_ref[0:32, :] = low[0, 0:32, :]
    nat_ref[32:64, :] = low[1, 0:32, :]
    nat_ref[64:96, :] = low[0, 32:64, :]
    nat_ref[96:128, :] = low[1, 32:64, :]
    own, oth = nat_ref[:, half_at(shard, True)], nat_ref[:, half_at(shard, False)]
    own_ref[...] = own
    oth_ref[...] = oth
    d_out = (mm(own, wo_own[...], NT) + mm(oth, wo_oth[...], NT)).astype(BF)
    d_ref[...] = d_out
    turned = (d_out.astype(F32) * o[...]).T
    delta = jnp.concatenate(
        [
            jnp.sum(turned[head * HD : (head + 1) * HD], axis=0, keepdims=True)
            for head in range(HEADS)
        ],
        axis=1,
    )
    delta_ref[...] = delta
    rows = [d_out]
    for row in parts(lse[...]) + parts(delta):
        rows += [row[:, 0:COLS], row[:, COLS : 2 * COLS]]
    rows.append(jnp.zeros((4, COLS), BF))
    packed = jnp.concatenate(rows, axis=0)
    for index in range(RING):
        pack_ref[index] = packed


def query_grad_kernel(place, q, k, v, d_out, lse, delta, id_q, id_k, dq_ref, acc_ref):
    q_heads = by_head(q[place[1]].reshape(BLK, COLS) * BF(HD ** -0.5))
    d_heads = by_head(d_out[...])
    acc_ref[...] = jnp.zeros_like(acc_ref)

    @pl.loop(0, RING // 2)
    def _(step):
        blocks = pl.ds(step * 2, 2)
        keys, values = k[blocks].reshape(256, COLS), v[blocks].reshape(256, COLS)
        allowed = id_k[blocks].reshape(256, 1) == id_q[...]
        probs = jnp.where(allowed, jnp.exp(mm(keys, q_heads, NT) - lse[...]), 0.0)
        d_scores = (probs * (mm(values, d_heads, NT) - delta[...])).astype(BF)
        acc_ref[...] += mm(d_scores, keys, TN)

    lane = lax.broadcasted_iota(jnp.int32, (BLK, COLS), 1) // HD
    total = jnp.zeros((BLK, COLS), F32)
    for head in range(HEADS):
        total = jnp.where(lane == head, acc_ref[head * BLK : (head + 1) * BLK, :], total)
    dq_ref[...] = (total * HD ** -0.5).astype(BF)


def key_grad_kernel(
    place, q, k, v, dq, recv, ids, id_k, w_own, w_oth, d_ref, mine_ref, theirs_ref, part_ref
):
    shard, block = place[0], place[1]
    keys, values = k[block].reshape(BLK, COLS), v[block].reshape(BLK, COLS)
    own_ids = id_k[block]

    def step(index, carry):
        d_key, d_value = carry
        q_heads = by_head(q[index].reshape(BLK, COLS) * BF(HD ** -0.5))
        d_heads = by_head(recv[index, 0:BLK, :])
        tail = recv[index, BLK : BLK + 16, :].astype(F32)
        rows = [
            jnp.concatenate(
                [tail[at + side : at + side + 1] + tail[at + 2 + side : at + 3 + side]
                 + tail[at + 4 + side : at + 5 + side] for side in range(2)],
                axis=1,
            )
            for at in (0, 6)
        ]
        allowed = own_ids == ids[index]
        probs = jnp.where(allowed, jnp.exp(mm(keys, q_heads, NT) - rows[0]), 0.0)
        d_scores = (probs * (mm(values, d_heads, NT) - rows[1])).astype(BF)
        return d_key + mm(d_scores, q_heads), d_value + mm(probs.astype(BF), d_heads)

    start = jnp.zeros((BLK, COLS), F32)
    d_key, d_value = lax.fori_loop(0, RING, step, (start, start), unroll=2)
    d_ref[:, 0:COLS] = dq[...]
    d_ref[:, COLS : 2 * COLS] = d_key.astype(BF)
    d_ref[:, 2 * COLS : 3 * COLS] = d_value.astype(BF)
    for own, weight in ((True, w_own), (False, w_oth)):
        part_ref[:, half_at(shard, own)] = (
            mm(d_ref[:, 0:COLS], weight[0], NT)
            + mm(d_ref[:, COLS : 2 * COLS], weight[1], NT)
            + mm(d_ref[:, 2 * COLS : 3 * COLS], weight[2], NT)
        )
    split_rows(place, part_ref, mine_ref, theirs_ref)


def ring_sum(recv, rows):
    total = recv[0, rows, :].astype(F32)
    for index in range(1, RING):
        total = total + recv[index, rows, :].astype(F32)
    return total


def in_grads_kernel(
    place, tokens, d, d_pair, pair_in, ob, low, low_pair, sums, out_ref
):
    shard = place[0]
    rows = jnp.concatenate([tokens[:, half_at(shard, True)], pair_in[:, 256:768]], axis=0)
    grads = jnp.concatenate([d[...], d_pair[...]], axis=0)
    for part in range(3):
        term = mm(rows, grads[:, part * COLS : (part + 1) * COLS], TN).astype(BF)
        out_ref[:, part * 32 : part * 32 + 32, :] = term.reshape(RING, 32, COLS)
    heads = jnp.concatenate([ob[...], pair_in[:, 0:256]], axis=0)
    outs = jnp.concatenate([low[...], low_pair[...]], axis=0)
    for side in range(2):
        term = mm(heads, outs[:, side * COLS : (side + 1) * COLS], TN).astype(BF)
        out_ref[:, 96 + side * 16 : 112 + side * 16, :] = term.reshape(RING, 16, COLS)
    wide = grads.astype(F32)
    small = jnp.concatenate(
        [
            sums[0:6, :],
            jnp.sum(wide[:, 0:COLS], axis=0, keepdims=True),
            jnp.sum(wide[:, 2 * COLS : 3 * COLS], axis=0, keepdims=True),
            jnp.zeros((8, COLS), F32),
        ],
        axis=0,
    ).astype(BF)
    for index in range(RING):
        out_ref[index, 128:144, :] = small


def unit_total_kernel(place, recv, low_ref, bias_ref):
    low_ref[...] = ring_sum(recv, slice(0, 256)).astype(BF)
    bias_ref[...] = ring_sum(recv, slice(256, 272))


def total_kernel(place, recv, small_ref, out_ref):
    total = ring_sum(recv, slice(0, 144))
    small_ref[...] = total[128:144]
    low = total[0:128].astype(BF)
    for index in range(RING):
        out_ref[index] = low


def unpack_units_kernel(place, recv, up_ref, down_ref):
    for part in range(4):
        up_ref[:, part * COLS : (part + 1) * COLS] = (
            recv[:, part * 32 : part * 32 + 32, :].reshape(HALF, COLS).astype(F32)
        )
    for side in range(2):
        down_ref[:, side * COLS : (side + 1) * COLS] = (
            recv[:, 128 + side * 64 : 192 + side * 64, :].reshape(UNITS, COLS).astype(F32)
        )


def unpack_kernel(place, recv, in_ref, out_ref):
    for part in range(3):
        in_ref[part] = recv[:, part * 32 : part * 32 + 32, :].reshape(HALF, COLS).astype(F32)
    for side in range(2):
        out_ref[:, side * COLS : (side + 1) * COLS] = (
            recv[:, 96 + side * 16 : 112 + side * 16, :].reshape(COLS, COLS).astype(F32)
        )


def swap(value, axis, bit):
    size = lax.axis_size(axis)
    return lax.ppermute(value, axis, [(index, index ^ bit) for index in range(size)])


def pair_gather(value):
    return lax.all_gather(value, "tensor", axis=0, axis_index_groups=[[0, 1], [2, 3]])


def tensor_sum(mine, theirs):
    chip = (mine.astype(F32) + swap(theirs, "tensor", 1).astype(F32)).astype(BF)
    return chip, swap(chip, "tensor", 2)


def shards(
    tokens, segment_ids, w_qkv, b_qv, w_out, w_up, b_up, w_down, out_bias, ln_gain, ln_bias, cotangent
):
    shard, block, tensor = (lax.axis_index(name) for name in ("shard", "context", "tensor"))
    core, far = tensor % 2, tensor // 2
    place = jnp.stack([shard, block, core, far]).astype(jnp.int32)
    w_in = jnp.transpose(w_qkv[0], (1, 0, 2))
    w_out, w_up, w_down = w_out[0], w_up[0], w_down[0]
    extra, gain, shift = out_bias[0], ln_gain[0], ln_bias[0]
    together = lax.optimization_barrier

    up_rows = lax.dynamic_slice_in_dim(w_up, block * 32, 32, 0)
    down_rows = lax.dynamic_slice_in_dim(w_down, block * 64, 64, 0)
    unit_rows = swap(
        jnp.concatenate([up_rows[:, :HALF], up_rows[:, HALF:], down_rows], axis=0), "shard", 1
    )
    other = lax.all_gather(unit_rows, "context", axis=0)
    in_oth = swap(w_in, "shard", 1)
    out_oth = swap(w_out, "shard", 1)

    spread = jnp.broadcast_to(
        lax.dynamic_slice_in_dim(tokens, core * 64, 64, 0)[None], (RING, 64, D)
    )
    spread, _ = together((spread, unit_rows))
    x_mine = lax.all_to_all(spread, "context", 0, 0, tiled=True)
    x_mine, in_oth, out_oth = together((x_mine, in_oth, out_oth))
    x_sib = swap(x_mine, "tensor", 1)

    id_q = lax.dynamic_slice_in_dim(segment_ids, block * BLK, BLK, 0)
    id_column = segment_ids.reshape(RING, BLK, 1)
    id_heads = jnp.tile(segment_ids.reshape(RING, 1, BLK), (1, 1, HEADS))
    all_heads = ((RING, 2, 64, COLS), BF)
    halves = [((64, D), BF), ((64, D), BF)]
    whole = pltpu.VMEM((BLK, D), F32)
    q, k, v, o, ob, lse, mine, theirs = call(
        attend_kernel, 10,
        [all_heads] * 3 + [((BLK, COLS), F32), ((BLK, COLS), BF), ((1, HEADS * BLK), F32)] + halves,
        place, x_mine, x_sib, w_in, in_oth, b_qv[0], id_q[:, None], segment_ids[None, :],
        w_out, out_oth,
        scratch=[whole], vmem=60,
    )
    chip, recv = tensor_sum(mine, theirs)
    first, low_mid = call(
        first_norm_kernel, 1, [((64, D), F32), ((64, D), BF)],
        place, tokens, chip, recv, extra, gain, shift,
    )
    hb = pair_gather(low_mid).reshape(BLK, D)
    ub, slope, mine, theirs = call(
        up_down_kernel, 2, [((BLK, UNITS), BF), ((BLK, UNITS), F32)] + halves,
        place, hb, w_up, w_down, other, b_up,
        scratch=[whole],
    )
    away = (1 - shard) * HALF
    pair_in = swap(
        jnp.concatenate([ob, lax.dynamic_slice_in_dim(tokens, away, HALF, 1)], axis=1), "shard", 1
    )
    pair_fwd = swap(
        jnp.concatenate([lax.dynamic_slice_in_dim(hb, away, HALF, 1), ub], axis=1), "shard", 1
    )
    chip, recv = tensor_sum(mine, theirs)
    hidden_out, dx, low_second, sums = call(
        second_norm_kernel, 2,
        [((32, D), F32), ((64, D), F32), ((64, D), BF), ((8, D), F32)],
        place, first, chip, recv, extra, gain, shift, cotangent,
        scratch=[pltpu.VMEM((64, D), F32)],
    )
    dz = pair_gather(low_second).reshape(BLK, D)
    pair_dz = swap(lax.dynamic_slice_in_dim(dz, away, HALF, 1), "shard", 1)
    da, mine, theirs = call(
        down_up_kernel, 2, [((BLK, UNITS), BF)] + halves,
        place, dz, slope, w_up, w_down, other,
        scratch=[whole],
    )
    pair_da = swap(da, "shard", 1)
    chip, recv = tensor_sum(mine, theirs)
    pair_da, chip = together((pair_da, chip))
    (unit_grads,) = call(
        unit_grads_kernel, 3, [((RING, 272, COLS), BF)],
        place, hb, da, ub, dz, pair_fwd, pair_dz, pair_da,
    )
    recv, unit_grads = together((recv, unit_grads))
    unit_recv = lax.all_to_all(unit_grads, "context", 0, 0, tiled=True)
    d_first, low_first, sums = call(
        first_back_kernel, 1.5,
        [((32, D), F32), ((64, D), BF), ((8, D), F32)],
        place, first, dx, chip, recv, gain, shift, sums,
        scratch=[pltpu.VMEM((64, D), F32)], vmem=60,
    )
    low_pairs = pair_gather(low_first)
    low_own, low_oth, d_out, delta, packed = call(
        out_back_kernel, 1.5,
        [
            ((BLK, HALF), BF), ((BLK, HALF), BF), ((BLK, COLS), BF), ((1, HEADS * BLK), F32),
            ((RING, 144, COLS), BF),
        ],
        place, low_pairs, o, lse, w_out, out_oth,
        scratch=[pltpu.VMEM((BLK, D), BF)],
    )
    packed, unit_recv = together((packed, unit_recv))
    packs = lax.all_to_all(packed, "context", 0, 0, tiled=True)
    unit_total, unit_small = call(
        unit_total_kernel, 1, [((COLS, COLS), BF), ((16, COLS), F32)], place, unit_recv
    )
    unit_all = lax.all_gather(unit_total, "context", axis=0)
    packs, unit_total = together((packs, unit_total))
    low_pair = swap(low_oth, "shard", 1)
    sums = sums + swap(sums, "tensor", 1)
    sums = lax.dynamic_slice_in_dim(sums, tensor * COLS, COLS, 1)
    sums = sums + swap(sums, "shard", 1)
    (dq,) = call(
        query_grad_kernel, 5, [((BLK, COLS), BF)],
        place, q, k, v, d_out, lse, delta, jnp.tile(id_q[None, :], (1, HEADS)), id_column,
        scratch=[pltpu.VMEM((HEADS * BLK, COLS), F32)], vmem=60,
    )
    d_mixed, mine, theirs = call(
        key_grad_kernel, 6, [((BLK, 3 * COLS), BF)] + halves,
        place, q, k, v, dq, packs, id_heads, id_column, w_in, in_oth,
        scratch=[whole], vmem=60,
    )
    d_pair = swap(d_mixed, "shard", 1)
    chip = mine.astype(F32) + swap(theirs, "tensor", 1).astype(F32)
    chip_far = lax.dynamic_slice_in_dim(chip, (1 - far) * 32, 32, 0).astype(BF)
    chip_near = lax.dynamic_slice_in_dim(chip, far * 32, 32, 0)
    grad_tokens = d_first + (chip_near + swap(chip_far, "tensor", 2).astype(F32))
    (in_grads,) = call(
        in_grads_kernel, 2.5, [((RING, 144, COLS), BF)],
        place, tokens, d_mixed, d_pair, pair_in, ob, low_own, low_pair, sums,
    )
    recv = lax.all_to_all(in_grads, "context", 0, 0, tiled=True)
    small, totals = call(
        total_kernel, 2, [((16, COLS), F32), ((RING, 128, COLS), BF)], place, recv
    )
    recv = lax.all_to_all(totals, "context", 0, 0, tiled=True)
    grad_in, grad_w_out = call(
        unpack_kernel, 2, [((3, HALF, COLS), F32), ((COLS, HALF), F32)], place, recv
    )
    grad_w_up, grad_w_down = call(
        unpack_units_kernel, 2, [((HALF, UNITS), F32), ((UNITS, HALF), F32)], place, unit_all
    )
    return (
        hidden_out,
        grad_tokens,
        jnp.transpose(grad_in, (1, 0, 2))[None],
        grad_w_out[None],
        grad_w_up[None],
        grad_w_down[None],
        small[6:8][None],
        unit_small[0:4].reshape(1, UNITS),
        jnp.stack([small[3], small[0]])[None],
        jnp.stack([small[4], small[1]])[None],
        jnp.stack([small[5], small[2]])[None],
    )


def solution(mesh):
    rows = P(("shard", "context"), None)
    own_rows = P(("shard", "context", "tensor"), None)
    by_column = P(None, None, "tensor")
    in_specs = (
        rows,
        P("shard"),
        P(None, "shard", None, "tensor"),
        by_column,
        P(None, "tensor", "shard"),
        P(None, "shard", "tensor"),
        P(None, "tensor"),
        P(None, "tensor", "shard"),
        P(),
        P(),
        P(),
        rows,
    )
    out_specs = (
        own_rows,
        own_rows,
        P(None, "shard", None, "tensor"),
        P(None, "tensor", "shard"),
        P(None, "shard", "tensor"),
        P(None, "tensor", "shard"),
        by_column,
        P(None, "tensor"),
        by_column,
        by_column,
        by_column,
    )
    return jax.shard_map(shards, mesh=mesh, in_specs=in_specs, out_specs=out_specs, check_vma=False)
```

time: 326 us -> 262 us (0.80)
  blocking collectives: 42.5 us -> 6.34 us
  waiting for transfers between devices: 151 us -> 121 us
  Pallas kernels: 35.6 us -> 51.2 us
  local copies, waits for them, and re-layouts: 31.2 us -> 19.3 us
  other arithmetic: 12.7 us -> 3.55 us
  starting transfers between devices: 37.6 us -> 44.7 us
    psum x1 -> x0, waiting for transfers between devices: 63.7 us -> none  [shards(): unit_total = lax.psum(unit_grads, 'context')]
    all_to_all x1 -> x0, blocking collectives: 36.6 us -> none  [shards(): lax.all_to_all(jnp.broadcast_to(mine[None], (RING, BLK, HALF)), 'context'...]
    all_to_all x1 -> x3, waiting for transfers between devices: 3.01 us -> 38.2 us  [the longest x1 26.2 us: shards(): unit_recv = lax.all_to_all(unit_grads, 'context', 0, 0, tiled=True)]
    all_to_all x1, waiting for transfers between devices: 0.01 us -> 16.7 us  [shards(): recv = lax.all_to_all(in_grads, 'context', 0, 0, tiled=True)]
    pallas_call x12 -> x15, Pallas kernels: 35.6 us -> 51.2 us  [call(): pl.pallas_call(kernel, out_shape=[jax.ShapeDtypeStruct(shape, dtype) for...]
    ppermute x17 -> x20, waiting for transfers between devices: 67.5 us -> 52.3 us  [swap(): lax.ppermute(value, axis, [(index, index ^ bit) for index in range(size)])]
    all_to_all x1 -> x3, starting transfers between devices: 4.94 us -> 16.5 us  [the longest x1 8.43 us: shards(): x_mine = lax.all_to_all(spread, 'context', 0, 0, tiled=True)]
    unnamed x114 -> x82, local copies, waits for them, and re-layouts: 21.1 us -> 10.9 us
  transfers between devices with their start and end apart: 23 -> 27, of which waited for: 17 -> 17; matrix products, arithmetic and copies ran while one was open for 6% -> 4% of each run, Pallas kernels for 5% -> 18%
where the time goes in v2:
time: 262 us; the launch traced here: 261 us
  waiting for transfers between devices  121 us (46%)
  Pallas kernels  51.2 us (20%)
  starting transfers between devices  44.7 us (17%)
  local copies, waits for them, and re-layouts  19.3 us (7%)
  between operations  14.5 us (6%)
  blocking collectives  6.34 us (2%)
  other arithmetic  3.55 us (1%)
    ppermute x20, waiting for transfers between devices, swap(): lax.ppermute(value, axis, [(index, index ^ bit) for index in range(size)])  52.3 us
    pallas_call x15, Pallas kernels, call(): pl.pallas_call(kernel, out_shape=[jax.ShapeDtypeStruct(shape, dtype) for...  51.2 us
    all_to_all x1, waiting for transfers between devices, shards(): unit_recv = lax.all_to_all(unit_grads, 'context', 0, 0, tiled=True)  26.2 us
    ppermute x20, starting transfers between devices, swap(): lax.ppermute(value, axis, [(index, index ^ bit) for index in range(size)])  20.3 us
    all_to_all x1, waiting for transfers between devices, shards(): recv = lax.all_to_all(in_grads, 'context', 0, 0, tiled=True)  16.7 us
    all_to_all x1, waiting for transfers between devices, shards(): recv = lax.all_to_all(totals, 'context', 0, 0, tiled=True)  13.7 us
    unnamed x82, local copies, waits for them, and re-layouts  10.9 us
    all_to_all x1, starting transfers between devices, shards(): x_mine = lax.all_to_all(spread, 'context', 0, 0, tiled=True)  8.43 us
  transfers between devices with their start and end apart: 27, of which 17 were waited for; matrix products, arithmetic and copies ran while one was open for 4% of the time, Pallas kernels for 18%

profile of v2, /device:TPU:0, one launch (start us, length us, event | category | flops | bytes accessed | tf_op | source)
XLA Modules:
  0.0 260.5 jit_solution(12537417617903982764)
XLA Ops:
  7.2 0.8 dynamic-slice_bitcast_fusion.1
  8.0 0.8 dynamic-slice_bitcast_fusion
  8.9 1.7 collective-permute-start
  10.6 0.9 constant_dynamic-slice_fusion.3
  11.5 2.6 collective-permute-done
  14.1 1.6 broadcast_in_dim.36
  15.6 8.4 %all-to-all-start = ((bf16[16,64,1024]{2,1,0:T(8,128)(2,1)}), bf16[16,64,1024]{2,1,0:T(8,128)(2,1)S(1)}, u32[]{:S(2)}, u32[]{:S(2)}) async-start(bf16[16,64,1024]{2,1,0:T(8,128)(2,1)} %broadcast_in_dim.36), calls=%async_computation | async-start | bytes 4194304 | tf_op jit(solution)/shard_map/all_to_all | solution.py:459
  24.1 1.6 collective-permute-start.1
  26.3 21.9 %collective-permute-done.2.wo_oth = bf16[256,512]{1,0:T(8,128)(2,1)S(1)} collective-permute-done((bf16[256,512]{1,0:T(8,128)(2,1)S(1)}, bf16[256,512]{1,0:T(8,128)(2,1)S(1)}, u32[]{:S(2)}, u32[]{:S(2)}) %collective-permute-start.2) | collective-permute-done | bytes 262176 | tf_op jit(solution)/shard_map/ppermute | solution.py:423
  48.2 5.9 %all-to-all-done.x_mine = bf16[16,64,1024]{2,1,0:T(8,128)(2,1)S(1)} async-done(((bf16[16,64,1024]{2,1,0:T(8,128)(2,1)}), bf16[16,64,1024]{2,1,0:T(8,128)(2,1)S(1)}, u32[]{:S(2)}, u32[]{:S(2)}) %all-to-all-start) | async-done | bytes 2097184 | tf_op jit(solution)/shard_map/all_to_all | solution.py:459
  54.1 0.8 dynamic-slice_bitcast_fusion.2
  54.8 0.7 copy.24.id_q
  56.1 2.2 collective-permute-done.3.x_sib
  58.4 10.9 %shard_map.203 = (bf16[16,2,64,256]{3,2,1,0:T(8,128)(2,1)}, bf16[16,2,64,256]{3,2,1,0:T(8,128)(2,1)}, bf16[16,2,64,256]{3,2,1,0:T(8,128)(2,1)}, f32[128,256]{1,0...) custom-call(s32[4]{0:T(128)} %pad_add_fusion.place, ...), custom_call_target="tpu_custom_call" | custom-call | flops 11000000512 | bytes 30000000 | tf_op jit(solution)/shard_map/pallas_call | solution.py:38
  69.5 1.4 collective-permute-done.4
  70.9 0.9 add_convert_fusion.2.chip
  71.8 3.2 %collective-permute-start.5 = (bf16[64,1024]{1,0:T(8,128)(2,1)S(1)}, bf16[64,1024]{1,0:T(8,128)(2,1)S(1)}, u32[]{:S(2)}, u32[]{:S(2)}) collective-permute-start(bf16[64,1024]{1,0:T(8,128)(2,1)S(1)} %add_convert_fusion.2.chip), channel_id=1, source_target_pairs={{0,2},{1,3},{2,0},{3,1},{4,6},{5,7},{6,4},{7,5},{8,10},{9,11},{10,... | collective-permute-start | bytes 393224 | tf_op jit(solution)/shard_map/ppermute | solution.py:423
  75.0 4.0 %collective-permute-done.5.recv = bf16[64,1024]{1,0:T(8,128)(2,1)S(1)} collective-permute-done((bf16[64,1024]{1,0:T(8,128)(2,1)S(1)}, bf16[64,1024]{1,0:T(8,128)(2,1)S(1)}, u32[]{:S(2)}, u32[]{:S(2)}) %collective-permute-start.5) | collective-permute-done | bytes 131104 | tf_op jit(solution)/shard_map/ppermute | solution.py:423
  79.0 0.8 shard_map.204
  80.5 2.0 all-gather.hb
  82.5 1.6 copy-done.9
  84.1 1.5 shard_map.205
  85.6 0.8 copy-done.21
  86.6 1.2 collective-permute-done.6
  87.8 3.2 %collective-permute-start.7 = (bf16[64,1024]{1,0:T(8,128)(2,1)S(1)}, bf16[64,1024]{1,0:T(8,128)(2,1)S(1)}, u32[]{:S(2)}, u32[]{:S(2)}) collective-permute-start(bf16[64,1024]{1,0:T(8,128)(2,1)S(1)} %add_convert_fusion.1.chip), channel_id=1, source_target_pairs={{0,2},{1,3},{2,0},{3,1},{4,6},{5,7},{6,4},{7,5},{8,10},{9,11},{10,... | collective-permute-start | bytes 393224 | tf_op jit(solution)/shard_map/ppermute | solution.py:423
  91.0 0.7 collective-permute-start.11
  91.7 4.0 %collective-permute-done.7.recv = bf16[64,1024]{1,0:T(8,128)(2,1)S(1)} collective-permute-done((bf16[64,1024]{1,0:T(8,128)(2,1)S(1)}, bf16[64,1024]{1,0:T(8,128)(2,1)S(1)}, u32[]{:S(2)}, u32[]{:S(2)}) %collective-permute-start.7) | collective-permute-done | bytes 131104 | tf_op jit(solution)/shard_map/ppermute | solution.py:423
  95.7 1.0 copy-done.11
  96.8 0.9 copy-done.24
  97.7 1.6 shard_map.206
  99.3 2.0 all-gather.2.dz
  101.3 2.1 shard_map.207
  103.6 1.5 collective-permute-start.8
  105.8 3.2 %collective-permute-start.10 = (bf16[64,1024]{1,0:T(8,128)(2,1)S(1)}, bf16[64,1024]{1,0:T(8,128)(2,1)S(1)}, u32[]{:S(2)}, u32[]{:S(2)}) collective-permute-start(bf16[64,1024]{1,0:T(8,128)(2,1)S(1)} %add_convert_fusion.chip), channel_id=1, source_target_pairs={{0,2},{1,3},{2,0},{3,1},{4,6},{5,7},{6,4},{7,5},{8,10},{9,11},{10,... | collective-permute-start | bytes 393224 | tf_op jit(solution)/shard_map/ppermute | solution.py:423
  109.0 3.8 %collective-permute-done.8.pair_da = bf16[128,1024]{1,0:T(8,128)(2,1)S(1)} collective-permute-done((bf16[128,1024]{1,0:T(8,128)(2,1)S(1)}, bf16[128,1024]{1,0:T(8,128)(2,1)S(1)}, u32[]{:S(2)}, u32[]{:S(2)}) %collective-permute-start.8) | collective-permute-done | bytes 262176 | tf_op jit(solution)/shard_map/ppermute | solution.py:423
  112.8 2.8 %collective-permute-done.12.pair_dz = bf16[128,512]{1,0:T(8,128)(2,1)S(1)} collective-permute-done((bf16[128,512]{1,0:T(8,128)(2,1)S(1)}, bf16[128,512]{1,0:T(8,128)(2,1)S(1)}, u32[]{:S(2)}, u32[]{:S(2)}) %collective-permute-start.12) | collective-permute-done | bytes 131104 | tf_op jit(solution)/shard_map/ppermute | solution.py:423
  115.6 1.3 shard_map.208
  116.9 1.3 copy-done
  118.2 1.9 collective-permute-done.10.recv
  120.8 3.7 %all-to-all-start.1 = ((bf16[16,272,256]{2,1,0:T(8,128)(2,1)}), bf16[16,272,256]{2,1,0:T(8,128)(2,1)S(1)}, u32[]{:S(2)}, u32[]{:S(2)}) async-start(bf16[16,272,256]{2,1,0:T(8,128)(2,1)} %copy-done), calls=%async_computation.1 | async-start | bytes 4456448 | tf_op jit(solution)/shard_map/all_to_all | solution.py:516
  124.6 2.3 shard_map.209
  126.8 2.4 all-gather.3
  129.2 2.0 shard_map.210
  131.8 26.2 %all-to-all-done.1.recv = bf16[16,272,256]{2,1,0:T(8,128)(2,1)S(1)} async-done(((bf16[16,272,256]{2,1,0:T(8,128)(2,1)}), bf16[16,272,256]{2,1,0:T(8,128)(2,1)S(1)}, u32[]{:S(2)}, u32[]{:S(2)}) %all-to-all-start.1) | async-done | bytes 2228256 | tf_op jit(solution)/shard_map/all_to_all | solution.py:516
  158.0 4.4 %all-to-all-start.2 = ((bf16[16,144,256]{2,1,0:T(8,128)(2,1)}), bf16[16,144,256]{2,1,0:T(8,128)(2,1)}, u32[]{:S(2)}, u32[]{:S(2)}) async-start(bf16[16,144,256]{2,1,0:T(8,128)(2,1)} %get-tuple-element.95), calls=%async_computation.2 | async-start | bytes 2359296 | tf_op jit(solution)/shard_map/all_to_all | solution.py:534
  162.6 1.3 copy.25.id_k
  164.2 1.5 shard_map.212
  166.3 8.1 %shard_map.211.dq = bf16[128,256]{1,0:T(8,128)(2,1)} custom-call(s32[4]{0:T(128)} %pad_add_fusion.place, bf16[16,2,64,256]{3,2,1,0:T(8,128)(2,1)} %get-tuple-element.85.q, bf16[16,2,64,256]{3,2,1,0:T(8,128)(2,1)} %get-tuple-element.86.k, bf16[16,2,64,256]{3,2,1,0:T(8,128)(2,1)} %get-tuple-element.87.v, bf16[128,256]{1,0:T(8,128)(2,1)} %copy-done.27, ...), custom_call_target="tpu_custom_call" | custom-call | flops 5500000256 | bytes 15000000 | tf_op jit(solution)/shard_map/pallas_call | solution.py:38
  174.4 6.1 %all-to-all-done.2.recv = bf16[16,144,256]{2,1,0:T(8,128)(2,1)} async-done(((bf16[16,144,256]{2,1,0:T(8,128)(2,1)}), bf16[16,144,256]{2,1,0:T(8,128)(2,1)}, u32[]{:S(2)}, u32[]{:S(2)}) %all-to-all-start.2) | async-done | bytes 1179680 | tf_op jit(solution)/shard_map/all_to_all | solution.py:534
  181.1 10.9 %shard_map.213 = (bf16[128,768]{1,0:T(8,128)(2,1)}, bf16[64,1024]{1,0:T(8,128)(2,1)}, bf16[64,1024]{1,0:T(8,128)(2,1)}) custom-call(s32[4]{0:T(128)} %pad_add_fusion.place, bf16[16,2,64,256]{3,2,1,0:T(8,128)(2,1)} %get-tuple-element.85.q, bf16[16,2,64,256]{3,2,1,0:T(8,128)(2,1)} %get-tuple-element.86.k, bf16[16,2,64,256]{3,2,1,0:T(8,128)(2,1)} %get-tuple-element.87.v, ...), custom_call_target="tpu_custom_call" | custom-call | flops 6600000000 | bytes 18000000 | tf_op jit(solution)/shard_map/pallas_call | solution.py:38
  192.2 1.9 collective-permute-start.17
  194.1 1.2 collective-permute-start.19
  195.3 5.2 %collective-permute-done.19 = f32[8,256]{1,0:T(8,128)S(1)} collective-permute-done((f32[8,256]{1,0:T(8,128)S(1)}, f32[8,256]{1,0:T(8,128)S(1)}, u32[]{:S(2)}, u32[]{:S(2)}) %collective-permute-start.19) | collective-permute-done | bytes 8224 | tf_op jit(solution)/shard_map/ppermute | solution.py:423
  200.5 0.9 copy-done.16
  201.5 2.0 shard_map.214
  203.5 4.0 %all-to-all-start.3 = ((bf16[16,144,256]{2,1,0:T(8,128)(2,1)}), bf16[16,144,256]{2,1,0:T(8,128)(2,1)S(1)}, u32[]{:S(2)}, u32[]{:S(2)}) async-start(bf16[16,144,256]{2,1,0:T(8,128)(2,1)} %shard_map.214), calls=%async_computation.3 | async-start | bytes 2359296 | tf_op jit(solution)/shard_map/all_to_all | solution.py:563
  207.6 1.3 collective-permute-done.13
  209.1 16.7 %all-to-all-done.3.recv = bf16[16,144,256]{2,1,0:T(8,128)(2,1)S(1)} async-done(((bf16[16,144,256]{2,1,0:T(8,128)(2,1)}), bf16[16,144,256]{2,1,0:T(8,128)(2,1)S(1)}, u32[]{:S(2)}, u32[]{:S(2)}) %all-to-all-start.3) | async-done | bytes 1179680 | tf_op jit(solution)/shard_map/all_to_all | solution.py:563
  225.8 1.7 shard_map.215
  227.5 3.8 %all-to-all-start.4 = ((bf16[16,128,256]{2,1,0:T(8,128)(2,1)}), bf16[16,128,256]{2,1,0:T(8,128)(2,1)S(1)}, u32[]{:S(2)}, u32[]{:S(2)}) async-start(bf16[16,128,256]{2,1,0:T(8,128)(2,1)} %get-tuple-element.106), calls=%async_computation.4 | async-start | bytes 2097152 | tf_op jit(solution)/shard_map/all_to_all | solution.py:567
  233.8 13.7 %all-to-all-done.4.recv = bf16[16,128,256]{2,1,0:T(8,128)(2,1)S(1)} async-done(((bf16[16,128,256]{2,1,0:T(8,128)(2,1)}), bf16[16,128,256]{2,1,0:T(8,128)(2,1)S(1)}, u32[]{:S(2)}, u32[]{:S(2)}) %all-to-all-start.4) | async-done | bytes 1048608 | tf_op jit(solution)/shard_map/all_to_all | solution.py:567
  247.5 2.0 shard_map.216
  249.4 1.6 copy-done.8
  251.0 2.7 %shard_map.217 = (f32[512,1024]{1,0:T(8,128)}, f32[1024,512]{1,0:T(8,128)}) custom-call(s32[4]{0:T(128)S(1)} %copy-done.7, bf16[16,256,256]{2,1,0:T(8,128)(2,1)S(1)} %bitcast.51), custom_call_target="tpu_custom_call" | custom-call | flops 2200000000 | bytes 6000000 | tf_op jit(solution)/shard_map/pallas_call | solution.py:38
  (121 shorter events, 9.1 us)
Async XLA Ops:
  8.9 5.2 %collective-permute-start = (bf16[128,512]{1,0:T(8,128)(2,1)S(1)}, bf16[128,512]{1,0:T(8,128)(2,1)S(1)}, u32[]{:S(2)}, u32[]{:S(2)}) collective-permute-start(bf16[128,512]{1,0:T(8,128)(2,1)S(1)} %pad_maximum_fusion.2), channel_id=1, source_target_pairs={{0,64},{64,0},{1,65},{65,1},{2,66},{66,2},{3,67},{67,3},{4,68},{68... | collective-permute-start | bytes 393224 | tf_op jit(solution)/shard_map/ppermute | solution.py:423
  14.1 1.6 copy-start.33
  15.6 10.1 %copy-start.12 = (bf16[1,256,512]{2,1,0:T(8,128)(2,1)S(1)}, bf16[1,256,512]{2,1,0:T(8,128)(2,1)}, u32[]{:S(2)}) copy-start(bf16[1,256,512]{2,1,0:T(8,128)(2,1)} %param.16) | copy-start | bytes 786436
  15.6 38.4 %all-to-all-start = ((bf16[16,64,1024]{2,1,0:T(8,128)(2,1)}), bf16[16,64,1024]{2,1,0:T(8,128)(2,1)S(1)}, u32[]{:S(2)}, u32[]{:S(2)}) async-start(bf16[16,64,1024]{2,1,0:T(8,128)(2,1)} %broadcast_in_dim.36), calls=%async_computation | async-start | bytes 4194304 | tf_op jit(solution)/shard_map/all_to_all | solution.py:459
  24.1 58.4 %all-gather.8.cloned.1.call-start = ((), (), s32[]{:S(2)}) async-start(), calls=%async_computation.5 | async-start | bytes 2228224 | tf_op jit(solution)/shard_map/all_gather | solution.py:451
  24.1 24.0 %collective-permute-start.1 = (bf16[3,512,256]{2,1,0:T(8,128)(2,1)}, bf16[3,512,256]{2,1,0:T(8,128)(2,1)}, u32[]{:S(2)}, u32[]{:S(2)}) collective-permute-start(bf16[3,512,256]{2,1,0:T(8,128)(2,1)} %bitcast.7.w_own), channel_id=1, source_target_pairs={{0,64},{64,0},{1,65},{65,1},{2,66},{66,2},{3,67},{67,3},{4,68},{68... | collective-permute-start | bytes 2359304 | tf_op jit(solution)/shard_map/ppermute | solution.py:423
  25.7 22.5 %collective-permute-start.2 = (bf16[256,512]{1,0:T(8,128)(2,1)S(1)}, bf16[256,512]{1,0:T(8,128)(2,1)S(1)}, u32[]{:S(2)}, u32[]{:S(2)}) collective-permute-start(bf16[256,512]{1,0:T(8,128)(2,1)S(1)} %bitcast.55), channel_id=1, source_target_pairs={{0,64},{64,0},{1,65},{65,1},{2,66},{66,2},{3,67},{67,3},{4,68},{68... | collective-permute-start | bytes 786440 | tf_op jit(solution)/shard_map/ppermute | solution.py:423
  48.2 10.2 %copy-start.14 = (bf16[256,512]{1,0:T(8,128)(2,1)}, bf16[256,512]{1,0:T(8,128)(2,1)S(1)}, u32[]{:S(2)}) copy-start(bf16[256,512]{1,0:T(8,128)(2,1)S(1)} %collective-permute-done.2.wo_oth) | copy-start | bytes 786436
  54.1 4.3 %copy-start.31 = (bf16[16,64,1024]{2,1,0:T(8,128)(2,1)}, bf16[16,64,1024]{2,1,0:T(8,128)(2,1)S(1)}, u32[]{:S(2)}) copy-start(bf16[16,64,1024]{2,1,0:T(8,128)(2,1)S(1)} %all-to-all-done.x_mine) | copy-start | bytes 6291460
  54.1 4.3 %collective-permute-start.3 = (bf16[16,64,1024]{2,1,0:T(8,128)(2,1)S(1)}, bf16[16,64,1024]{2,1,0:T(8,128)(2,1)}, u32[]{:S(2)}, u32[]{:S(2)}) collective-permute-start(bf16[16,64,1024]{2,1,0:T(8,128)(2,1)S(1)} %all-to-all-done.x_mine), channel_id=1, source_target_pairs={{0,1},{1,0},{2,3},{3,2},{4,5},{5,4},{6,7},{7,6},{8,9},{9,8},{10,11... | collective-permute-start | bytes 6291464 | tf_op jit(solution)/shard_map/ppermute | solution.py:423
  58.4 20.6 %copy-start.1 = (bf16[128,1024]{1,0:T(8,128)(2,1)S(1)}, bf16[128,1024]{1,0:T(8,128)(2,1)}, u32[]{:S(2)}) copy-start(bf16[128,1024]{1,0:T(8,128)(2,1)} %tokens.3) | copy-start | bytes 786436
  58.4 20.6 %copy-start.5 = (s32[4]{0:T(128)S(1)}, s32[4]{0:T(128)}, u32[]{:S(2)}) copy-start(s32[4]{0:T(128)} %pad_add_fusion.place) | copy-start | bytes 52
  58.4 20.6 %copy-start.18 = (bf16[1,2,1024]{2,1,0:T(2,128)(2,1)S(1)}, bf16[1,2,1024]{2,1,0:T(2,128)(2,1)}, u32[]{:S(2)}) copy-start(bf16[1,2,1024]{2,1,0:T(2,128)(2,1)} %param.20) | copy-start | bytes 12292
  58.4 20.6 %copy-start.19 = (bf16[1,2,1024]{2,1,0:T(2,128)(2,1)S(1)}, bf16[1,2,1024]{2,1,0:T(2,128)(2,1)}, u32[]{:S(2)}) copy-start(bf16[1,2,1024]{2,1,0:T(2,128)(2,1)} %param.21) | copy-start | bytes 12292
  58.4 20.6 %copy-start.20 = (bf16[1,2,1024]{2,1,0:T(2,128)(2,1)S(1)}, bf16[1,2,1024]{2,1,0:T(2,128)(2,1)}, u32[]{:S(2)}) copy-start(bf16[1,2,1024]{2,1,0:T(2,128)(2,1)} %param.22) | copy-start | bytes 12292
  69.3 1.6 collective-permute-start.4
  71.8 7.1 %collective-permute-start.5 = (bf16[64,1024]{1,0:T(8,128)(2,1)S(1)}, bf16[64,1024]{1,0:T(8,128)(2,1)S(1)}, u32[]{:S(2)}, u32[]{:S(2)}) collective-permute-start(bf16[64,1024]{1,0:T(8,128)(2,1)S(1)} %add_convert_fusion.2.chip), channel_id=1, source_target_pairs={{0,2},{1,3},{2,0},{3,1},{4,6},{5,7},{6,4},{7,5},{8,10},{9,11},{10,... | collective-permute-start | bytes 393224 | tf_op jit(solution)/shard_map/ppermute | solution.py:423
  79.0 3.5 %copy-start.3 = (bf16[1,512,1024]{2,1,0:T(8,128)(2,1)S(1)}, bf16[1,512,1024]{2,1,0:T(8,128)(2,1)}, u32[]{:S(2)}) copy-start(bf16[1,512,1024]{2,1,0:T(8,128)(2,1)} %param.17) | copy-start | bytes 3145732
  79.0 3.5 %copy-start.4 = (bf16[1,1024,512]{2,1,0:T(8,128)(2,1)S(1)}, bf16[1,1024,512]{2,1,0:T(8,128)(2,1)}, u32[]{:S(2)}) copy-start(bf16[1,1024,512]{2,1,0:T(8,128)(2,1)} %param.19) | copy-start | bytes 3145732
  79.0 3.5 %copy-start.17 = (bf16[1,1024]{1,0:T(2,128)(2,1)S(1)}, bf16[1,1024]{1,0:T(2,128)(2,1)}, u32[]{:S(2)}) copy-start(bf16[1,1024]{1,0:T(2,128)(2,1)} %b_up.1) | copy-start | bytes 6148
  82.5 1.6 copy-start.9
  85.6 0.8 copy-start.21
  86.4 1.3 collective-permute-start.6
  87.8 7.9 %collective-permute-start.7 = (bf16[64,1024]{1,0:T(8,128)(2,1)S(1)}, bf16[64,1024]{1,0:T(8,128)(2,1)S(1)}, u32[]{:S(2)}, u32[]{:S(2)}) collective-permute-start(bf16[64,1024]{1,0:T(8,128)(2,1)S(1)} %add_convert_fusion.1.chip), channel_id=1, source_target_pairs={{0,2},{1,3},{2,0},{3,1},{4,6},{5,7},{6,4},{7,5},{8,10},{9,11},{10,... | collective-permute-start | bytes 393224 | tf_op jit(solution)/shard_map/ppermute | solution.py:423
  91.0 21.8 %collective-permute-start.11 = (bf16[128,1536]{1,0:T(8,128)(2,1)S(1)}, bf16[128,1536]{1,0:T(8,128)(2,1)S(1)}, u32[]{:S(2)}, u32[]{:S(2)}) collective-permute-start(bf16[128,1536]{1,0:T(8,128)(2,1)S(1)} %pad_maximum_fusion), channel_id=1, source_target_pairs={{0,64},{64,0},{1,65},{65,1},{2,66},{66,2},{3,67},{67,3},{4,68},{68... | collective-permute-start | bytes 1179656 | tf_op jit(solution)/shard_map/ppermute | solution.py:423
  95.7 1.0 copy-start.11
  96.8 0.9 copy-start.24
  97.7 3.6 %copy-start.10 = (bf16[2048,512]{1,0:T(8,128)(2,1)S(1)}, bf16[2048,512]{1,0:T(8,128)(2,1)}, u32[]{:S(2)}) copy-start(bf16[2048,512]{1,0:T(8,128)(2,1)} %all-gather.8.cloned.1.call-done) | copy-start | bytes 6291460
  97.7 3.6 %copy-start.22 = (f32[128,1024]{1,0:T(8,128)S(1)}, f32[128,1024]{1,0:T(8,128)}, u32[]{:S(2)}) copy-start(f32[128,1024]{1,0:T(8,128)} %copy-done.21) | copy-start | bytes 1572868
  99.3 4.1 %copy-start.25 = (f32[64,1024]{1,0:T(8,128)}, f32[64,1024]{1,0:T(8,128)S(1)}, u32[]{:S(2)}) copy-start(f32[64,1024]{1,0:T(8,128)S(1)} %get-tuple-element.73.dx) | copy-start | bytes 786436
  99.3 4.1 %copy-start.28 = (f32[8,1024]{1,0:T(8,128)}, f32[8,1024]{1,0:T(8,128)S(1)}, u32[]{:S(2)}) copy-start(f32[8,1024]{1,0:T(8,128)S(1)} %get-tuple-element.83.sums_in) | copy-start | bytes 98308
  103.4 2.4 collective-permute-start.9
  103.6 9.1 %collective-permute-start.8 = (bf16[128,1024]{1,0:T(8,128)(2,1)S(1)}, bf16[128,1024]{1,0:T(8,128)(2,1)S(1)}, u32[]{:S(2)}, u32[]{:S(2)}) collective-permute-start(bf16[128,1024]{1,0:T(8,128)(2,1)S(1)} %get-tuple-element.76.da), channel_id=1, source_target_pairs={{0,64},{64,0},{1,65},{65,1},{2,66},{66,2},{3,67},{67,3},{4,68},{68... | collective-permute-start | bytes 786440 | tf_op jit(solution)/shard_map/ppermute | solution.py:423
  105.1 10.5 %collective-permute-start.12 = (bf16[128,512]{1,0:T(8,128)(2,1)S(1)}, bf16[128,512]{1,0:T(8,128)(2,1)S(1)}, u32[]{:S(2)}, u32[]{:S(2)}) collective-permute-start(bf16[128,512]{1,0:T(8,128)(2,1)S(1)} %constant_dynamic-slice_fusion.1), channel_id=1, source_target_pairs={{0,64},{64,0},{1,65},{65,1},{2,66},{66,2},{3,67},{67,3},{4,68},{68... | collective-permute-start | bytes 393224 | tf_op jit(solution)/shard_map/ppermute | solution.py:423
  105.8 11.1 %copy-start.32 = (bf16[64,1024]{1,0:T(8,128)(2,1)}, bf16[64,1024]{1,0:T(8,128)(2,1)S(1)}, u32[]{:S(2)}) copy-start(bf16[64,1024]{1,0:T(8,128)(2,1)S(1)} %add_convert_fusion.chip) | copy-start | bytes 393220
  105.8 14.3 %collective-permute-start.10 = (bf16[64,1024]{1,0:T(8,128)(2,1)S(1)}, bf16[64,1024]{1,0:T(8,128)(2,1)S(1)}, u32[]{:S(2)}, u32[]{:S(2)}) collective-permute-start(bf16[64,1024]{1,0:T(8,128)(2,1)S(1)} %add_convert_fusion.chip), channel_id=1, source_target_pairs={{0,2},{1,3},{2,0},{3,1},{4,6},{5,7},{6,4},{7,5},{8,10},{9,11},{10,... | collective-permute-start | bytes 393224 | tf_op jit(solution)/shard_map/ppermute | solution.py:423
  116.9 1.3 copy-start
  120.8 37.2 %all-to-all-start.1 = ((bf16[16,272,256]{2,1,0:T(8,128)(2,1)}), bf16[16,272,256]{2,1,0:T(8,128)(2,1)S(1)}, u32[]{:S(2)}, u32[]{:S(2)}) async-start(bf16[16,272,256]{2,1,0:T(8,128)(2,1)} %copy-done), calls=%async_computation.1 | async-start | bytes 4456448 | tf_op jit(solution)/shard_map/all_to_all | solution.py:516
  124.5 4.7 %copy-start.6 = (s32[4]{0:T(128)S(1)}, s32[4]{0:T(128)}, u32[]{:S(2)}) copy-start(s32[4]{0:T(128)} %pad_add_fusion.place) | copy-start | bytes 52
  124.5 4.7 %copy-start.13 = (bf16[1,256,512]{2,1,0:T(8,128)(2,1)S(1)}, bf16[1,256,512]{2,1,0:T(8,128)(2,1)}, u32[]{:S(2)}) copy-start(bf16[1,256,512]{2,1,0:T(8,128)(2,1)} %param.16) | copy-start | bytes 786436
  124.5 4.7 %copy-start.15 = (bf16[256,512]{1,0:T(8,128)(2,1)S(1)}, bf16[256,512]{1,0:T(8,128)(2,1)}, u32[]{:S(2)}) copy-start(bf16[256,512]{1,0:T(8,128)(2,1)} %copy-done.14) | copy-start | bytes 786436
  124.6 4.7 %copy-start.26 = (f32[128,256]{1,0:T(8,128)S(1)}, f32[128,256]{1,0:T(8,128)}, u32[]{:S(2)}) copy-start(f32[128,256]{1,0:T(8,128)} %get-tuple-element.89.o) | copy-start | bytes 393220
  124.6 4.7 %copy-start.29 = (f32[1,512]{1,0:T(1,128)S(1)}, f32[1,512]{1,0:T(1,128)}, u32[]{:S(2)}) copy-start(f32[1,512]{1,0:T(1,128)} %get-tuple-element.90.lse) | copy-start | bytes 6148
  131.8 32.1 %copy-start.27 = (bf16[128,256]{1,0:T(8,128)(2,1)}, bf16[128,256]{1,0:T(8,128)(2,1)S(1)}, u32[]{:S(2)}) copy-start(bf16[128,256]{1,0:T(8,128)(2,1)S(1)} %get-tuple-element.91.d_out) | copy-start | bytes 196612
  131.8 30.7 %copy-start.36 = (s32[2048]{0:T(1024)S(1)}, s32[2048]{0:T(1024)}, u32[]{:S(2)}) copy-start(s32[2048]{0:T(1024)} %param.13) | copy-start | bytes 24580
  131.8 32.1 %copy-start.2 = (bf16[128,256]{1,0:T(8,128)(2,1)S(1)}, bf16[128,256]{1,0:T(8,128)(2,1)}, u32[]{:S(2)}) copy-start(bf16[128,256]{1,0:T(8,128)(2,1)} %get-tuple-element.102.ob) | copy-start | bytes 196612
  158.0 22.5 %all-to-all-start.2 = ((bf16[16,144,256]{2,1,0:T(8,128)(2,1)}), bf16[16,144,256]{2,1,0:T(8,128)(2,1)}, u32[]{:S(2)}, u32[]{:S(2)}) async-start(bf16[16,144,256]{2,1,0:T(8,128)(2,1)} %get-tuple-element.95), calls=%async_computation.2 | async-start | bytes 2359296 | tf_op jit(solution)/shard_map/all_to_all | solution.py:534
  162.4 87.0 %all-gather.10.cloned.1.call-start = ((), (), s32[]{:S(2)}) async-start(), calls=%async_computation.6 | async-start | bytes 2228224 | tf_op jit(solution)/shard_map/all_gather | solution.py:538
  164.0 36.6 %collective-permute-start.16 = (bf16[128,768]{1,0:T(8,128)(2,1)S(1)}, bf16[128,768]{1,0:T(8,128)(2,1)S(1)}, u32[]{:S(2)}, u32[]{:S(2)}) collective-permute-start(bf16[128,768]{1,0:T(8,128)(2,1)S(1)} %pad_maximum_fusion.1), channel_id=1, source_target_pairs={{0,64},{64,0},{1,65},{65,1},{2,66},{66,2},{3,67},{67,3},{4,68},{68... | collective-permute-start | bytes 589832 | tf_op jit(solution)/shard_map/ppermute | solution.py:423
  181.1 11.1 %copy-start.37 = (f32[8,1024]{1,0:T(8,128)S(1)}, f32[8,1024]{1,0:T(8,128)}, u32[]{:S(2)}) copy-start(f32[8,1024]{1,0:T(8,128)} %get-tuple-element.105) | copy-start | bytes 98308
  181.1 19.4 %copy-start.7 = (s32[4]{0:T(128)S(1)}, s32[4]{0:T(128)}, u32[]{:S(2)}) copy-start(s32[4]{0:T(128)} %pad_add_fusion.place) | copy-start | bytes 52
  192.0 8.5 %collective-permute-start.15 = (bf16[128,768]{1,0:T(8,128)(2,1)}, bf16[128,768]{1,0:T(8,128)(2,1)S(1)}, u32[]{:S(2)}, u32[]{:S(2)}) collective-permute-start(bf16[128,768]{1,0:T(8,128)(2,1)} %get-tuple-element.101.d), channel_id=1, source_target_pairs={{0,64},{64,0},{1,65},{65,1},{2,66},{66,2},{3,67},{67,3},{4,68},{68... | collective-permute-start | bytes 589832 | tf_op jit(solution)/shard_map/ppermute | solution.py:423
  192.2 1.9 collective-permute-start.18
  192.2 8.3 %collective-permute-start.17 = (bf16[128,512]{1,0:T(8,128)(2,1)S(1)}, bf16[128,512]{1,0:T(8,128)(2,1)S(1)}, u32[]{:S(2)}, u32[]{:S(2)}) collective-permute-start(bf16[128,512]{1,0:T(8,128)(2,1)S(1)} %get-tuple-element.104), channel_id=1, source_target_pairs={{0,64},{64,0},{1,65},{65,1},{2,66},{66,2},{3,67},{67,3},{4,68},{68... | collective-permute-start | bytes 393224 | tf_op jit(solution)/shard_map/ppermute | solution.py:423
  194.1 6.4 %collective-permute-start.19 = (f32[8,256]{1,0:T(8,128)S(1)}, f32[8,256]{1,0:T(8,128)S(1)}, u32[]{:S(2)}, u32[]{:S(2)}) collective-permute-start(f32[8,256]{1,0:T(8,128)S(1)} %dynamic-slice_add_fusion), channel_id=1, source_target_pairs={{0,64},{64,0},{1,65},{65,1},{2,66},{66,2},{3,67},{67,3},{4,68},{68... | collective-permute-start | bytes 24584 | tf_op jit(solution)/shard_map/ppermute | solution.py:423
  200.5 0.9 copy-start.16
  203.5 4.0 %copy-start.38 = (bf16[64,1024]{1,0:T(8,128)(2,1)S(1)}, bf16[64,1024]{1,0:T(8,128)(2,1)}, u32[]{:S(2)}) copy-start(bf16[64,1024]{1,0:T(8,128)(2,1)} %get-tuple-element.100) | copy-start | bytes 393220
  203.5 5.4 %copy-start.35 = (bf16[64,1024]{1,0:T(8,128)(2,1)S(1)}, bf16[64,1024]{1,0:T(8,128)(2,1)}, u32[]{:S(2)}) copy-start(bf16[64,1024]{1,0:T(8,128)(2,1)} %get-tuple-element.99) | copy-start | bytes 393220
  203.5 22.3 %all-to-all-start.3 = ((bf16[16,144,256]{2,1,0:T(8,128)(2,1)}), bf16[16,144,256]{2,1,0:T(8,128)(2,1)S(1)}, u32[]{:S(2)}, u32[]{:S(2)}) async-start(bf16[16,144,256]{2,1,0:T(8,128)(2,1)} %shard_map.214), calls=%async_computation.3 | async-start | bytes 2359296 | tf_op jit(solution)/shard_map/all_to_all | solution.py:563
  207.5 1.4 collective-permute-start.13
  209.0 22.9 %collective-permute-start.14 = (bf16[32,1024]{1,0:T(8,128)(2,1)S(1)}, bf16[32,1024]{1,0:T(8,128)(2,1)S(1)}, u32[]{:S(2)}, u32[]{:S(2)}) collective-permute-start(bf16[32,1024]{1,0:T(8,128)(2,1)S(1)} %dynamic-slice_convert_fusion), channel_id=1, source_target_pairs={{0,2},{1,3},{2,0},{3,1},{4,6},{5,7},{6,4},{7,5},{8,10},{9,11},{10,... | collective-permute-start | bytes 196616 | tf_op jit(solution)/shard_map/ppermute | solution.py:423
  227.5 4.4 %copy-start.34 = (f32[32,1024]{1,0:T(8,128)S(1)}, f32[32,1024]{1,0:T(8,128)}, u32[]{:S(2)}) copy-start(f32[32,1024]{1,0:T(8,128)} %get-tuple-element.84) | copy-start | bytes 393220
  227.5 19.9 %all-to-all-start.4 = ((bf16[16,128,256]{2,1,0:T(8,128)(2,1)}), bf16[16,128,256]{2,1,0:T(8,128)(2,1)S(1)}, u32[]{:S(2)}, u32[]{:S(2)}) async-start(bf16[16,128,256]{2,1,0:T(8,128)(2,1)} %get-tuple-element.106), calls=%async_computation.4 | async-start | bytes 2097152 | tf_op jit(solution)/shard_map/all_to_all | solution.py:567
  249.4 1.6 copy-start.8
  (3 other events, 1.9 us)
Sparse Core Ops, SparseCore 0:
  27.1 54.0 all-gather.7
  165.8 50.0 all-gather.9

commit v3 on v2

--- a/solution.py
+++ b/solution.py
@@ -118,7 +118,9 @@
 
     keys, values = k_ref[...].reshape(LEN, COLS), v_ref[...].reshape(LEN, COLS)
     q_heads = by_head(q_ref[block].reshape(BLK, COLS) * BF(HD ** -0.5))
-    allowed = id_q[...] == id_k[...]
+    allowed = id_k[place[1]] == jnp.concatenate(
+        [id_q[index][:, 0:BLK] for index in range(RING)], axis=1
+    )
     lane = lax.broadcasted_iota(jnp.int32, (BLK, COLS), 1) // HD
     out = jnp.zeros((BLK, COLS), F32)
     for head in range(HEADS):
@@ -211,7 +213,7 @@
     split_halves(place, part_ref, mine_ref, theirs_ref)
 
 
-def unit_grads_kernel(place, hb, da, ub, dz, pair_fwd, pair_dz, pair_da, out_ref):
+def unit_grads_kernel(place, hb, da, ub, dz, pair_fwd, pair_dz, pair_da, out_ref, bias_ref):
     shard = place[0]
     rows = jnp.concatenate([hb[:, half_at(shard, True)], pair_fwd[:, 0:512]], axis=0)
     units = jnp.concatenate([da[...], pair_da[...]], axis=0)
@@ -226,13 +228,11 @@
         term = mm(after, grads[:, cols], TN).astype(BF)
         out_ref[:, 128 + side * 64 : 192 + side * 64, :] = term.reshape(RING, 64, COLS)
     total = jnp.sum(units.astype(F32), axis=0, keepdims=True)
-    small = jnp.concatenate(
+    bias_ref[...] = jnp.concatenate(
         [total[:, part * COLS : (part + 1) * COLS] for part in range(4)]
-        + [jnp.zeros((12, COLS), F32)],
+        + [jnp.zeros((4, COLS), F32)],
         axis=0,
-    ).astype(BF)
-    for index in range(RING):
-        out_ref[index, 256:272, :] = small
+    )
 
 
 def first_back_kernel(
@@ -299,7 +299,7 @@
     def _(step):
         blocks = pl.ds(step * 2, 2)
         keys, values = k[blocks].reshape(256, COLS), v[blocks].reshape(256, COLS)
-        allowed = id_k[blocks].reshape(256, 1) == id_q[...]
+        allowed = id_k[blocks].reshape(256, 1) == id_q[place[1]]
         probs = jnp.where(allowed, jnp.exp(mm(keys, q_heads, NT) - lse[...]), 0.0)
         d_scores = (probs * (mm(values, d_heads, NT) - delta[...])).astype(BF)
         acc_ref[...] += mm(d_scores, keys, TN)
@@ -358,7 +358,7 @@
 
 
 def in_grads_kernel(
-    place, tokens, d, d_pair, pair_in, ob, low, low_pair, sums, out_ref
+    place, tokens, d, d_pair, pair_in, ob, low, low_pair, sums, unit_sums, out_ref
 ):
     shard = place[0]
     rows = jnp.concatenate([tokens[:, half_at(shard, True)], pair_in[:, 256:768]], axis=0)
@@ -377,7 +377,7 @@
             sums[0:6, :],
             jnp.sum(wide[:, 0:COLS], axis=0, keepdims=True),
             jnp.sum(wide[:, 2 * COLS : 3 * COLS], axis=0, keepdims=True),
-            jnp.zeros((8, COLS), F32),
+            unit_sums[...],
         ],
         axis=0,
     ).astype(BF)
@@ -385,9 +385,8 @@
         out_ref[index, 128:144, :] = small
 
 
-def unit_total_kernel(place, recv, low_ref, bias_ref):
+def unit_total_kernel(place, recv, low_ref):
     low_ref[...] = ring_sum(recv, slice(0, 256)).astype(BF)
-    bias_ref[...] = ring_sum(recv, slice(256, 272))
 
 
 def total_kernel(place, recv, small_ref, out_ref):
@@ -449,18 +448,17 @@
         jnp.concatenate([up_rows[:, :HALF], up_rows[:, HALF:], down_rows], axis=0), "shard", 1
     )
     other = lax.all_gather(unit_rows, "context", axis=0)
-    in_oth = swap(w_in, "shard", 1)
+    w_in_late, _ = together((w_in, unit_rows))
+    in_oth = swap(w_in_late, "shard", 1)
     out_oth = swap(w_out, "shard", 1)
 
     spread = jnp.broadcast_to(
-        lax.dynamic_slice_in_dim(tokens, core * 64, 64, 0)[None], (RING, 64, D)
-    )
-    spread, _ = together((spread, unit_rows))
+        jnp.where(core == 0, tokens[0:64], tokens[64:128])[None], (RING, 64, D)
+    )
     x_mine = lax.all_to_all(spread, "context", 0, 0, tiled=True)
     x_mine, in_oth, out_oth = together((x_mine, in_oth, out_oth))
     x_sib = swap(x_mine, "tensor", 1)
 
-    id_q = lax.dynamic_slice_in_dim(segment_ids, block * BLK, BLK, 0)
     id_column = segment_ids.reshape(RING, BLK, 1)
     id_heads = jnp.tile(segment_ids.reshape(RING, 1, BLK), (1, 1, HEADS))
     all_heads = ((RING, 2, 64, COLS), BF)
@@ -469,7 +467,7 @@
     q, k, v, o, ob, lse, mine, theirs = call(
         attend_kernel, 10,
         [all_heads] * 3 + [((BLK, COLS), F32), ((BLK, COLS), BF), ((1, HEADS * BLK), F32)] + halves,
-        place, x_mine, x_sib, w_in, in_oth, b_qv[0], id_q[:, None], segment_ids[None, :],
+        place, x_mine, x_sib, w_in, in_oth, b_qv[0], id_heads, id_column,
         w_out, out_oth,
         scratch=[whole], vmem=60,
     )
@@ -506,14 +504,8 @@
         scratch=[whole],
     )
     pair_da = swap(da, "shard", 1)
+    mine, pair_fwd = together((mine, pair_fwd))
     chip, recv = tensor_sum(mine, theirs)
-    pair_da, chip = together((pair_da, chip))
-    (unit_grads,) = call(
-        unit_grads_kernel, 3, [((RING, 272, COLS), BF)],
-        place, hb, da, ub, dz, pair_fwd, pair_dz, pair_da,
-    )
-    recv, unit_grads = together((recv, unit_grads))
-    unit_recv = lax.all_to_all(unit_grads, "context", 0, 0, tiled=True)
     d_first, low_first, sums = call(
         first_back_kernel, 1.5,
         [((32, D), F32), ((64, D), BF), ((8, D), F32)],
@@ -530,22 +522,23 @@
         place, low_pairs, o, lse, w_out, out_oth,
         scratch=[pltpu.VMEM((BLK, D), BF)],
     )
-    packed, unit_recv = together((packed, unit_recv))
     packs = lax.all_to_all(packed, "context", 0, 0, tiled=True)
-    unit_total, unit_small = call(
-        unit_total_kernel, 1, [((COLS, COLS), BF), ((16, COLS), F32)], place, unit_recv
-    )
-    unit_all = lax.all_gather(unit_total, "context", axis=0)
-    packs, unit_total = together((packs, unit_total))
+    (dq,) = call(
+        query_grad_kernel, 5, [((BLK, COLS), BF)],
+        place, q, k, v, d_out, lse, delta, id_heads, id_column,
+        scratch=[pltpu.VMEM((HEADS * BLK, COLS), F32)], vmem=60,
+    )
+    hb, dq = together((hb, dq))
+    unit_grads, unit_small = call(
+        unit_grads_kernel, 3, [((RING, 256, COLS), BF), ((8, COLS), F32)],
+        place, hb, da, ub, dz, pair_fwd, pair_dz, pair_da,
+    )
+    packs, unit_grads, dq = together((packs, unit_grads, dq))
+    unit_recv = lax.all_to_all(unit_grads, "context", 0, 0, tiled=True)
     low_pair = swap(low_oth, "shard", 1)
     sums = sums + swap(sums, "tensor", 1)
     sums = lax.dynamic_slice_in_dim(sums, tensor * COLS, COLS, 1)
     sums = sums + swap(sums, "shard", 1)
-    (dq,) = call(
-        query_grad_kernel, 5, [((BLK, COLS), BF)],
-        place, q, k, v, d_out, lse, delta, jnp.tile(id_q[None, :], (1, HEADS)), id_column,
-        scratch=[pltpu.VMEM((HEADS * BLK, COLS), F32)], vmem=60,
-    )
     d_mixed, mine, theirs = call(
         key_grad_kernel, 6, [((BLK, 3 * COLS), BF)] + halves,
         place, q, k, v, dq, packs, id_heads, id_column, w_in, in_oth,
@@ -558,9 +551,13 @@
     grad_tokens = d_first + (chip_near + swap(chip_far, "tensor", 2).astype(F32))
     (in_grads,) = call(
         in_grads_kernel, 2.5, [((RING, 144, COLS), BF)],
-        place, tokens, d_mixed, d_pair, pair_in, ob, low_own, low_pair, sums,
-    )
+        place, tokens, d_mixed, d_pair, pair_in, ob, low_own, low_pair, sums, unit_small,
+    )
+    in_grads, unit_recv = together((in_grads, unit_recv))
     recv = lax.all_to_all(in_grads, "context", 0, 0, tiled=True)
+    (unit_total,) = call(unit_total_kernel, 1, [((COLS, COLS), BF)], place, unit_recv)
+    unit_all = lax.all_gather(unit_total, "context", axis=0)
+    recv, _ = together((recv, unit_total))
     small, totals = call(
         total_kernel, 2, [((16, COLS), F32), ((RING, 128, COLS), BF)], place, recv
     )
@@ -569,7 +566,8 @@
         unpack_kernel, 2, [((3, HALF, COLS), F32), ((COLS, HALF), F32)], place, recv
     )
     grad_w_up, grad_w_down = call(
-        unpack_units_kernel, 2, [((HALF, UNITS), F32), ((UNITS, HALF), F32)], place, unit_all
+        unpack_units_kernel, 2, [((HALF, UNITS), F32), ((UNITS, HALF), F32)],
+        place, unit_all, vmem=60,
     )
     return (
         hidden_out,
@@ -579,7 +577,7 @@
         grad_w_up[None],
         grad_w_down[None],
         small[6:8][None],
-        unit_small[0:4].reshape(1, UNITS),
+        small[8:12].reshape(1, UNITS),
         jnp.stack([small[3], small[0]])[None],
         jnp.stack([small[4], small[1]])[None],
         jnp.stack([small[5], small[2]])[None],

time: 262 us -> 244 us (0.931)
  waiting for transfers between devices: 121 us -> 103 us
  local copies, waits for them, and re-layouts: 19.3 us -> 12.6 us
  starting transfers between devices: 44.7 us -> 48.1 us
  Pallas kernels: 51.2 us -> 53.9 us
    all_to_all x1, waiting for transfers between devices: 26.2 us -> 6.24 us  [shards(): unit_recv = lax.all_to_all(unit_grads, 'context', 0, 0, tiled=True)]
    all_to_all x1, waiting for transfers between devices: 13.7 us -> 18.3 us  [shards(): recv = lax.all_to_all(totals, 'context', 0, 0, tiled=True)]
    ppermute x20, starting transfers between devices: 20.3 us -> 24.5 us  [swap(): lax.ppermute(value, axis, [(index, index ^ bit) for index in range(size)])]
    all_gather x1, waiting for transfers between devices: 0.01 us -> 2.88 us  [shards(): unit_all = lax.all_gather(unit_total, 'context', axis=0)]
    pallas_call x15, Pallas kernels: 51.2 us -> 53.9 us  [call(): pl.pallas_call(kernel, out_shape=[jax.ShapeDtypeStruct(shape, dtype) for...]
    unnamed x82 -> x84, local copies, waits for them, and re-layouts: 10.9 us -> 8.96 us
  transfers between devices with their start and end apart: 27 -> 27, of which waited for: 17 -> 18; matrix products, arithmetic and copies ran while one was open for 4% -> 3% of each run, Pallas kernels for 18% -> 18%
where the time goes in v3:
time: 244 us; the launch traced here: 243 us
  waiting for transfers between devices  103 us (42%)
  Pallas kernels  53.9 us (22%)
  starting transfers between devices  48.1 us (20%)
  between operations  14.5 us (6%)
  local copies, waits for them, and re-layouts  12.6 us (5%)
  blocking collectives  6.15 us (3%)
  other arithmetic  4.6 us (2%)
    pallas_call x15, Pallas kernels, call(): pl.pallas_call(kernel, out_shape=[jax.ShapeDtypeStruct(shape, dtype) for...  53.9 us
    ppermute x20, waiting for transfers between devices, swap(): lax.ppermute(value, axis, [(index, index ^ bit) for index in range(size)])  51.1 us
    ppermute x20, starting transfers between devices, swap(): lax.ppermute(value, axis, [(index, index ^ bit) for index in range(size)])  24.5 us
    all_to_all x1, waiting for transfers between devices, shards(): recv = lax.all_to_all(totals, 'context', 0, 0, tiled=True)  18.3 us
    all_to_all x1, waiting for transfers between devices, shards(): recv = lax.all_to_all(in_grads, 'context', 0, 0, tiled=True)  15.2 us
    unnamed x84, local copies, waits for them, and re-layouts  8.96 us
    all_to_all x1, starting transfers between devices, shards(): x_mine = lax.all_to_all(spread, 'context', 0, 0, tiled=True)  8.33 us
    all_to_all x1, waiting for transfers between devices, shards(): unit_recv = lax.all_to_all(unit_grads, 'context', 0, 0, tiled=True)  6.24 us
  transfers between devices with their start and end apart: 27, of which 18 were waited for; matrix products, arithmetic and copies ran while one was open for 3% of the time, Pallas kernels for 18%

profile of v3, /device:TPU:0, one launch (start us, length us, event | category | flops | bytes accessed | tf_op | source)
XLA Modules:
  0.0 243.2 jit_solution(1964990436683854905)
XLA Ops:
  7.2 1.0 slice_select_fusion
  8.2 1.6 broadcast_in_dim.30
  9.8 8.3 %all-to-all-start = ((bf16[16,64,1024]{2,1,0:T(8,128)(2,1)}), bf16[16,64,1024]{2,1,0:T(8,128)(2,1)}, u32[]{:S(2)}, u32[]{:S(2)}) async-start(bf16[16,64,1024]{2,1,0:T(8,128)(2,1)} %broadcast_in_dim.30), calls=%async_computation | async-start | bytes 4194304 | tf_op jit(solution)/shard_map/all_to_all | solution.py:458
  18.3 1.6 collective-permute-start
  19.8 3.5 %collective-permute-done = bf16[128,512]{1,0:T(8,128)(2,1)S(1)} collective-permute-done((bf16[128,512]{1,0:T(8,128)(2,1)S(1)}, bf16[128,512]{1,0:T(8,128)(2,1)S(1)}, u32[]{:S(2)}, u32[]{:S(2)}) %collective-permute-start) | collective-permute-done | bytes 131104 | tf_op jit(solution)/shard_map/ppermute | solution.py:422
  23.3 1.5 collective-permute-start.1
  25.4 21.6 %collective-permute-done.2.wo_oth = bf16[256,512]{1,0:T(8,128)(2,1)S(1)} collective-permute-done((bf16[256,512]{1,0:T(8,128)(2,1)S(1)}, bf16[256,512]{1,0:T(8,128)(2,1)S(1)}, u32[]{:S(2)}, u32[]{:S(2)}) %collective-permute-start.2) | collective-permute-done | bytes 262176 | tf_op jit(solution)/shard_map/ppermute | solution.py:422
  47.0 3.5 %all-to-all-done.x_mine = bf16[16,64,1024]{2,1,0:T(8,128)(2,1)} async-done(((bf16[16,64,1024]{2,1,0:T(8,128)(2,1)}), bf16[16,64,1024]{2,1,0:T(8,128)(2,1)}, u32[]{:S(2)}, u32[]{:S(2)}) %all-to-all-start) | async-done | bytes 2097184 | tf_op jit(solution)/shard_map/all_to_all | solution.py:458
  50.5 1.3 copy.23.id_k
  52.5 2.5 %collective-permute-done.3.x_sib = bf16[16,64,1024]{2,1,0:T(8,128)(2,1)} collective-permute-done((bf16[16,64,1024]{2,1,0:T(8,128)(2,1)}, bf16[16,64,1024]{2,1,0:T(8,128)(2,1)}, u32[]{:S(2)}, u32[]{:S(2)}) %collective-permute-start.3) | collective-permute-done | bytes 2097184 | tf_op jit(solution)/shard_map/ppermute | solution.py:422
  55.6 11.2 %shard_map.203 = (bf16[16,2,64,256]{3,2,1,0:T(8,128)(2,1)}, bf16[16,2,64,256]{3,2,1,0:T(8,128)(2,1)}, bf16[16,2,64,256]{3,2,1,0:T(8,128)(2,1)}, f32[128,256]{1,0...) custom-call(s32[4]{0:T(128)} %pad_add_fusion.place, ...), custom_call_target="tpu_custom_call" | custom-call | flops 11000000512 | bytes 30000000 | tf_op jit(solution)/shard_map/pallas_call | solution.py:38
  66.9 1.4 collective-permute-done.4
  68.4 0.9 add_convert_fusion.2.chip
  69.3 3.1 %collective-permute-start.5 = (bf16[64,1024]{1,0:T(8,128)(2,1)S(1)}, bf16[64,1024]{1,0:T(8,128)(2,1)S(1)}, u32[]{:S(2)}, u32[]{:S(2)}) collective-permute-start(bf16[64,1024]{1,0:T(8,128)(2,1)S(1)} %add_convert_fusion.2.chip), channel_id=1, source_target_pairs={{0,2},{1,3},{2,0},{3,1},{4,6},{5,7},{6,4},{7,5},{8,10},{9,11},{10,... | collective-permute-start | bytes 393224 | tf_op jit(solution)/shard_map/ppermute | solution.py:422
  72.4 4.0 %collective-permute-done.5.recv = bf16[64,1024]{1,0:T(8,128)(2,1)S(1)} collective-permute-done((bf16[64,1024]{1,0:T(8,128)(2,1)S(1)}, bf16[64,1024]{1,0:T(8,128)(2,1)S(1)}, u32[]{:S(2)}, u32[]{:S(2)}) %collective-permute-start.5) | collective-permute-done | bytes 131104 | tf_op jit(solution)/shard_map/ppermute | solution.py:422
  76.5 0.8 shard_map.204
  77.3 0.7 copy-done.24
  78.0 2.0 all-gather.hb
  80.0 1.6 copy-done.8
  81.6 1.5 shard_map.205
  83.1 0.8 copy-done.22
  84.0 1.2 collective-permute-done.6
  85.2 3.1 %collective-permute-start.7 = (bf16[64,1024]{1,0:T(8,128)(2,1)S(1)}, bf16[64,1024]{1,0:T(8,128)(2,1)S(1)}, u32[]{:S(2)}, u32[]{:S(2)}) collective-permute-start(bf16[64,1024]{1,0:T(8,128)(2,1)S(1)} %add_convert_fusion.1.chip), channel_id=1, source_target_pairs={{0,2},{1,3},{2,0},{3,1},{4,6},{5,7},{6,4},{7,5},{8,10},{9,11},{10,... | collective-permute-start | bytes 393224 | tf_op jit(solution)/shard_map/ppermute | solution.py:422
  88.4 0.7 collective-permute-start.8
  89.0 4.1 %collective-permute-done.7.recv = bf16[64,1024]{1,0:T(8,128)(2,1)S(1)} collective-permute-done((bf16[64,1024]{1,0:T(8,128)(2,1)S(1)}, bf16[64,1024]{1,0:T(8,128)(2,1)S(1)}, u32[]{:S(2)}, u32[]{:S(2)}) %collective-permute-start.7) | collective-permute-done | bytes 131104 | tf_op jit(solution)/shard_map/ppermute | solution.py:422
  93.2 1.0 copy-done.10
  94.2 0.9 copy-done.25
  95.1 1.6 shard_map.206
  96.8 2.0 all-gather.2.dz
  98.8 2.1 shard_map.207
  101.1 1.2 collective-permute-done.9
  102.3 3.1 %collective-permute-start.10 = (bf16[64,1024]{1,0:T(8,128)(2,1)S(1)}, bf16[64,1024]{1,0:T(8,128)(2,1)S(1)}, u32[]{:S(2)}, u32[]{:S(2)}) collective-permute-start(bf16[64,1024]{1,0:T(8,128)(2,1)S(1)} %add_convert_fusion.chip), channel_id=1, source_target_pairs={{0,2},{1,3},{2,0},{3,1},{4,6},{5,7},{6,4},{7,5},{8,10},{9,11},{10,... | collective-permute-start | bytes 393224 | tf_op jit(solution)/shard_map/ppermute | solution.py:422
  105.4 4.0 %collective-permute-done.10.recv = bf16[64,1024]{1,0:T(8,128)(2,1)S(1)} collective-permute-done((bf16[64,1024]{1,0:T(8,128)(2,1)S(1)}, bf16[64,1024]{1,0:T(8,128)(2,1)S(1)}, u32[]{:S(2)}, u32[]{:S(2)}) %collective-permute-start.10) | collective-permute-done | bytes 131104 | tf_op jit(solution)/shard_map/ppermute | solution.py:422
  110.1 2.3 shard_map.208
  112.4 2.2 all-gather.3
  114.6 2.0 shard_map.209
  117.2 3.9 %all-to-all-start.1 = ((bf16[16,144,256]{2,1,0:T(8,128)(2,1)}), bf16[16,144,256]{2,1,0:T(8,128)(2,1)S(1)}, u32[]{:S(2)}, u32[]{:S(2)}) async-start(bf16[16,144,256]{2,1,0:T(8,128)(2,1)} %get-tuple-element.91), calls=%async_computation.1 | async-start | bytes 2359296 | tf_op jit(solution)/shard_map/all_to_all | solution.py:525
  121.1 1.5 collective-permute-start.12
  122.7 0.8 collective-permute-start.11
  123.5 8.2 %shard_map.210.dq = bf16[128,256]{1,0:T(8,128)(2,1)} custom-call(s32[4]{0:T(128)} %pad_add_fusion.place, bf16[16,2,64,256]{3,2,1,0:T(8,128)(2,1)} %get-tuple-element.85.q, bf16[16,2,64,256]{3,2,1,0:T(8,128)(2,1)} %get-tuple-element.86.k, bf16[16,2,64,256]{3,2,1,0:T(8,128)(2,1)} %get-tuple-element.87.v, bf16[128,256]{1,0:T(8,128)(2,1)} %copy-done.28, ...), custom_call_target="tpu_custom_call" | custom-call | flops 5500000256 | bytes 15000000 | tf_op jit(solution)/shard_map/pallas_call | solution.py:38
  132.2 2.6 %shard_map.211 = (bf16[16,256,256]{2,1,0:T(8,128)(2,1)}, f32[8,256]{1,0:T(8,128)S(1)}) custom-call(s32[4]{0:T(128)S(1)} %copy-done.6, bf16[128,1024]{1,0:T(8,128)(2,1)S(1)} %all-gather.hb, bf16[128,1024]{1,0:T(8,128)(2,1)S(1)} %get-tuple-element.95.da, bf16[128,1024]{1,0:T(8,128)(2,1)S(1)} %get-tuple-element.80.ub, bf16[128,1024]{1,0:T(8,128)(2,1)S(1)} %all-gather.2.dz, ...), custom_call_target="tpu_custom_call" | custom-call | flops 3300000000 | bytes 9000000 | tf_op jit(solution)/shard_map/pallas_call | solution.py:38
  134.8 6.1 %all-to-all-done.1.recv = bf16[16,144,256]{2,1,0:T(8,128)(2,1)S(1)} async-done(((bf16[16,144,256]{2,1,0:T(8,128)(2,1)}), bf16[16,144,256]{2,1,0:T(8,128)(2,1)S(1)}, u32[]{:S(2)}, u32[]{:S(2)}) %all-to-all-start.1) | async-done | bytes 1179680 | tf_op jit(solution)/shard_map/all_to_all | solution.py:525
  140.9 1.0 copy-done.32
  141.9 3.7 %all-to-all-start.2 = ((bf16[16,256,256]{2,1,0:T(8,128)(2,1)}), bf16[16,256,256]{2,1,0:T(8,128)(2,1)S(1)}, u32[]{:S(2)}, u32[]{:S(2)}) async-start(bf16[16,256,256]{2,1,0:T(8,128)(2,1)} %get-tuple-element.109), calls=%async_computation.2 | async-start | bytes 4194304 | tf_op jit(solution)/shard_map/all_to_all | solution.py:537
  145.8 1.6 collective-permute-start.16
  147.4 10.8 %shard_map.212 = (bf16[128,768]{1,0:T(8,128)(2,1)}, bf16[64,1024]{1,0:T(8,128)(2,1)}, bf16[64,1024]{1,0:T(8,128)(2,1)}) custom-call(s32[4]{0:T(128)} %pad_add_fusion.place, bf16[16,2,64,256]{3,2,1,0:T(8,128)(2,1)} %get-tuple-element.85.q, bf16[16,2,64,256]{3,2,1,0:T(8,128)(2,1)} %get-tuple-element.86.k, bf16[16,2,64,256]{3,2,1,0:T(8,128)(2,1)} %get-tuple-element.87.v, ...), custom_call_target="tpu_custom_call" | custom-call | flops 6600000000 | bytes 18000000 | tf_op jit(solution)/shard_map/pallas_call | solution.py:38
  158.7 1.5 collective-permute-start.17
  160.2 1.2 collective-permute-start.19
  161.4 5.7 %collective-permute-done.19 = f32[8,256]{1,0:T(8,128)S(1)} collective-permute-done((f32[8,256]{1,0:T(8,128)S(1)}, f32[8,256]{1,0:T(8,128)S(1)}, u32[]{:S(2)}, u32[]{:S(2)}) %collective-permute-start.19) | collective-permute-done | bytes 8224 | tf_op jit(solution)/shard_map/ppermute | solution.py:422
  167.1 0.9 copy-done.17
  168.0 2.0 shard_map.213
  170.1 6.2 %all-to-all-done.2.recv = bf16[16,256,256]{2,1,0:T(8,128)(2,1)S(1)} async-done(((bf16[16,256,256]{2,1,0:T(8,128)(2,1)}), bf16[16,256,256]{2,1,0:T(8,128)(2,1)S(1)}, u32[]{:S(2)}, u32[]{:S(2)}) %all-to-all-start.2) | async-done | bytes 2097184 | tf_op jit(solution)/shard_map/all_to_all | solution.py:537
  176.3 1.5 shard_map.214
  177.8 3.8 %all-to-all-start.3 = ((bf16[16,144,256]{2,1,0:T(8,128)(2,1)}), bf16[16,144,256]{2,1,0:T(8,128)(2,1)S(1)}, u32[]{:S(2)}, u32[]{:S(2)}) async-start(bf16[16,144,256]{2,1,0:T(8,128)(2,1)} %shard_map.213), calls=%async_computation.3 | async-start | bytes 2359296 | tf_op jit(solution)/shard_map/all_to_all | solution.py:557
  181.8 1.3 collective-permute-done.13
  183.2 3.1 %collective-permute-start.14 = (bf16[32,1024]{1,0:T(8,128)(2,1)S(1)}, bf16[32,1024]{1,0:T(8,128)(2,1)S(1)}, u32[]{:S(2)}, u32[]{:S(2)}) collective-permute-start(bf16[32,1024]{1,0:T(8,128)(2,1)S(1)} %dynamic-slice_convert_fusion), channel_id=1, source_target_pairs={{0,2},{1,3},{2,0},{3,1},{4,6},{5,7},{6,4},{7,5},{8,10},{9,11},{10,... | collective-permute-start | bytes 196616 | tf_op jit(solution)/shard_map/ppermute | solution.py:422
  186.3 15.2 %all-to-all-done.3.recv = bf16[16,144,256]{2,1,0:T(8,128)(2,1)S(1)} async-done(((bf16[16,144,256]{2,1,0:T(8,128)(2,1)}), bf16[16,144,256]{2,1,0:T(8,128)(2,1)S(1)}, u32[]{:S(2)}, u32[]{:S(2)}) %all-to-all-start.3) | async-done | bytes 1179680 | tf_op jit(solution)/shard_map/all_to_all | solution.py:557
  201.4 1.7 shard_map.215
  203.1 3.8 %all-to-all-start.4 = ((bf16[16,128,256]{2,1,0:T(8,128)(2,1)}), bf16[16,128,256]{2,1,0:T(8,128)(2,1)S(1)}, u32[]{:S(2)}, u32[]{:S(2)}) async-start(bf16[16,128,256]{2,1,0:T(8,128)(2,1)} %get-tuple-element.113), calls=%async_computation.4 | async-start | bytes 2097152 | tf_op jit(solution)/shard_map/all_to_all | solution.py:564
  206.9 0.7 add_add_fusion
  209.4 18.3 %all-to-all-done.4.recv = bf16[16,128,256]{2,1,0:T(8,128)(2,1)S(1)} async-done(((bf16[16,128,256]{2,1,0:T(8,128)(2,1)}), bf16[16,128,256]{2,1,0:T(8,128)(2,1)S(1)}, u32[]{:S(2)}, u32[]{:S(2)}) %all-to-all-start.4) | async-done | bytes 1048608 | tf_op jit(solution)/shard_map/all_to_all | solution.py:564
  227.8 2.0 shard_map.216
  229.7 2.9 %all-gather.10.cloned.1.call-done = bf16[4096,256]{1,0:T(8,128)(2,1)} async-done(((bf16[256,256]{1,0:T(8,128)(2,1)}), bf16[4096,256]{1,0:T(8,128)(2,1)}) %all-gather.10.cloned.1.call-update) | async-done | bytes 2097168 | tf_op jit(solution)/shard_map/all_gather | solution.py:559
  232.6 3.8 %shard_map.217 = (f32[512,1024]{1,0:T(8,128)}, f32[1024,512]{1,0:T(8,128)}) custom-call(s32[4]{0:T(128)} %pad_add_fusion.place, bf16[16,256,256]{2,1,0:T(8,128)(2,1)} %bitcast.66), custom_call_target="tpu_custom_call" | custom-call | flops 2200000000 | bytes 6000000 | tf_op jit(solution)/shard_map/pallas_call | solution.py:38
  (119 shorter events, 7.0 us)
Async XLA Ops:
  9.8 8.4 %copy-start.2 = (bf16[1,512,1024]{2,1,0:T(8,128)(2,1)S(1)}, bf16[1,512,1024]{2,1,0:T(8,128)(2,1)}, u32[]{:S(2)}) copy-start(bf16[1,512,1024]{2,1,0:T(8,128)(2,1)} %param.17) | copy-start | bytes 3145732
  9.8 8.4 %copy-start.3 = (bf16[1,1024,512]{2,1,0:T(8,128)(2,1)S(1)}, bf16[1,1024,512]{2,1,0:T(8,128)(2,1)}, u32[]{:S(2)}) copy-start(bf16[1,1024,512]{2,1,0:T(8,128)(2,1)} %param.19) | copy-start | bytes 3145732
  9.8 15.0 %copy-start.13 = (bf16[1,256,512]{2,1,0:T(8,128)(2,1)S(1)}, bf16[1,256,512]{2,1,0:T(8,128)(2,1)}, u32[]{:S(2)}) copy-start(bf16[1,256,512]{2,1,0:T(8,128)(2,1)} %param.16) | copy-start | bytes 786436
  9.8 40.7 %copy-start.37 = (s32[2048]{0:T(1024)S(1)}, s32[2048]{0:T(1024)}, u32[]{:S(2)}) copy-start(s32[2048]{0:T(1024)} %param.13) | copy-start | bytes 24580
  9.8 40.7 %all-to-all-start = ((bf16[16,64,1024]{2,1,0:T(8,128)(2,1)}), bf16[16,64,1024]{2,1,0:T(8,128)(2,1)}, u32[]{:S(2)}, u32[]{:S(2)}) async-start(bf16[16,64,1024]{2,1,0:T(8,128)(2,1)} %broadcast_in_dim.30), calls=%async_computation | async-start | bytes 4194304 | tf_op jit(solution)/shard_map/all_to_all | solution.py:458
  18.1 61.9 %all-gather.8.cloned.1.call-start = ((), (), s32[]{:S(2)}) async-start(), calls=%async_computation.5 | async-start | bytes 2228224 | tf_op jit(solution)/shard_map/all_gather | solution.py:450
  18.3 5.0 %collective-permute-start = (bf16[128,512]{1,0:T(8,128)(2,1)S(1)}, bf16[128,512]{1,0:T(8,128)(2,1)S(1)}, u32[]{:S(2)}, u32[]{:S(2)}) collective-permute-start(bf16[128,512]{1,0:T(8,128)(2,1)S(1)} %pad_maximum_fusion.2), channel_id=1, source_target_pairs={{0,64},{64,0},{1,65},{65,1},{2,66},{66,2},{3,67},{67,3},{4,68},{68... | collective-permute-start | bytes 393224 | tf_op jit(solution)/shard_map/ppermute | solution.py:422
  23.3 2.0 copy-start.34
  23.3 23.7 %collective-permute-start.1 = (bf16[3,512,256]{2,1,0:T(8,128)(2,1)}, bf16[3,512,256]{2,1,0:T(8,128)(2,1)}, u32[]{:S(2)}, u32[]{:S(2)}) collective-permute-start(bf16[3,512,256]{2,1,0:T(8,128)(2,1)} %bitcast.5.w_own), channel_id=1, source_target_pairs={{0,64},{64,0},{1,65},{65,1},{2,66},{66,2},{3,67},{67,3},{4,68},{68... | collective-permute-start | bytes 2359304 | tf_op jit(solution)/shard_map/ppermute | solution.py:422
  24.8 22.2 %collective-permute-start.2 = (bf16[256,512]{1,0:T(8,128)(2,1)S(1)}, bf16[256,512]{1,0:T(8,128)(2,1)S(1)}, u32[]{:S(2)}, u32[]{:S(2)}) collective-permute-start(bf16[256,512]{1,0:T(8,128)(2,1)S(1)} %bitcast.50), channel_id=1, source_target_pairs={{0,64},{64,0},{1,65},{65,1},{2,66},{66,2},{3,67},{67,3},{4,68},{68... | collective-permute-start | bytes 786440 | tf_op jit(solution)/shard_map/ppermute | solution.py:422
  47.0 8.6 %copy-start.15 = (bf16[256,512]{1,0:T(8,128)(2,1)}, bf16[256,512]{1,0:T(8,128)(2,1)S(1)}, u32[]{:S(2)}) copy-start(bf16[256,512]{1,0:T(8,128)(2,1)S(1)} %collective-permute-done.2.wo_oth) | copy-start | bytes 786436
  50.5 4.5 %collective-permute-start.3 = (bf16[16,64,1024]{2,1,0:T(8,128)(2,1)}, bf16[16,64,1024]{2,1,0:T(8,128)(2,1)}, u32[]{:S(2)}, u32[]{:S(2)}) collective-permute-start(bf16[16,64,1024]{2,1,0:T(8,128)(2,1)} %all-to-all-done.x_mine), channel_id=1, source_target_pairs={{0,1},{1,0},{2,3},{3,2},{4,5},{5,4},{6,7},{7,6},{8,9},{9,8},{10,11... | collective-permute-start | bytes 6291464 | tf_op jit(solution)/shard_map/ppermute | solution.py:422
  55.6 20.8 %copy-start = (bf16[128,1024]{1,0:T(8,128)(2,1)S(1)}, bf16[128,1024]{1,0:T(8,128)(2,1)}, u32[]{:S(2)}) copy-start(bf16[128,1024]{1,0:T(8,128)(2,1)} %tokens.3) | copy-start | bytes 786436
  55.6 20.8 %copy-start.4 = (s32[4]{0:T(128)S(1)}, s32[4]{0:T(128)}, u32[]{:S(2)}) copy-start(s32[4]{0:T(128)} %pad_add_fusion.place) | copy-start | bytes 52
  55.6 20.8 %copy-start.19 = (bf16[1,2,1024]{2,1,0:T(2,128)(2,1)S(1)}, bf16[1,2,1024]{2,1,0:T(2,128)(2,1)}, u32[]{:S(2)}) copy-start(bf16[1,2,1024]{2,1,0:T(2,128)(2,1)} %param.20) | copy-start | bytes 12292
  55.6 20.8 %copy-start.20 = (bf16[1,2,1024]{2,1,0:T(2,128)(2,1)S(1)}, bf16[1,2,1024]{2,1,0:T(2,128)(2,1)}, u32[]{:S(2)}) copy-start(bf16[1,2,1024]{2,1,0:T(2,128)(2,1)} %param.21) | copy-start | bytes 12292
  55.6 20.8 %copy-start.21 = (bf16[1,2,1024]{2,1,0:T(2,128)(2,1)S(1)}, bf16[1,2,1024]{2,1,0:T(2,128)(2,1)}, u32[]{:S(2)}) copy-start(bf16[1,2,1024]{2,1,0:T(2,128)(2,1)} %param.22) | copy-start | bytes 12292
  66.8 1.6 collective-permute-start.4
  69.3 7.1 %collective-permute-start.5 = (bf16[64,1024]{1,0:T(8,128)(2,1)S(1)}, bf16[64,1024]{1,0:T(8,128)(2,1)S(1)}, u32[]{:S(2)}, u32[]{:S(2)}) collective-permute-start(bf16[64,1024]{1,0:T(8,128)(2,1)S(1)} %add_convert_fusion.2.chip), channel_id=1, source_target_pairs={{0,2},{1,3},{2,0},{3,1},{4,6},{5,7},{6,4},{7,5},{8,10},{9,11},{10,... | collective-permute-start | bytes 393224 | tf_op jit(solution)/shard_map/ppermute | solution.py:422
  76.5 3.5 %copy-start.18 = (bf16[1,1024]{1,0:T(2,128)(2,1)S(1)}, bf16[1,1024]{1,0:T(2,128)(2,1)}, u32[]{:S(2)}) copy-start(bf16[1,1024]{1,0:T(2,128)(2,1)} %b_up.1) | copy-start | bytes 6148
  80.0 1.6 copy-start.8
  83.8 1.3 collective-permute-start.6
  85.2 7.9 %collective-permute-start.7 = (bf16[64,1024]{1,0:T(8,128)(2,1)S(1)}, bf16[64,1024]{1,0:T(8,128)(2,1)S(1)}, u32[]{:S(2)}, u32[]{:S(2)}) collective-permute-start(bf16[64,1024]{1,0:T(8,128)(2,1)S(1)} %add_convert_fusion.1.chip), channel_id=1, source_target_pairs={{0,2},{1,3},{2,0},{3,1},{4,6},{5,7},{6,4},{7,5},{8,10},{9,11},{10,... | collective-permute-start | bytes 393224 | tf_op jit(solution)/shard_map/ppermute | solution.py:422
  88.4 12.7 %collective-permute-start.8 = (bf16[128,1536]{1,0:T(8,128)(2,1)S(1)}, bf16[128,1536]{1,0:T(8,128)(2,1)S(1)}, u32[]{:S(2)}, u32[]{:S(2)}) collective-permute-start(bf16[128,1536]{1,0:T(8,128)(2,1)S(1)} %pad_maximum_fusion), channel_id=1, source_target_pairs={{0,64},{64,0},{1,65},{65,1},{2,66},{66,2},{3,67},{67,3},{4,68},{68... | collective-permute-start | bytes 1179656 | tf_op jit(solution)/shard_map/ppermute | solution.py:422
  93.2 1.0 copy-start.10
  94.2 0.9 copy-start.25
  95.1 3.6 %copy-start.9 = (bf16[2048,512]{1,0:T(8,128)(2,1)S(1)}, bf16[2048,512]{1,0:T(8,128)(2,1)}, u32[]{:S(2)}) copy-start(bf16[2048,512]{1,0:T(8,128)(2,1)} %all-gather.8.cloned.1.call-done) | copy-start | bytes 6291460
  95.1 3.6 %copy-start.23 = (f32[128,1024]{1,0:T(8,128)S(1)}, f32[128,1024]{1,0:T(8,128)}, u32[]{:S(2)}) copy-start(f32[128,1024]{1,0:T(8,128)} %copy-done.22) | copy-start | bytes 1572868
  96.8 4.1 %copy-start.26 = (f32[64,1024]{1,0:T(8,128)}, f32[64,1024]{1,0:T(8,128)S(1)}, u32[]{:S(2)}) copy-start(f32[64,1024]{1,0:T(8,128)S(1)} %get-tuple-element.76.dx) | copy-start | bytes 786436
  96.8 4.1 %copy-start.29 = (f32[8,1024]{1,0:T(8,128)}, f32[8,1024]{1,0:T(8,128)S(1)}, u32[]{:S(2)}) copy-start(f32[8,1024]{1,0:T(8,128)S(1)} %get-tuple-element.83.sums_in) | copy-start | bytes 98308
  100.8 1.4 collective-permute-start.9
  101.1 8.4 %copy-start.11 = (bf16[128,1536]{1,0:T(8,128)(2,1)}, bf16[128,1536]{1,0:T(8,128)(2,1)S(1)}, u32[]{:S(2)}) copy-start(bf16[128,1536]{1,0:T(8,128)(2,1)S(1)} %collective-permute-done.8.pair_fwd) | copy-start | bytes 1179652
  102.3 7.2 %copy-start.33 = (bf16[64,1024]{1,0:T(8,128)(2,1)}, bf16[64,1024]{1,0:T(8,128)(2,1)S(1)}, u32[]{:S(2)}) copy-start(bf16[64,1024]{1,0:T(8,128)(2,1)S(1)} %add_convert_fusion.chip) | copy-start | bytes 393220
  102.3 7.1 %collective-permute-start.10 = (bf16[64,1024]{1,0:T(8,128)(2,1)S(1)}, bf16[64,1024]{1,0:T(8,128)(2,1)S(1)}, u32[]{:S(2)}, u32[]{:S(2)}) collective-permute-start(bf16[64,1024]{1,0:T(8,128)(2,1)S(1)} %add_convert_fusion.chip), channel_id=1, source_target_pairs={{0,2},{1,3},{2,0},{3,1},{4,6},{5,7},{6,4},{7,5},{8,10},{9,11},{10,... | collective-permute-start | bytes 393224 | tf_op jit(solution)/shard_map/ppermute | solution.py:422
  110.1 4.5 %copy-start.5 = (s32[4]{0:T(128)S(1)}, s32[4]{0:T(128)}, u32[]{:S(2)}) copy-start(s32[4]{0:T(128)} %pad_add_fusion.place) | copy-start | bytes 52
  110.1 4.5 %copy-start.14 = (bf16[1,256,512]{2,1,0:T(8,128)(2,1)S(1)}, bf16[1,256,512]{2,1,0:T(8,128)(2,1)}, u32[]{:S(2)}) copy-start(bf16[1,256,512]{2,1,0:T(8,128)(2,1)} %param.16) | copy-start | bytes 786436
  110.1 4.5 %copy-start.16 = (bf16[256,512]{1,0:T(8,128)(2,1)S(1)}, bf16[256,512]{1,0:T(8,128)(2,1)}, u32[]{:S(2)}) copy-start(bf16[256,512]{1,0:T(8,128)(2,1)} %copy-done.15) | copy-start | bytes 786436
  110.1 4.5 %copy-start.27 = (f32[128,256]{1,0:T(8,128)S(1)}, f32[128,256]{1,0:T(8,128)}, u32[]{:S(2)}) copy-start(f32[128,256]{1,0:T(8,128)} %get-tuple-element.89.o) | copy-start | bytes 393220
  110.1 4.5 %copy-start.30 = (f32[1,512]{1,0:T(1,128)S(1)}, f32[1,512]{1,0:T(1,128)}, u32[]{:S(2)}) copy-start(f32[1,512]{1,0:T(1,128)} %get-tuple-element.90.lse) | copy-start | bytes 6148
  117.2 6.3 %copy-start.28 = (bf16[128,256]{1,0:T(8,128)(2,1)}, bf16[128,256]{1,0:T(8,128)(2,1)S(1)}, u32[]{:S(2)}) copy-start(bf16[128,256]{1,0:T(8,128)(2,1)S(1)} %get-tuple-element.92.d_out) | copy-start | bytes 196612
  117.2 23.7 %all-to-all-start.1 = ((bf16[16,144,256]{2,1,0:T(8,128)(2,1)}), bf16[16,144,256]{2,1,0:T(8,128)(2,1)S(1)}, u32[]{:S(2)}, u32[]{:S(2)}) async-start(bf16[16,144,256]{2,1,0:T(8,128)(2,1)} %get-tuple-element.91), calls=%async_computation.1 | async-start | bytes 2359296 | tf_op jit(solution)/shard_map/all_to_all | solution.py:525
  121.1 11.1 %collective-permute-start.12 = (bf16[128,1024]{1,0:T(8,128)(2,1)S(1)}, bf16[128,1024]{1,0:T(8,128)(2,1)S(1)}, u32[]{:S(2)}, u32[]{:S(2)}) collective-permute-start(bf16[128,1024]{1,0:T(8,128)(2,1)S(1)} %get-tuple-element.95.da), channel_id=1, source_target_pairs={{0,64},{64,0},{1,65},{65,1},{2,66},{66,2},{3,67},{67,3},{4,68},{68... | collective-permute-start | bytes 786440 | tf_op jit(solution)/shard_map/ppermute | solution.py:422
  122.7 9.5 %collective-permute-start.11 = (bf16[128,512]{1,0:T(8,128)(2,1)S(1)}, bf16[128,512]{1,0:T(8,128)(2,1)S(1)}, u32[]{:S(2)}, u32[]{:S(2)}) collective-permute-start(bf16[128,512]{1,0:T(8,128)(2,1)S(1)} %constant_dynamic-slice_fusion.1), channel_id=1, source_target_pairs={{0,64},{64,0},{1,65},{65,1},{2,66},{66,2},{3,67},{67,3},{4,68},{68... | collective-permute-start | bytes 393224 | tf_op jit(solution)/shard_map/ppermute | solution.py:422
  123.5 8.7 %copy-start.6 = (s32[4]{0:T(128)S(1)}, s32[4]{0:T(128)}, u32[]{:S(2)}) copy-start(s32[4]{0:T(128)} %pad_add_fusion.place) | copy-start | bytes 52
  123.5 8.7 %copy-start.12 = (bf16[128,1536]{1,0:T(8,128)(2,1)S(1)}, bf16[128,1536]{1,0:T(8,128)(2,1)}, u32[]{:S(2)}) copy-start(bf16[128,1536]{1,0:T(8,128)(2,1)} %copy-done.11) | copy-start | bytes 1179652
  140.9 1.0 copy-start.32
  140.9 4.8 %copy-start.1 = (bf16[128,256]{1,0:T(8,128)(2,1)S(1)}, bf16[128,256]{1,0:T(8,128)(2,1)}, u32[]{:S(2)}) copy-start(bf16[128,256]{1,0:T(8,128)(2,1)} %get-tuple-element.104.ob) | copy-start | bytes 196612
  141.9 34.4 %all-to-all-start.2 = ((bf16[16,256,256]{2,1,0:T(8,128)(2,1)}), bf16[16,256,256]{2,1,0:T(8,128)(2,1)S(1)}, u32[]{:S(2)}, u32[]{:S(2)}) async-start(bf16[16,256,256]{2,1,0:T(8,128)(2,1)} %get-tuple-element.109), calls=%async_computation.2 | async-start | bytes 4194304 | tf_op jit(solution)/shard_map/all_to_all | solution.py:537
  145.7 86.9 %all-gather.10.cloned.1.call-start = ((), (), s32[]{:S(2)}) async-start(), calls=%async_computation.6 | async-start | bytes 2228224 | tf_op jit(solution)/shard_map/all_gather | solution.py:559
  145.8 13.0 %copy-start.38 = (f32[8,1024]{1,0:T(8,128)S(1)}, f32[8,1024]{1,0:T(8,128)}, u32[]{:S(2)}) copy-start(f32[8,1024]{1,0:T(8,128)} %get-tuple-element.107) | copy-start | bytes 98308
  145.8 21.3 %copy-start.7 = (s32[4]{0:T(128)S(1)}, s32[4]{0:T(128)}, u32[]{:S(2)}) copy-start(s32[4]{0:T(128)} %pad_add_fusion.place) | copy-start | bytes 52
  145.8 21.3 %collective-permute-start.16 = (bf16[128,768]{1,0:T(8,128)(2,1)S(1)}, bf16[128,768]{1,0:T(8,128)(2,1)S(1)}, u32[]{:S(2)}, u32[]{:S(2)}) collective-permute-start(bf16[128,768]{1,0:T(8,128)(2,1)S(1)} %pad_maximum_fusion.1), channel_id=1, source_target_pairs={{0,64},{64,0},{1,65},{65,1},{2,66},{66,2},{3,67},{67,3},{4,68},{68... | collective-permute-start | bytes 589832 | tf_op jit(solution)/shard_map/ppermute | solution.py:422
  158.2 8.9 %collective-permute-start.15 = (bf16[128,768]{1,0:T(8,128)(2,1)}, bf16[128,768]{1,0:T(8,128)(2,1)S(1)}, u32[]{:S(2)}, u32[]{:S(2)}) collective-permute-start(bf16[128,768]{1,0:T(8,128)(2,1)} %get-tuple-element.103.d), channel_id=1, source_target_pairs={{0,64},{64,0},{1,65},{65,1},{2,66},{66,2},{3,67},{67,3},{4,68},{68... | collective-permute-start | bytes 589832 | tf_op jit(solution)/shard_map/ppermute | solution.py:422
  158.7 1.5 collective-permute-start.18
  158.7 8.4 %collective-permute-start.17 = (bf16[128,512]{1,0:T(8,128)(2,1)S(1)}, bf16[128,512]{1,0:T(8,128)(2,1)S(1)}, u32[]{:S(2)}, u32[]{:S(2)}) collective-permute-start(bf16[128,512]{1,0:T(8,128)(2,1)S(1)} %get-tuple-element.106), channel_id=1, source_target_pairs={{0,64},{64,0},{1,65},{65,1},{2,66},{66,2},{3,67},{67,3},{4,68},{68... | collective-permute-start | bytes 393224 | tf_op jit(solution)/shard_map/ppermute | solution.py:422
  160.2 6.9 %collective-permute-start.19 = (f32[8,256]{1,0:T(8,128)S(1)}, f32[8,256]{1,0:T(8,128)S(1)}, u32[]{:S(2)}, u32[]{:S(2)}) collective-permute-start(f32[8,256]{1,0:T(8,128)S(1)} %dynamic-slice_add_fusion), channel_id=1, source_target_pairs={{0,64},{64,0},{1,65},{65,1},{2,66},{66,2},{3,67},{67,3},{4,68},{68... | collective-permute-start | bytes 24584 | tf_op jit(solution)/shard_map/ppermute | solution.py:422
  167.1 0.9 copy-start.17
  177.8 3.9 %copy-start.39 = (bf16[64,1024]{1,0:T(8,128)(2,1)S(1)}, bf16[64,1024]{1,0:T(8,128)(2,1)}, u32[]{:S(2)}) copy-start(bf16[64,1024]{1,0:T(8,128)(2,1)} %get-tuple-element.102) | copy-start | bytes 393220
  177.8 5.3 %copy-start.36 = (bf16[64,1024]{1,0:T(8,128)(2,1)S(1)}, bf16[64,1024]{1,0:T(8,128)(2,1)}, u32[]{:S(2)}) copy-start(bf16[64,1024]{1,0:T(8,128)(2,1)} %get-tuple-element.101) | copy-start | bytes 393220
  177.8 23.6 %all-to-all-start.3 = ((bf16[16,144,256]{2,1,0:T(8,128)(2,1)}), bf16[16,144,256]{2,1,0:T(8,128)(2,1)S(1)}, u32[]{:S(2)}, u32[]{:S(2)}) async-start(bf16[16,144,256]{2,1,0:T(8,128)(2,1)} %shard_map.213), calls=%async_computation.3 | async-start | bytes 2359296 | tf_op jit(solution)/shard_map/all_to_all | solution.py:557
  181.7 1.4 collective-permute-start.13
  183.2 23.8 %collective-permute-start.14 = (bf16[32,1024]{1,0:T(8,128)(2,1)S(1)}, bf16[32,1024]{1,0:T(8,128)(2,1)S(1)}, u32[]{:S(2)}, u32[]{:S(2)}) collective-permute-start(bf16[32,1024]{1,0:T(8,128)(2,1)S(1)} %dynamic-slice_convert_fusion), channel_id=1, source_target_pairs={{0,2},{1,3},{2,0},{3,1},{4,6},{5,7},{6,4},{7,5},{8,10},{9,11},{10,... | collective-permute-start | bytes 196616 | tf_op jit(solution)/shard_map/ppermute | solution.py:422
  203.1 3.8 %copy-start.35 = (f32[32,1024]{1,0:T(8,128)S(1)}, f32[32,1024]{1,0:T(8,128)}, u32[]{:S(2)}) copy-start(f32[32,1024]{1,0:T(8,128)} %get-tuple-element.84) | copy-start | bytes 393220
  203.1 24.6 %all-to-all-start.4 = ((bf16[16,128,256]{2,1,0:T(8,128)(2,1)}), bf16[16,128,256]{2,1,0:T(8,128)(2,1)S(1)}, u32[]{:S(2)}, u32[]{:S(2)}) async-start(bf16[16,128,256]{2,1,0:T(8,128)(2,1)} %get-tuple-element.113), calls=%async_computation.4 | async-start | bytes 2097152 | tf_op jit(solution)/shard_map/all_to_all | solution.py:564
  (4 other events, 2.7 us)
Sparse Core Ops, SparseCore 0:
  25.5 51.3 all-gather.7
  177.9 54.6 all-gather.9

commit v4 on v3

--- a/solution.py
+++ b/solution.py
@@ -82,10 +82,9 @@
         theirs_ref[pl.ds(part * 32, 32), :] = rows_ref[pl.ds(theirs, 32), :].astype(BF)
 
 
-def split_halves(place, rows_ref, mine_ref, theirs_ref):
-    core = place[2]
-    mine_ref[...] = rows_ref[pl.ds(pl.multiple_of(core * 64, 64), 64), :].astype(BF)
-    theirs_ref[...] = rows_ref[pl.ds(pl.multiple_of((1 - core) * 64, 64), 64), :].astype(BF)
+def both(mine, sibling, shard, own):
+    cols = half_at(shard, own)
+    return jnp.concatenate([mine[:, cols], sibling[:, cols]], axis=0)
 
 
 def core_rows(place, ref):
@@ -96,10 +95,10 @@
 
 
 def attend_kernel(
-    place, x_mine, x_sib, w_own, w_oth, b_qv, id_q, id_k, wo_own, wo_oth,
+    place, x_mine, x_sib, tokens, w_own, w_oth, b_qv, id_q, id_k, wo_own, wo_oth,
     q_ref, k_ref, v_ref, o_ref, ob_ref, lse_ref, mine_ref, theirs_ref, part_ref,
 ):
-    shard, block, core = place[0], place[1], place[2]
+    shard, core = place[0], place[2]
     biases = b_qv[...].astype(F32)
     own, oth = half_at(shard, True), half_at(shard, False)
 
@@ -109,15 +108,15 @@
         for x, side in ((x_mine, core), (x_sib, 1 - core)):
             x_own = x[blocks, :, own].reshape(256, HALF)
             x_oth = x[blocks, :, oth].reshape(256, HALF)
-            queries = mm(x_own, w_own[0]) + mm(x_oth, w_oth[0]) + biases[0:1]
             keys = mm(x_own, w_own[1]) + mm(x_oth, w_oth[1])
             values = mm(x_own, w_own[2]) + mm(x_oth, w_oth[2]) + biases[1:2]
-            q_ref[blocks, side] = queries.astype(BF).reshape(4, 64, COLS)
             k_ref[blocks, side] = keys.astype(BF).reshape(4, 64, COLS)
             v_ref[blocks, side] = values.astype(BF).reshape(4, 64, COLS)
 
     keys, values = k_ref[...].reshape(LEN, COLS), v_ref[...].reshape(LEN, COLS)
-    q_heads = by_head(q_ref[block].reshape(BLK, COLS) * BF(HD ** -0.5))
+    q = (mm(tokens[:, own], w_own[0]) + mm(tokens[:, oth], w_oth[0]) + biases[0:1]).astype(BF)
+    q_ref[...] = q
+    q_heads = by_head(q * BF(HD ** -0.5))
     allowed = id_k[place[1]] == jnp.concatenate(
         [id_q[index][:, 0:BLK] for index in range(RING)], axis=1
     )
@@ -142,13 +141,13 @@
 
 
 def first_norm(summed, gain, shift):
-    return norm_rows(summed[...], gain[0:1, :].astype(F32), shift[0:1, :].astype(F32))
+    return norm_rows(summed, gain[0:1, :].astype(F32), shift[0:1, :].astype(F32))
 
 
 def first_norm_kernel(place, tokens, chip, recv, extra, gain, shift, s_ref, hb_ref):
     branch = chip[...].astype(F32) + recv[...].astype(F32) + extra[0:1, :].astype(F32)
     s_ref[...] = core_rows(place, tokens).astype(F32) + branch
-    hb_ref[...] = first_norm(s_ref, gain, shift)[0].astype(BF)
+    hb_ref[...] = first_norm(s_ref[...], gain, shift)[0].astype(BF)
 
 
 def other_up(other, side):
@@ -160,11 +159,11 @@
 
 
 def up_down_kernel(
-    place, hb, up_own, down_own, other, b_up,
+    place, hb, hb_sib, up_own, down_own, other, b_up,
     ub_ref, slope_ref, mine_ref, theirs_ref, part_ref,
 ):
     shard = place[0]
-    own, oth = hb[:, half_at(shard, True)], hb[:, half_at(shard, False)]
+    own, oth = both(hb, hb_sib, shard, True), both(hb, hb_sib, shard, False)
     for side in range(2):
         cols = pl.ds(side * HALF, HALF)
         before = mm(own, up_own[:, cols]) + mm(oth, other_up(other, side)) + b_up[:, cols].astype(F32)
@@ -174,14 +173,15 @@
     after = ub_ref[...]
     part_ref[:, half_at(shard, True)] = mm(after, down_own[...])
     part_ref[:, half_at(shard, False)] = mm(after, other_down(other))
-    split_halves(place, part_ref, mine_ref, theirs_ref)
+    mine_ref[...] = part_ref[0:64, :].astype(BF)
+    theirs_ref[...] = part_ref[64:128, :].astype(BF)
 
 
 def second_norm_kernel(
     place, first, chip, recv, extra, gain, shift, cot, out_ref, dx_ref, dz_ref, sums_ref, keep
 ):
     far = place[3]
-    middle = first_norm(first, gain, shift)[0]
+    middle = first_norm(first[...], gain, shift)[0]
     gains = gain[1:2, :].astype(F32)
     branch = chip[...].astype(F32) + recv[...].astype(F32) + extra[1:2, :].astype(F32)
     hidden, normed, factor = norm_rows(middle + branch, gains, shift[1:2, :].astype(F32))
@@ -189,7 +189,8 @@
     out_ref[...] = keep[pl.ds(pl.multiple_of(far * 32, 32), 32), :]
     grad = core_rows(place, cot)
     back = norm_back(grad, normed, factor, gains)
-    dx_ref[...] = back
+    dx_ref[0:64, :] = back
+    dx_ref[64:128, :] = first[...]
     low = back.astype(BF)
     dz_ref[...] = low
     sums_ref[0:1, :] = jnp.sum(low.astype(F32), axis=0, keepdims=True)
@@ -199,10 +200,10 @@
 
 
 def down_up_kernel(
-    place, dz, slope, up_own, down_own, other, da_ref, mine_ref, theirs_ref, part_ref
+    place, dz, dz_sib, slope, up_own, down_own, other, da_ref, mine_ref, theirs_ref, part_ref
 ):
     shard = place[0]
-    own, oth = dz[:, half_at(shard, True)], dz[:, half_at(shard, False)]
+    own, oth = both(dz, dz_sib, shard, True), both(dz, dz_sib, shard, False)
     after = mm(own, down_own[...], NT) + mm(oth, other_down(other), NT)
     da_ref[...] = (after * slope[...]).astype(BF)
     before = da_ref[...]
@@ -210,15 +211,19 @@
     part_ref[:, half_at(shard, False)] = sum(
         mm(before[:, side * HALF : (side + 1) * HALF], other_up(other, side), NT) for side in range(2)
     )
-    split_halves(place, part_ref, mine_ref, theirs_ref)
-
-
-def unit_grads_kernel(place, hb, da, ub, dz, pair_fwd, pair_dz, pair_da, out_ref, bias_ref):
+    mine_ref[...] = part_ref[0:64, :].astype(BF)
+    theirs_ref[...] = part_ref[64:128, :].astype(BF)
+
+
+def unit_grads_kernel(
+    place, hb, hb_sib, da, ub, dz, dz_sib, pair_ub, pair_late, pair_dz, pair_da, out_ref, bias_ref
+):
     shard = place[0]
-    rows = jnp.concatenate([hb[:, half_at(shard, True)], pair_fwd[:, 0:512]], axis=0)
+    rows = jnp.concatenate([both(hb, hb_sib, shard, True), pair_late[:, 0:512]], axis=0)
     units = jnp.concatenate([da[...], pair_da[...]], axis=0)
-    after = jnp.concatenate([ub[...], pair_fwd[:, 512:1536]], axis=0)
-    grads = jnp.concatenate([dz[:, half_at(shard, True)], pair_dz[...]], axis=0)
+    pair_after = jnp.concatenate([pair_ub[...], pair_late[:, 512:1024]], axis=1)
+    after = jnp.concatenate([ub[...], pair_after], axis=0)
+    grads = jnp.concatenate([both(dz, dz_sib, shard, True), pair_dz[...]], axis=0)
     for part in range(4):
         cols = slice(part * COLS, (part + 1) * COLS)
         term = mm(rows, units[:, cols], TN).astype(BF)
@@ -236,11 +241,11 @@
 
 
 def first_back_kernel(
-    place, first, dx, chip, recv, gain, shift, sums_in, d_ref, low_ref, sums_ref, keep
+    place, dx, chip, recv, gain, shift, sums_in, d_ref, low_ref, sums_ref, keep
 ):
     far = place[3]
-    _, normed, factor = first_norm(first, gain, shift)
-    grad = dx[...] + (chip[...].astype(F32) + recv[...].astype(F32))
+    _, normed, factor = first_norm(dx[64:128, :], gain, shift)
+    grad = dx[0:64, :] + (chip[...].astype(F32) + recv[...].astype(F32))
     back = norm_back(grad, normed, factor, gain[0:1, :].astype(F32))
     keep[...] = back
     d_ref[...] = keep[pl.ds(pl.multiple_of(far * 32, 32), 32), :]
@@ -260,13 +265,14 @@
 
 
 def out_back_kernel(
-    place, low, o, lse, wo_own, wo_oth, own_ref, oth_ref, d_ref, delta_ref, pack_ref, nat_ref
+    place, low, low_sib, o, lse, wo_own, wo_oth, own_ref, oth_ref, d_ref, delta_ref, pack_ref, nat_ref
 ):
     shard = place[0]
-    nat_ref[0:32, :] = low[0, 0:32, :]
-    nat_ref[32:64, :] = low[1, 0:32, :]
-    nat_ref[64:96, :] = low[0, 32:64, :]
-    nat_ref[96:128, :] = low[1, 32:64, :]
+    core = place[2]
+    for part in range(2):
+        for rows, side in ((low, core), (low_sib, 1 - core)):
+            at = pl.ds(pl.multiple_of(part * 64 + side * 32, 32), 32)
+            nat_ref[at, :] = rows[part * 32 : part * 32 + 32, :]
     own, oth = nat_ref[:, half_at(shard, True)], nat_ref[:, half_at(shard, False)]
     own_ref[...] = own
     oth_ref[...] = oth
@@ -291,7 +297,7 @@
 
 
 def query_grad_kernel(place, q, k, v, d_out, lse, delta, id_q, id_k, dq_ref, acc_ref):
-    q_heads = by_head(q[place[1]].reshape(BLK, COLS) * BF(HD ** -0.5))
+    q_heads = by_head(q[...] * BF(HD ** -0.5))
     d_heads = by_head(d_out[...])
     acc_ref[...] = jnp.zeros_like(acc_ref)
 
@@ -312,9 +318,23 @@
 
 
 def key_grad_kernel(
-    place, q, k, v, dq, recv, ids, id_k, w_own, w_oth, d_ref, mine_ref, theirs_ref, part_ref
-):
-    shard, block = place[0], place[1]
+    place, x_mine, x_sib, b_qv, k, v, dq, recv, ids, id_k, w_own, w_oth,
+    d_ref, mine_ref, theirs_ref, part_ref, q,
+):
+    shard, block, core = place[0], place[1], place[2]
+    bias = b_qv[0:1, :].astype(F32)
+
+    @pl.loop(0, RING // 4)
+    def _(step):
+        blocks = pl.ds(step * 4, 4)
+        for x, side in ((x_mine, core), (x_sib, 1 - core)):
+            queries = (
+                mm(x[blocks, :, half_at(shard, True)].reshape(256, HALF), w_own[0])
+                + mm(x[blocks, :, half_at(shard, False)].reshape(256, HALF), w_oth[0])
+                + bias
+            )
+            q[blocks, side] = queries.astype(BF).reshape(4, 64, COLS)
+
     keys, values = k[block].reshape(BLK, COLS), v[block].reshape(BLK, COLS)
     own_ids = id_k[block]
 
@@ -422,10 +442,6 @@
     return lax.ppermute(value, axis, [(index, index ^ bit) for index in range(size)])
 
 
-def pair_gather(value):
-    return lax.all_gather(value, "tensor", axis=0, axis_index_groups=[[0, 1], [2, 3]])
-
-
 def tensor_sum(mine, theirs):
     chip = (mine.astype(F32) + swap(theirs, "tensor", 1).astype(F32)).astype(BF)
     return chip, swap(chip, "tensor", 2)
@@ -466,8 +482,8 @@
     whole = pltpu.VMEM((BLK, D), F32)
     q, k, v, o, ob, lse, mine, theirs = call(
         attend_kernel, 10,
-        [all_heads] * 3 + [((BLK, COLS), F32), ((BLK, COLS), BF), ((1, HEADS * BLK), F32)] + halves,
-        place, x_mine, x_sib, w_in, in_oth, b_qv[0], id_heads, id_column,
+        [((BLK, COLS), BF)] + [all_heads] * 2 + [((BLK, COLS), F32), ((BLK, COLS), BF), ((1, HEADS * BLK), F32)] + halves,
+        place, x_mine, x_sib, tokens, w_in, in_oth, b_qv[0], id_heads, id_column,
         w_out, out_oth,
         scratch=[whole], vmem=60,
     )
@@ -476,51 +492,57 @@
         first_norm_kernel, 1, [((64, D), F32), ((64, D), BF)],
         place, tokens, chip, recv, extra, gain, shift,
     )
-    hb = pair_gather(low_mid).reshape(BLK, D)
+    hb_sib = swap(low_mid, "tensor", 1)
     ub, slope, mine, theirs = call(
         up_down_kernel, 2, [((BLK, UNITS), BF), ((BLK, UNITS), F32)] + halves,
-        place, hb, w_up, w_down, other, b_up,
+        place, low_mid, hb_sib, w_up, w_down, other, b_up,
         scratch=[whole],
     )
     away = (1 - shard) * HALF
+
+    def away_half(mine, sibling):
+        rows = [lax.dynamic_slice_in_dim(half, away, HALF, 1) for half in (mine, sibling)]
+        return jnp.concatenate(rows, axis=0)
+
     pair_in = swap(
         jnp.concatenate([ob, lax.dynamic_slice_in_dim(tokens, away, HALF, 1)], axis=1), "shard", 1
     )
-    pair_fwd = swap(
-        jnp.concatenate([lax.dynamic_slice_in_dim(hb, away, HALF, 1), ub], axis=1), "shard", 1
+    pair_ub = swap(ub[:, 0:HALF], "shard", 1)
+    pair_late = swap(
+        jnp.concatenate([away_half(low_mid, hb_sib), ub[:, HALF:UNITS]], axis=1), "shard", 1
     )
     chip, recv = tensor_sum(mine, theirs)
     hidden_out, dx, low_second, sums = call(
         second_norm_kernel, 2,
-        [((32, D), F32), ((64, D), F32), ((64, D), BF), ((8, D), F32)],
+        [((32, D), F32), ((BLK, D), F32), ((64, D), BF), ((8, D), F32)],
         place, first, chip, recv, extra, gain, shift, cotangent,
         scratch=[pltpu.VMEM((64, D), F32)],
     )
-    dz = pair_gather(low_second).reshape(BLK, D)
-    pair_dz = swap(lax.dynamic_slice_in_dim(dz, away, HALF, 1), "shard", 1)
+    dz_sib = swap(low_second, "tensor", 1)
+    dz_sib, pair_ub = together((dz_sib, pair_ub))
+    pair_dz = swap(away_half(low_second, dz_sib), "shard", 1)
     da, mine, theirs = call(
         down_up_kernel, 2, [((BLK, UNITS), BF)] + halves,
-        place, dz, slope, w_up, w_down, other,
+        place, low_second, dz_sib, slope, w_up, w_down, other,
         scratch=[whole],
     )
     pair_da = swap(da, "shard", 1)
-    mine, pair_fwd = together((mine, pair_fwd))
     chip, recv = tensor_sum(mine, theirs)
     d_first, low_first, sums = call(
         first_back_kernel, 1.5,
         [((32, D), F32), ((64, D), BF), ((8, D), F32)],
-        place, first, dx, chip, recv, gain, shift, sums,
-        scratch=[pltpu.VMEM((64, D), F32)], vmem=60,
-    )
-    low_pairs = pair_gather(low_first)
+        place, dx, chip, recv, gain, shift, sums,
+        scratch=[pltpu.VMEM((64, D), F32)],
+    )
+    low_sib = swap(low_first, "tensor", 1)
     low_own, low_oth, d_out, delta, packed = call(
         out_back_kernel, 1.5,
         [
             ((BLK, HALF), BF), ((BLK, HALF), BF), ((BLK, COLS), BF), ((1, HEADS * BLK), F32),
             ((RING, 144, COLS), BF),
         ],
-        place, low_pairs, o, lse, w_out, out_oth,
-        scratch=[pltpu.VMEM((BLK, D), BF)],
+        place, low_first, low_sib, o, lse, w_out, out_oth,
+        scratch=[pltpu.VMEM((BLK, D), BF)], vmem=60,
     )
     packs = lax.all_to_all(packed, "context", 0, 0, tiled=True)
     (dq,) = call(
@@ -528,10 +550,10 @@
         place, q, k, v, d_out, lse, delta, id_heads, id_column,
         scratch=[pltpu.VMEM((HEADS * BLK, COLS), F32)], vmem=60,
     )
-    hb, dq = together((hb, dq))
+    low_mid, dq = together((low_mid, dq))
     unit_grads, unit_small = call(
         unit_grads_kernel, 3, [((RING, 256, COLS), BF), ((8, COLS), F32)],
-        place, hb, da, ub, dz, pair_fwd, pair_dz, pair_da,
+        place, low_mid, hb_sib, da, ub, low_second, dz_sib, pair_ub, pair_late, pair_dz, pair_da,
     )
     packs, unit_grads, dq = together((packs, unit_grads, dq))
     unit_recv = lax.all_to_all(unit_grads, "context", 0, 0, tiled=True)
@@ -541,8 +563,8 @@
     sums = sums + swap(sums, "shard", 1)
     d_mixed, mine, theirs = call(
         key_grad_kernel, 6, [((BLK, 3 * COLS), BF)] + halves,
-        place, q, k, v, dq, packs, id_heads, id_column, w_in, in_oth,
-        scratch=[whole], vmem=60,
+        place, x_mine, x_sib, b_qv[0], k, v, dq, packs, id_heads, id_column, w_in, in_oth,
+        scratch=[whole, pltpu.VMEM((RING, 2, 64, COLS), BF)], vmem=60,
     )
     d_pair = swap(d_mixed, "shard", 1)
     chip = mine.astype(F32) + swap(theirs, "tensor", 1).astype(F32)

time: 244 us -> 239 us (0.980)
  blocking collectives: 6.15 us -> 0 us
    all_gather x3 -> x0, blocking collectives: 6.15 us -> none  [pair_gather(): lax.all_gather(value, 'tensor', axis=0, axis_index_groups=[[0, 1], [2, 3]])]
    ppermute x20 -> x24, waiting for transfers between devices: 51.1 us -> 54.9 us  [swap(): lax.ppermute(value, axis, [(index, index ^ bit) for index in range(size)])]
    unnamed x84 -> x64, local copies, waits for them, and re-layouts: 8.96 us -> 6.62 us
    ppermute x20 -> x24, starting transfers between devices: 24.5 us -> 24.2 us  [swap(): lax.ppermute(value, axis, [(index, index ^ bit) for index in range(size)])]
  transfers between devices with their start and end apart: 27 -> 31, of which waited for: 18 -> 22; matrix products, arithmetic and copies ran while one was open for 3% -> 3% of each run, Pallas kernels for 18% -> 19%
where the time goes in v4:
time: 239 us; the launch traced here: 238 us
  waiting for transfers between devices  105 us (44%)
  Pallas kernels  54.8 us (23%)
  starting transfers between devices  48 us (20%)
  between operations  14.5 us (6%)
  local copies, waits for them, and re-layouts  10.3 us (4%)
  other arithmetic  5.32 us (2%)
    ppermute x24, waiting for transfers between devices, swap(): lax.ppermute(value, axis, [(index, index ^ bit) for index in range(size)])  54.9 us
    pallas_call x15, Pallas kernels, call(): pl.pallas_call(kernel, out_shape=[jax.ShapeDtypeStruct(shape, dtype) for...  54.8 us
    ppermute x24, starting transfers between devices, swap(): lax.ppermute(value, axis, [(index, index ^ bit) for index in range(size)])  24.2 us
    all_to_all x1, waiting for transfers between devices, shards(): recv = lax.all_to_all(totals, 'context', 0, 0, tiled=True)  17.8 us
    all_to_all x1, waiting for transfers between devices, shards(): recv = lax.all_to_all(in_grads, 'context', 0, 0, tiled=True)  15.3 us
    all_to_all x1, starting transfers between devices, shards(): x_mine = lax.all_to_all(spread, 'context', 0, 0, tiled=True)  8.46 us
    unnamed x64, local copies, waits for them, and re-layouts  6.62 us
    all_to_all x1, waiting for transfers between devices, shards(): packs = lax.all_to_all(packed, 'context', 0, 0, tiled=True)  5.98 us
  transfers between devices with their start and end apart: 31, of which 22 were waited for; matrix products, arithmetic and copies ran while one was open for 3% of the time, Pallas kernels for 19%

profile of v4, /device:TPU:0, one launch (start us, length us, event | category | flops | bytes accessed | tf_op | source)
XLA Modules:
  0.0 238.3 jit_solution(13611613328938448450)
XLA Ops:
  7.2 1.0 slice_select_fusion
  8.2 1.6 broadcast_in_dim.30
  9.8 8.5 %all-to-all-start = ((bf16[16,64,1024]{2,1,0:T(8,128)(2,1)}), bf16[16,64,1024]{2,1,0:T(8,128)(2,1)}, u32[]{:S(2)}, u32[]{:S(2)}) async-start(bf16[16,64,1024]{2,1,0:T(8,128)(2,1)} %broadcast_in_dim.30), calls=%async_computation | async-start | bytes 4194304 | tf_op jit(solution)/shard_map/all_to_all | solution.py:474
  18.4 1.6 collective-permute-start
  20.0 3.5 %collective-permute-done = bf16[128,512]{1,0:T(8,128)(2,1)S(1)} collective-permute-done((bf16[128,512]{1,0:T(8,128)(2,1)S(1)}, bf16[128,512]{1,0:T(8,128)(2,1)S(1)}, u32[]{:S(2)}, u32[]{:S(2)}) %collective-permute-start) | collective-permute-done | bytes 131104 | tf_op jit(solution)/shard_map/ppermute | solution.py:442
  23.5 1.5 collective-permute-start.1
  25.5 21.5 %collective-permute-done.2.wo_oth = bf16[256,512]{1,0:T(8,128)(2,1)} collective-permute-done((bf16[256,512]{1,0:T(8,128)(2,1)S(1)}, bf16[256,512]{1,0:T(8,128)(2,1)}, u32[]{:S(2)}, u32[]{:S(2)}) %collective-permute-start.2) | collective-permute-done | bytes 262176 | tf_op jit(solution)/shard_map/ppermute | solution.py:442
  47.0 3.6 %all-to-all-done.x_mine = bf16[16,64,1024]{2,1,0:T(8,128)(2,1)} async-done(((bf16[16,64,1024]{2,1,0:T(8,128)(2,1)}), bf16[16,64,1024]{2,1,0:T(8,128)(2,1)}, u32[]{:S(2)}, u32[]{:S(2)}) %all-to-all-start) | async-done | bytes 2097184 | tf_op jit(solution)/shard_map/all_to_all | solution.py:474
  50.6 1.3 copy.23.id_k
  52.6 2.5 %collective-permute-done.3.x_sib = bf16[16,64,1024]{2,1,0:T(8,128)(2,1)} collective-permute-done((bf16[16,64,1024]{2,1,0:T(8,128)(2,1)}, bf16[16,64,1024]{2,1,0:T(8,128)(2,1)}, u32[]{:S(2)}, u32[]{:S(2)}) %collective-permute-start.3) | collective-permute-done | bytes 2097184 | tf_op jit(solution)/shard_map/ppermute | solution.py:442
  55.8 10.4 %shard_map.203 = (bf16[128,256]{1,0:T(8,128)(2,1)}, bf16[16,2,64,256]{3,2,1,0:T(8,128)(2,1)}, bf16[16,2,64,256]{3,2,1,0:T(8,128)(2,1)}, f32[128,256]{1,0:T(8,128...) custom-call(s32[4]{0:T(128)} %pad_add_fusion.place, ...), custom_call_target="tpu_custom_call" | custom-call | flops 11000000512 | bytes 30000000 | tf_op jit(solution)/shard_map/pallas_call | solution.py:38
  66.3 1.4 collective-permute-done.4
  67.7 0.9 add_convert_fusion.2.chip
  68.6 3.1 %collective-permute-start.5 = (bf16[64,1024]{1,0:T(8,128)(2,1)S(1)}, bf16[64,1024]{1,0:T(8,128)(2,1)S(1)}, u32[]{:S(2)}, u32[]{:S(2)}) collective-permute-start(bf16[64,1024]{1,0:T(8,128)(2,1)S(1)} %add_convert_fusion.2.chip), channel_id=1, source_target_pairs={{0,2},{1,3},{2,0},{3,1},{4,6},{5,7},{6,4},{7,5},{8,10},{9,11},{10,... | collective-permute-start | bytes 393224 | tf_op jit(solution)/shard_map/ppermute | solution.py:442
  71.8 4.0 %collective-permute-done.5.recv = bf16[64,1024]{1,0:T(8,128)(2,1)S(1)} collective-permute-done((bf16[64,1024]{1,0:T(8,128)(2,1)S(1)}, bf16[64,1024]{1,0:T(8,128)(2,1)S(1)}, u32[]{:S(2)}, u32[]{:S(2)}) %collective-permute-start.5) | collective-permute-done | bytes 131104 | tf_op jit(solution)/shard_map/ppermute | solution.py:442
  75.8 0.8 shard_map.204
  76.6 0.7 copy-done.18
  77.3 1.3 collective-permute-done.6.hb_sib
  78.7 1.6 copy-done.7
  80.3 1.5 shard_map.205
  82.0 1.2 collective-permute-done.7
  83.2 3.1 %collective-permute-start.8 = (bf16[64,1024]{1,0:T(8,128)(2,1)S(1)}, bf16[64,1024]{1,0:T(8,128)(2,1)S(1)}, u32[]{:S(2)}, u32[]{:S(2)}) collective-permute-start(bf16[64,1024]{1,0:T(8,128)(2,1)S(1)} %add_convert_fusion.1.chip), channel_id=1, source_target_pairs={{0,2},{1,3},{2,0},{3,1},{4,6},{5,7},{6,4},{7,5},{8,10},{9,11},{10,... | collective-permute-start | bytes 393224 | tf_op jit(solution)/shard_map/ppermute | solution.py:442
  86.3 0.7 collective-permute-start.10
  87.0 4.1 %collective-permute-done.8.recv = bf16[64,1024]{1,0:T(8,128)(2,1)S(1)} collective-permute-done((bf16[64,1024]{1,0:T(8,128)(2,1)S(1)}, bf16[64,1024]{1,0:T(8,128)(2,1)S(1)}, u32[]{:S(2)}, u32[]{:S(2)}) %collective-permute-start.8) | collective-permute-done | bytes 131104 | tf_op jit(solution)/shard_map/ppermute | solution.py:442
  91.1 1.6 shard_map.206
  93.3 0.9 collective-permute-done.9.dz_sib
  94.1 2.0 shard_map.207
  96.4 1.2 collective-permute-done.11
  97.7 3.1 %collective-permute-start.12 = (bf16[64,1024]{1,0:T(8,128)(2,1)S(1)}, bf16[64,1024]{1,0:T(8,128)(2,1)S(1)}, u32[]{:S(2)}, u32[]{:S(2)}) collective-permute-start(bf16[64,1024]{1,0:T(8,128)(2,1)S(1)} %add_convert_fusion.chip), channel_id=1, source_target_pairs={{0,2},{1,3},{2,0},{3,1},{4,6},{5,7},{6,4},{7,5},{8,10},{9,11},{10,... | collective-permute-start | bytes 393224 | tf_op jit(solution)/shard_map/ppermute | solution.py:442
  100.8 4.0 %collective-permute-done.12.recv = bf16[64,1024]{1,0:T(8,128)(2,1)S(1)} collective-permute-done((bf16[64,1024]{1,0:T(8,128)(2,1)S(1)}, bf16[64,1024]{1,0:T(8,128)(2,1)S(1)}, u32[]{:S(2)}, u32[]{:S(2)}) %collective-permute-start.12) | collective-permute-done | bytes 131104 | tf_op jit(solution)/shard_map/ppermute | solution.py:442
  104.8 1.0 copy-done.21
  105.8 0.9 shard_map.208
  106.9 0.7 pad_maximum_fusion
  107.6 1.5 collective-permute-start.14
  109.7 2.7 %shard_map.209 = (bf16[128,512]{1,0:T(8,128)(2,1)}, bf16[128,512]{1,0:T(8,128)(2,1)}, bf16[128,256]{1,0:T(8,128)(2,1)}, f32[1,512]{1,0:T(1,128)}, bf16[16,144,256]{2,1,0:T(8,128)(2,1)}) custom-call(s32[4]{0:T(128)} %pad_add_fusion.place, bf16[64,1024]{1,0:T(8,128)(2,1)} %copy-done.13, bf16[64,1024]{1,0:T(8,128)(2,1)} %copy-done.30, ...), custom_call_target="tpu_custom_call" | custom-call | flops 1650000000 | bytes 4500000 | tf_op jit(solution)/shard_map/pallas_call | solution.py:38
  112.4 4.0 %all-to-all-start.1 = ((bf16[16,144,256]{2,1,0:T(8,128)(2,1)}), bf16[16,144,256]{2,1,0:T(8,128)(2,1)S(1)}, u32[]{:S(2)}, u32[]{:S(2)}) async-start(bf16[16,144,256]{2,1,0:T(8,128)(2,1)} %get-tuple-element.90), calls=%async_computation.1 | async-start | bytes 2359296 | tf_op jit(solution)/shard_map/all_to_all | solution.py:547
  116.6 0.7 collective-permute-start.15
  117.2 1.5 collective-permute-start.16
  118.7 7.8 %shard_map.210.dq = bf16[128,256]{1,0:T(8,128)(2,1)} custom-call(s32[4]{0:T(128)} %pad_add_fusion.place, bf16[128,256]{1,0:T(8,128)(2,1)} %get-tuple-element.91.q, bf16[16,2,64,256]{3,2,1,0:T(8,128)(2,1)} %get-tuple-element.85.k, bf16[16,2,64,256]{3,2,1,0:T(8,128)(2,1)} %get-tuple-element.86.v, bf16[128,256]{1,0:T(8,128)(2,1)} %get-tuple-element.92.d_out, ...), custom_call_target="tpu_custom_call" | custom-call | flops 5500000256 | bytes 15000000 | tf_op jit(solution)/shard_map/pallas_call | solution.py:38
  126.5 1.3 collective-permute-done.16.pair_da
  127.8 2.6 %shard_map.211 = (bf16[16,256,256]{2,1,0:T(8,128)(2,1)}, f32[8,256]{1,0:T(8,128)S(1)}) custom-call(s32[4]{0:T(128)S(1)} %copy-done.5, bf16[64,1024]{1,0:T(8,128)(2,1)S(1)} %get-tuple-element.94.hb, bf16[64,1024]{1,0:T(8,128)(2,1)S(1)} %collective-permute-done.6.hb_sib, bf16[128,1024]{1,0:T(8,128)(2,1)S(1)} %copy-done.11, ...), custom_call_target="tpu_custom_call" | custom-call | flops 3300000000 | bytes 9000000 | tf_op jit(solution)/shard_map/pallas_call | solution.py:38
  130.4 6.0 %all-to-all-done.1.recv = bf16[16,144,256]{2,1,0:T(8,128)(2,1)S(1)} async-done(((bf16[16,144,256]{2,1,0:T(8,128)(2,1)}), bf16[16,144,256]{2,1,0:T(8,128)(2,1)S(1)}, u32[]{:S(2)}, u32[]{:S(2)}) %all-to-all-start.1) | async-done | bytes 1179680 | tf_op jit(solution)/shard_map/all_to_all | solution.py:547
  136.4 1.0 copy-done.23
  137.4 3.7 %all-to-all-start.2 = ((bf16[16,256,256]{2,1,0:T(8,128)(2,1)}), bf16[16,256,256]{2,1,0:T(8,128)(2,1)S(1)}, u32[]{:S(2)}, u32[]{:S(2)}) async-start(bf16[16,256,256]{2,1,0:T(8,128)(2,1)} %get-tuple-element.109), calls=%async_computation.2 | async-start | bytes 4194304 | tf_op jit(solution)/shard_map/all_to_all | solution.py:559
  141.9 13.6 %shard_map.212 = (bf16[128,768]{1,0:T(8,128)(2,1)}, bf16[64,1024]{1,0:T(8,128)(2,1)}, bf16[64,1024]{1,0:T(8,128)(2,1)}) custom-call(s32[4]{0:T(128)} %pad_add_fusion.place, bf16[16,64,1024]{2,1,0:T(8,128)(2,1)} %all-to-all-done.x_mine, bf16[16,64,1024]{2,1,0:T(8,128)(2,1)} %collective-permute-done.3.x_sib, bf16[2,256]{1,0:T(2,128)(2,1)} %bitcast.69, ...), custom_call_target="tpu_custom_call" | custom-call | flops 6600000000 | bytes 18000000 | tf_op jit(solution)/shard_map/pallas_call | solution.py:38
  155.4 1.5 collective-permute-start.19
  157.5 0.7 collective-permute-done.22
  158.1 0.8 collective-permute-start.23
  159.0 5.4 %collective-permute-done.23 = f32[8,256]{1,0:T(8,128)S(1)} collective-permute-done((f32[8,256]{1,0:T(8,128)S(1)}, f32[8,256]{1,0:T(8,128)S(1)}, u32[]{:S(2)}, u32[]{:S(2)}) %collective-permute-start.23) | collective-permute-done | bytes 8224 | tf_op jit(solution)/shard_map/ppermute | solution.py:442
  164.4 0.9 copy-done.12
  165.3 2.0 shard_map.213
  167.4 4.6 %all-to-all-done.2.recv = bf16[16,256,256]{2,1,0:T(8,128)(2,1)S(1)} async-done(((bf16[16,256,256]{2,1,0:T(8,128)(2,1)}), bf16[16,256,256]{2,1,0:T(8,128)(2,1)S(1)}, u32[]{:S(2)}, u32[]{:S(2)}) %all-to-all-start.2) | async-done | bytes 2097184 | tf_op jit(solution)/shard_map/all_to_all | solution.py:559
  172.0 1.5 shard_map.214
  173.5 3.8 %all-to-all-start.3 = ((bf16[16,144,256]{2,1,0:T(8,128)(2,1)}), bf16[16,144,256]{2,1,0:T(8,128)(2,1)S(1)}, u32[]{:S(2)}, u32[]{:S(2)}) async-start(bf16[16,144,256]{2,1,0:T(8,128)(2,1)} %shard_map.213), calls=%async_computation.3 | async-start | bytes 2359296 | tf_op jit(solution)/shard_map/all_to_all | solution.py:579
  177.5 1.3 collective-permute-done.17
  178.8 2.8 %collective-permute-start.18 = (bf16[32,1024]{1,0:T(8,128)(2,1)S(1)}, bf16[32,1024]{1,0:T(8,128)(2,1)S(1)}, u32[]{:S(2)}, u32[]{:S(2)}) collective-permute-start(bf16[32,1024]{1,0:T(8,128)(2,1)S(1)} %dynamic-slice_convert_fusion), channel_id=1, source_target_pairs={{0,2},{1,3},{2,0},{3,1},{4,6},{5,7},{6,4},{7,5},{8,10},{9,11},{10,... | collective-permute-start | bytes 196616 | tf_op jit(solution)/shard_map/ppermute | solution.py:442
  181.6 15.3 %all-to-all-done.3.recv = bf16[16,144,256]{2,1,0:T(8,128)(2,1)S(1)} async-done(((bf16[16,144,256]{2,1,0:T(8,128)(2,1)}), bf16[16,144,256]{2,1,0:T(8,128)(2,1)S(1)}, u32[]{:S(2)}, u32[]{:S(2)}) %all-to-all-start.3) | async-done | bytes 1179680 | tf_op jit(solution)/shard_map/all_to_all | solution.py:579
  197.0 1.7 shard_map.215
  198.7 3.7 %all-to-all-start.4 = ((bf16[16,128,256]{2,1,0:T(8,128)(2,1)}), bf16[16,128,256]{2,1,0:T(8,128)(2,1)S(1)}, u32[]{:S(2)}, u32[]{:S(2)}) async-start(bf16[16,128,256]{2,1,0:T(8,128)(2,1)} %get-tuple-element.113), calls=%async_computation.4 | async-start | bytes 2097152 | tf_op jit(solution)/shard_map/all_to_all | solution.py:586
  202.3 0.7 add_add_fusion
  204.8 17.8 %all-to-all-done.4.recv = bf16[16,128,256]{2,1,0:T(8,128)(2,1)S(1)} async-done(((bf16[16,128,256]{2,1,0:T(8,128)(2,1)}), bf16[16,128,256]{2,1,0:T(8,128)(2,1)S(1)}, u32[]{:S(2)}, u32[]{:S(2)}) %all-to-all-start.4) | async-done | bytes 1048608 | tf_op jit(solution)/shard_map/all_to_all | solution.py:586
  222.6 2.0 shard_map.216
  224.6 3.2 %all-gather.7.cloned.1.call-done = bf16[4096,256]{1,0:T(8,128)(2,1)} async-done(((bf16[256,256]{1,0:T(8,128)(2,1)}), bf16[4096,256]{1,0:T(8,128)(2,1)}) %all-gather.7.cloned.1.call-update) | async-done | bytes 2097168 | tf_op jit(solution)/shard_map/all_gather | solution.py:581
  227.8 3.8 %shard_map.217 = (f32[512,1024]{1,0:T(8,128)}, f32[1024,512]{1,0:T(8,128)}) custom-call(s32[4]{0:T(128)} %pad_add_fusion.place, bf16[16,256,256]{2,1,0:T(8,128)(2,1)} %bitcast.61), custom_call_target="tpu_custom_call" | custom-call | flops 2200000000 | bytes 6000000 | tf_op jit(solution)/shard_map/pallas_call | solution.py:38
  (108 shorter events, 7.1 us)
Async XLA Ops:
  9.8 8.5 %copy-start.2 = (bf16[1,512,1024]{2,1,0:T(8,128)(2,1)S(1)}, bf16[1,512,1024]{2,1,0:T(8,128)(2,1)}, u32[]{:S(2)}) copy-start(bf16[1,512,1024]{2,1,0:T(8,128)(2,1)} %param.17) | copy-start | bytes 3145732
  9.8 8.6 %copy-start.3 = (bf16[1,1024,512]{2,1,0:T(8,128)(2,1)S(1)}, bf16[1,1024,512]{2,1,0:T(8,128)(2,1)}, u32[]{:S(2)}) copy-start(bf16[1,1024,512]{2,1,0:T(8,128)(2,1)} %param.19) | copy-start | bytes 3145732
  9.8 13.7 %copy-start.27 = (bf16[1,512,3,256]{3,1,2,0:T(8,128)(2,1)S(1)}, bf16[1,512,3,256]{3,1,2,0:T(8,128)(2,1)}, u32[]{:S(2)}) copy-start(bf16[1,512,3,256]{3,1,2,0:T(8,128)(2,1)} %param.14) | copy-start | bytes 2359300
  9.8 15.2 %copy-start.28 = (bf16[1,256,512]{2,1,0:T(8,128)(2,1)S(1)}, bf16[1,256,512]{2,1,0:T(8,128)(2,1)}, u32[]{:S(2)}) copy-start(bf16[1,256,512]{2,1,0:T(8,128)(2,1)} %param.16) | copy-start | bytes 786436
  9.8 40.9 %copy-start.26 = (s32[2048]{0:T(1024)S(1)}, s32[2048]{0:T(1024)}, u32[]{:S(2)}) copy-start(s32[2048]{0:T(1024)} %param.13) | copy-start | bytes 24580
  9.8 40.8 %all-to-all-start = ((bf16[16,64,1024]{2,1,0:T(8,128)(2,1)}), bf16[16,64,1024]{2,1,0:T(8,128)(2,1)}, u32[]{:S(2)}, u32[]{:S(2)}) async-start(bf16[16,64,1024]{2,1,0:T(8,128)(2,1)} %broadcast_in_dim.30), calls=%async_computation | async-start | bytes 4194304 | tf_op jit(solution)/shard_map/all_to_all | solution.py:474
  18.3 59.1 %all-gather.5.cloned.1.call-start = ((), (), s32[]{:S(2)}) async-start(), calls=%async_computation.5 | async-start | bytes 2228224 | tf_op jit(solution)/shard_map/all_gather | solution.py:466
  18.4 5.0 %collective-permute-start = (bf16[128,512]{1,0:T(8,128)(2,1)S(1)}, bf16[128,512]{1,0:T(8,128)(2,1)S(1)}, u32[]{:S(2)}, u32[]{:S(2)}) collective-permute-start(bf16[128,512]{1,0:T(8,128)(2,1)S(1)} %pad_maximum_fusion.2), channel_id=1, source_target_pairs={{0,64},{64,0},{1,65},{65,1},{2,66},{66,2},{3,67},{67,3},{4,68},{68... | collective-permute-start | bytes 393224 | tf_op jit(solution)/shard_map/ppermute | solution.py:442
  23.4 2.0 copy-start.24
  23.5 23.6 %collective-permute-start.1 = (bf16[3,512,256]{2,1,0:T(8,128)(2,1)S(1)}, bf16[3,512,256]{2,1,0:T(8,128)(2,1)}, u32[]{:S(2)}, u32[]{:S(2)}) collective-permute-start(bf16[3,512,256]{2,1,0:T(8,128)(2,1)S(1)} %bitcast.64), channel_id=1, source_target_pairs={{0,64},{64,0},{1,65},{65,1},{2,66},{66,2},{3,67},{67,3},{4,68},{68... | collective-permute-start | bytes 2359304 | tf_op jit(solution)/shard_map/ppermute | solution.py:442
  24.9 22.1 %collective-permute-start.2 = (bf16[256,512]{1,0:T(8,128)(2,1)S(1)}, bf16[256,512]{1,0:T(8,128)(2,1)}, u32[]{:S(2)}, u32[]{:S(2)}) collective-permute-start(bf16[256,512]{1,0:T(8,128)(2,1)S(1)} %bitcast.67), channel_id=1, source_target_pairs={{0,64},{64,0},{1,65},{65,1},{2,66},{66,2},{3,67},{67,3},{4,68},{68... | collective-permute-start | bytes 786440 | tf_op jit(solution)/shard_map/ppermute | solution.py:442
  50.6 4.5 %collective-permute-start.3 = (bf16[16,64,1024]{2,1,0:T(8,128)(2,1)}, bf16[16,64,1024]{2,1,0:T(8,128)(2,1)}, u32[]{:S(2)}, u32[]{:S(2)}) collective-permute-start(bf16[16,64,1024]{2,1,0:T(8,128)(2,1)} %all-to-all-done.x_mine), channel_id=1, source_target_pairs={{0,1},{1,0},{2,3},{3,2},{4,5},{5,4},{6,7},{7,6},{8,9},{9,8},{10,11... | collective-permute-start | bytes 6291464 | tf_op jit(solution)/shard_map/ppermute | solution.py:442
  55.7 20.0 %copy-start = (bf16[128,1024]{1,0:T(8,128)(2,1)S(1)}, bf16[128,1024]{1,0:T(8,128)(2,1)}, u32[]{:S(2)}) copy-start(bf16[128,1024]{1,0:T(8,128)(2,1)} %tokens.5) | copy-start | bytes 786436
  55.7 20.0 %copy-start.4 = (s32[4]{0:T(128)S(1)}, s32[4]{0:T(128)}, u32[]{:S(2)}) copy-start(s32[4]{0:T(128)} %pad_add_fusion.place) | copy-start | bytes 52
  55.7 20.0 %copy-start.15 = (bf16[1,2,1024]{2,1,0:T(2,128)(2,1)S(1)}, bf16[1,2,1024]{2,1,0:T(2,128)(2,1)}, u32[]{:S(2)}) copy-start(bf16[1,2,1024]{2,1,0:T(2,128)(2,1)} %param.20) | copy-start | bytes 12292
  55.7 20.1 %copy-start.16 = (bf16[1,2,1024]{2,1,0:T(2,128)(2,1)S(1)}, bf16[1,2,1024]{2,1,0:T(2,128)(2,1)}, u32[]{:S(2)}) copy-start(bf16[1,2,1024]{2,1,0:T(2,128)(2,1)} %param.21) | copy-start | bytes 12292
  55.7 20.1 %copy-start.17 = (bf16[1,2,1024]{2,1,0:T(2,128)(2,1)S(1)}, bf16[1,2,1024]{2,1,0:T(2,128)(2,1)}, u32[]{:S(2)}) copy-start(bf16[1,2,1024]{2,1,0:T(2,128)(2,1)} %param.22) | copy-start | bytes 12292
  66.1 1.6 collective-permute-start.4
  68.6 10.0 %copy-start.14 = (bf16[1,1024]{1,0:T(2,128)(2,1)S(1)}, bf16[1,1024]{1,0:T(2,128)(2,1)}, u32[]{:S(2)}) copy-start(bf16[1,1024]{1,0:T(2,128)(2,1)} %b_up.1) | copy-start | bytes 6148
  68.6 7.1 %collective-permute-start.5 = (bf16[64,1024]{1,0:T(8,128)(2,1)S(1)}, bf16[64,1024]{1,0:T(8,128)(2,1)S(1)}, u32[]{:S(2)}, u32[]{:S(2)}) collective-permute-start(bf16[64,1024]{1,0:T(8,128)(2,1)S(1)} %add_convert_fusion.2.chip), channel_id=1, source_target_pairs={{0,2},{1,3},{2,0},{3,1},{4,6},{5,7},{6,4},{7,5},{8,10},{9,11},{10,... | collective-permute-start | bytes 393224 | tf_op jit(solution)/shard_map/ppermute | solution.py:442
  76.6 0.7 copy-start.18
  77.3 1.3 collective-permute-start.6
  78.7 1.6 copy-start.7
  80.3 10.9 %copy-start.9 = (f32[128,1024]{1,0:T(8,128)S(1)}, f32[128,1024]{1,0:T(8,128)}, u32[]{:S(2)}) copy-start(f32[128,1024]{1,0:T(8,128)} %cot.1) | copy-start | bytes 1572868
  80.3 10.9 %copy-start.19 = (f32[64,1024]{1,0:T(8,128)S(1)}, f32[64,1024]{1,0:T(8,128)}, u32[]{:S(2)}) copy-start(f32[64,1024]{1,0:T(8,128)} %copy-done.18) | copy-start | bytes 786436
  81.7 1.4 collective-permute-start.7
  83.2 7.9 %collective-permute-start.8 = (bf16[64,1024]{1,0:T(8,128)(2,1)S(1)}, bf16[64,1024]{1,0:T(8,128)(2,1)S(1)}, u32[]{:S(2)}, u32[]{:S(2)}) collective-permute-start(bf16[64,1024]{1,0:T(8,128)(2,1)S(1)} %add_convert_fusion.1.chip), channel_id=1, source_target_pairs={{0,2},{1,3},{2,0},{3,1},{4,6},{5,7},{6,4},{7,5},{8,10},{9,11},{10,... | collective-permute-start | bytes 393224 | tf_op jit(solution)/shard_map/ppermute | solution.py:442
  86.3 6.9 %collective-permute-start.10 = (bf16[128,512]{1,0:T(8,128)(2,1)S(1)}, bf16[128,512]{1,0:T(8,128)(2,1)S(1)}, u32[]{:S(2)}, u32[]{:S(2)}) collective-permute-start(bf16[128,512]{1,0:T(8,128)(2,1)S(1)} %get-tuple-element.120), channel_id=1, source_target_pairs={{0,64},{64,0},{1,65},{65,1},{2,66},{66,2},{3,67},{67,3},{4,68},{68... | collective-permute-start | bytes 393224 | tf_op jit(solution)/shard_map/ppermute | solution.py:442
  91.1 3.0 %copy-start.8 = (bf16[2048,512]{1,0:T(8,128)(2,1)S(1)}, bf16[2048,512]{1,0:T(8,128)(2,1)}, u32[]{:S(2)}) copy-start(bf16[2048,512]{1,0:T(8,128)(2,1)} %all-gather.5.cloned.1.call-done) | copy-start | bytes 6291460
  92.8 3.4 %copy-start.20 = (f32[128,1024]{1,0:T(8,128)}, f32[128,1024]{1,0:T(8,128)S(1)}, u32[]{:S(2)}) copy-start(f32[128,1024]{1,0:T(8,128)S(1)} %get-tuple-element.76.dx) | copy-start | bytes 1572868
  92.8 1.3 collective-permute-start.9
  96.2 1.5 copy-start.10
  96.2 1.4 collective-permute-start.11
  97.7 7.1 %collective-permute-start.12 = (bf16[64,1024]{1,0:T(8,128)(2,1)S(1)}, bf16[64,1024]{1,0:T(8,128)(2,1)S(1)}, u32[]{:S(2)}, u32[]{:S(2)}) collective-permute-start(bf16[64,1024]{1,0:T(8,128)(2,1)S(1)} %add_convert_fusion.chip), channel_id=1, source_target_pairs={{0,2},{1,3},{2,0},{3,1},{4,6},{5,7},{6,4},{7,5},{8,10},{9,11},{10,... | collective-permute-start | bytes 393224 | tf_op jit(solution)/shard_map/ppermute | solution.py:442
  104.8 1.0 copy-start.21
  106.7 2.4 copy-start.13
  106.7 2.3 collective-permute-start.13
  107.6 18.9 %collective-permute-start.14 = (bf16[128,1024]{1,0:T(8,128)(2,1)}, bf16[128,1024]{1,0:T(8,128)(2,1)S(1)}, u32[]{:S(2)}, u32[]{:S(2)}) collective-permute-start(bf16[128,1024]{1,0:T(8,128)(2,1)} %pad_maximum_fusion), channel_id=1, source_target_pairs={{0,64},{64,0},{1,65},{65,1},{2,66},{66,2},{3,67},{67,3},{4,68},{68... | collective-permute-start | bytes 786440 | tf_op jit(solution)/shard_map/ppermute | solution.py:442
  109.1 0.7 copy-start.30
  112.4 4.8 %copy-start.11 = (bf16[128,1024]{1,0:T(8,128)(2,1)S(1)}, bf16[128,1024]{1,0:T(8,128)(2,1)}, u32[]{:S(2)}) copy-start(bf16[128,1024]{1,0:T(8,128)(2,1)} %copy-done.10) | copy-start | bytes 786436
  112.4 24.0 %all-to-all-start.1 = ((bf16[16,144,256]{2,1,0:T(8,128)(2,1)}), bf16[16,144,256]{2,1,0:T(8,128)(2,1)S(1)}, u32[]{:S(2)}, u32[]{:S(2)}) async-start(bf16[16,144,256]{2,1,0:T(8,128)(2,1)} %get-tuple-element.90), calls=%async_computation.1 | async-start | bytes 2359296 | tf_op jit(solution)/shard_map/all_to_all | solution.py:547
  116.6 9.9 %collective-permute-start.15 = (bf16[128,512]{1,0:T(8,128)(2,1)S(1)}, bf16[128,512]{1,0:T(8,128)(2,1)S(1)}, u32[]{:S(2)}, u32[]{:S(2)}) collective-permute-start(bf16[128,512]{1,0:T(8,128)(2,1)S(1)} %pad_maximum_fusion.3), channel_id=1, source_target_pairs={{0,64},{64,0},{1,65},{65,1},{2,66},{66,2},{3,67},{67,3},{4,68},{68... | collective-permute-start | bytes 393224 | tf_op jit(solution)/shard_map/ppermute | solution.py:442
  117.2 10.6 %collective-permute-start.16 = (bf16[128,1024]{1,0:T(8,128)(2,1)S(1)}, bf16[128,1024]{1,0:T(8,128)(2,1)S(1)}, u32[]{:S(2)}, u32[]{:S(2)}) collective-permute-start(bf16[128,1024]{1,0:T(8,128)(2,1)S(1)} %copy-done.11), channel_id=1, source_target_pairs={{0,64},{64,0},{1,65},{65,1},{2,66},{66,2},{3,67},{67,3},{4,68},{68... | collective-permute-start | bytes 786440 | tf_op jit(solution)/shard_map/ppermute | solution.py:442
  118.7 9.2 %copy-start.5 = (s32[4]{0:T(128)S(1)}, s32[4]{0:T(128)}, u32[]{:S(2)}) copy-start(s32[4]{0:T(128)} %pad_add_fusion.place) | copy-start | bytes 52
  136.4 1.0 copy-start.23
  136.4 4.8 %copy-start.1 = (bf16[128,256]{1,0:T(8,128)(2,1)S(1)}, bf16[128,256]{1,0:T(8,128)(2,1)}, u32[]{:S(2)}) copy-start(bf16[128,256]{1,0:T(8,128)(2,1)} %get-tuple-element.104.ob) | copy-start | bytes 196612
  137.4 34.6 %all-to-all-start.2 = ((bf16[16,256,256]{2,1,0:T(8,128)(2,1)}), bf16[16,256,256]{2,1,0:T(8,128)(2,1)S(1)}, u32[]{:S(2)}, u32[]{:S(2)}) async-start(bf16[16,256,256]{2,1,0:T(8,128)(2,1)} %get-tuple-element.109), calls=%async_computation.2 | async-start | bytes 4194304 | tf_op jit(solution)/shard_map/all_to_all | solution.py:559
  141.2 86.6 %all-gather.7.cloned.1.call-start = ((), (), s32[]{:S(2)}) async-start(), calls=%async_computation.6 | async-start | bytes 2228224 | tf_op jit(solution)/shard_map/all_gather | solution.py:581
  141.3 23.1 %copy-start.6 = (s32[4]{0:T(128)S(1)}, s32[4]{0:T(128)}, u32[]{:S(2)}) copy-start(s32[4]{0:T(128)} %pad_add_fusion.place) | copy-start | bytes 52
  141.3 23.1 %copy-start.22 = (bf16[128,512]{1,0:T(8,128)(2,1)S(1)}, bf16[128,512]{1,0:T(8,128)(2,1)}, u32[]{:S(2)}) copy-start(bf16[128,512]{1,0:T(8,128)(2,1)} %get-tuple-element.105.low) | copy-start | bytes 393220
  141.3 23.1 %collective-permute-start.20 = (bf16[128,768]{1,0:T(8,128)(2,1)S(1)}, bf16[128,768]{1,0:T(8,128)(2,1)S(1)}, u32[]{:S(2)}, u32[]{:S(2)}) collective-permute-start(bf16[128,768]{1,0:T(8,128)(2,1)S(1)} %pad_maximum_fusion.1), channel_id=1, source_target_pairs={{0,64},{64,0},{1,65},{65,1},{2,66},{66,2},{3,67},{67,3},{4,68},{68... | collective-permute-start | bytes 589832 | tf_op jit(solution)/shard_map/ppermute | solution.py:442
  155.4 8.9 %collective-permute-start.19 = (bf16[128,768]{1,0:T(8,128)(2,1)}, bf16[128,768]{1,0:T(8,128)(2,1)S(1)}, u32[]{:S(2)}, u32[]{:S(2)}) collective-permute-start(bf16[128,768]{1,0:T(8,128)(2,1)} %get-tuple-element.103.d), channel_id=1, source_target_pairs={{0,64},{64,0},{1,65},{65,1},{2,66},{66,2},{3,67},{67,3},{4,68},{68... | collective-permute-start | bytes 589832 | tf_op jit(solution)/shard_map/ppermute | solution.py:442
  156.9 1.2 collective-permute-start.22
  156.9 7.4 %collective-permute-start.21 = (bf16[128,512]{1,0:T(8,128)(2,1)}, bf16[128,512]{1,0:T(8,128)(2,1)S(1)}, u32[]{:S(2)}, u32[]{:S(2)}) collective-permute-start(bf16[128,512]{1,0:T(8,128)(2,1)} %get-tuple-element.106), channel_id=1, source_target_pairs={{0,64},{64,0},{1,65},{65,1},{2,66},{66,2},{3,67},{67,3},{4,68},{68... | collective-permute-start | bytes 393224 | tf_op jit(solution)/shard_map/ppermute | solution.py:442
  158.1 6.2 %collective-permute-start.23 = (f32[8,256]{1,0:T(8,128)S(1)}, f32[8,256]{1,0:T(8,128)S(1)}, u32[]{:S(2)}, u32[]{:S(2)}) collective-permute-start(f32[8,256]{1,0:T(8,128)S(1)} %dynamic-slice_add_fusion), channel_id=1, source_target_pairs={{0,64},{64,0},{1,65},{65,1},{2,66},{66,2},{3,67},{67,3},{4,68},{68... | collective-permute-start | bytes 24584 | tf_op jit(solution)/shard_map/ppermute | solution.py:442
  164.4 0.9 copy-start.12
  173.5 3.9 %copy-start.29 = (bf16[64,1024]{1,0:T(8,128)(2,1)S(1)}, bf16[64,1024]{1,0:T(8,128)(2,1)}, u32[]{:S(2)}) copy-start(bf16[64,1024]{1,0:T(8,128)(2,1)} %get-tuple-element.102) | copy-start | bytes 393220
  173.5 5.3 %copy-start.25 = (bf16[64,1024]{1,0:T(8,128)(2,1)S(1)}, bf16[64,1024]{1,0:T(8,128)(2,1)}, u32[]{:S(2)}) copy-start(bf16[64,1024]{1,0:T(8,128)(2,1)} %get-tuple-element.101) | copy-start | bytes 393220
  173.5 23.5 %all-to-all-start.3 = ((bf16[16,144,256]{2,1,0:T(8,128)(2,1)}), bf16[16,144,256]{2,1,0:T(8,128)(2,1)S(1)}, u32[]{:S(2)}, u32[]{:S(2)}) async-start(bf16[16,144,256]{2,1,0:T(8,128)(2,1)} %shard_map.213), calls=%async_computation.3 | async-start | bytes 2359296 | tf_op jit(solution)/shard_map/all_to_all | solution.py:579
  177.4 1.4 collective-permute-start.17
  178.8 23.5 %collective-permute-start.18 = (bf16[32,1024]{1,0:T(8,128)(2,1)S(1)}, bf16[32,1024]{1,0:T(8,128)(2,1)S(1)}, u32[]{:S(2)}, u32[]{:S(2)}) collective-permute-start(bf16[32,1024]{1,0:T(8,128)(2,1)S(1)} %dynamic-slice_convert_fusion), channel_id=1, source_target_pairs={{0,2},{1,3},{2,0},{3,1},{4,6},{5,7},{6,4},{7,5},{8,10},{9,11},{10,... | collective-permute-start | bytes 196616 | tf_op jit(solution)/shard_map/ppermute | solution.py:442
  198.7 24.0 %all-to-all-start.4 = ((bf16[16,128,256]{2,1,0:T(8,128)(2,1)}), bf16[16,128,256]{2,1,0:T(8,128)(2,1)S(1)}, u32[]{:S(2)}, u32[]{:S(2)}) async-start(bf16[16,128,256]{2,1,0:T(8,128)(2,1)} %get-tuple-element.113), calls=%async_computation.4 | async-start | bytes 2097152 | tf_op jit(solution)/shard_map/all_to_all | solution.py:586
Sparse Core Ops, SparseCore 0:
  25.6 51.2 all-gather.4
  173.6 54.0 all-gather.6

commit v5 on v4

--- a/solution.py
+++ b/solution.py
@@ -16,6 +16,7 @@
 COLS = 256
 UNITS = 1024
 RING = 16
+EARLY = 768
 EPSILON = 1e-05
 NEGATIVE = -1e30
 ROOT_HALF = 0.7071067811865476
@@ -221,7 +222,7 @@
     shard = place[0]
     rows = jnp.concatenate([both(hb, hb_sib, shard, True), pair_late[:, 0:512]], axis=0)
     units = jnp.concatenate([da[...], pair_da[...]], axis=0)
-    pair_after = jnp.concatenate([pair_ub[...], pair_late[:, 512:1024]], axis=1)
+    pair_after = jnp.concatenate([pair_ub[...], pair_late[:, HALF : HALF + UNITS - EARLY]], axis=1)
     after = jnp.concatenate([ub[...], pair_after], axis=0)
     grads = jnp.concatenate([both(dz, dz_sib, shard, True), pair_dz[...]], axis=0)
     for part in range(4):
@@ -507,10 +508,7 @@
     pair_in = swap(
         jnp.concatenate([ob, lax.dynamic_slice_in_dim(tokens, away, HALF, 1)], axis=1), "shard", 1
     )
-    pair_ub = swap(ub[:, 0:HALF], "shard", 1)
-    pair_late = swap(
-        jnp.concatenate([away_half(low_mid, hb_sib), ub[:, HALF:UNITS]], axis=1), "shard", 1
-    )
+    pair_ub = swap(ub[:, 0:EARLY], "shard", 1)
     chip, recv = tensor_sum(mine, theirs)
     hidden_out, dx, low_second, sums = call(
         second_norm_kernel, 2,
@@ -544,7 +542,11 @@
         place, low_first, low_sib, o, lse, w_out, out_oth,
         scratch=[pltpu.VMEM((BLK, D), BF)], vmem=60,
     )
+    ub, packed = together((ub, packed))
     packs = lax.all_to_all(packed, "context", 0, 0, tiled=True)
+    pair_late = swap(
+        jnp.concatenate([away_half(low_mid, hb_sib), ub[:, EARLY:UNITS]], axis=1), "shard", 1
+    )
     (dq,) = call(
         query_grad_kernel, 5, [((BLK, COLS), BF)],
         place, q, k, v, d_out, lse, delta, id_heads, id_column,

time: 239 us -> 238 us (level)
  waiting for transfers between devices: 105 us -> 102 us
  starting transfers between devices: 48 us -> 50.4 us
    ppermute x24, waiting for transfers between devices: 54.9 us -> 59.5 us  [swap(): lax.ppermute(value, axis, [(index, index ^ bit) for index in range(size)])]
    all_to_all x1, waiting for transfers between devices: 5.98 us -> 1.94 us  [shards(): packs = lax.all_to_all(packed, 'context', 0, 0, tiled=True)]
    unnamed x64 -> x68, local copies, waits for them, and re-layouts: 6.62 us -> 6.63 us
  transfers between devices with their start and end apart: 31 -> 31, of which waited for: 22 -> 22; matrix products, arithmetic and copies ran while one was open for 3% -> 3% of each run, Pallas kernels for 19% -> 18%
where the time goes in v5:
time: 238 us; the launch traced here: 237 us
  waiting for transfers between devices  102 us (43%)
  Pallas kernels  54.8 us (23%)
  starting transfers between devices  50.4 us (21%)
  between operations  14.5 us (6%)
  local copies, waits for them, and re-layouts  10.3 us (4%)
  other arithmetic  4.6 us (2%)
    ppermute x24, waiting for transfers between devices, swap(): lax.ppermute(value, axis, [(index, index ^ bit) for index in range(size)])  59.5 us
    pallas_call x15, Pallas kernels, call(): pl.pallas_call(kernel, out_shape=[jax.ShapeDtypeStruct(shape, dtype) for...  54.8 us
    ppermute x24, starting transfers between devices, swap(): lax.ppermute(value, axis, [(index, index ^ bit) for index in range(size)])  24.4 us
    all_to_all x1, waiting for transfers between devices, shards(): recv = lax.all_to_all(totals, 'context', 0, 0, tiled=True)  16.2 us
    all_to_all x1, waiting for transfers between devices, shards(): recv = lax.all_to_all(in_grads, 'context', 0, 0, tiled=True)  15.2 us
    all_to_all x1, starting transfers between devices, shards(): x_mine = lax.all_to_all(spread, 'context', 0, 0, tiled=True)  8.46 us
    unnamed x68, local copies, waits for them, and re-layouts  6.63 us
    all_to_all x1, starting transfers between devices, shards(): recv = lax.all_to_all(in_grads, 'context', 0, 0, tiled=True)  4.94 us
  transfers between devices with their start and end apart: 31, of which 22 were waited for; matrix products, arithmetic and copies ran while one was open for 3% of the time, Pallas kernels for 18%

profile of v5, /device:TPU:0, one launch (start us, length us, event | category | flops | bytes accessed | tf_op | source)
XLA Modules:
  0.0 237.1 jit_solution(9710894912503001579)
XLA Ops:
  7.2 1.0 slice_select_fusion
  8.2 1.6 broadcast_in_dim.30
  9.8 8.5 %all-to-all-start = ((bf16[16,64,1024]{2,1,0:T(8,128)(2,1)}), bf16[16,64,1024]{2,1,0:T(8,128)(2,1)}, u32[]{:S(2)}, u32[]{:S(2)}) async-start(bf16[16,64,1024]{2,1,0:T(8,128)(2,1)} %broadcast_in_dim.30), calls=%async_computation | async-start | bytes 4194304 | tf_op jit(solution)/shard_map/all_to_all | solution.py:475
  18.4 1.6 collective-permute-start
  20.0 3.5 %collective-permute-done = bf16[128,512]{1,0:T(8,128)(2,1)S(1)} collective-permute-done((bf16[128,512]{1,0:T(8,128)(2,1)S(1)}, bf16[128,512]{1,0:T(8,128)(2,1)S(1)}, u32[]{:S(2)}, u32[]{:S(2)}) %collective-permute-start) | collective-permute-done | bytes 131104 | tf_op jit(solution)/shard_map/ppermute | solution.py:443
  23.5 1.5 collective-permute-start.1
  25.5 21.5 %collective-permute-done.2.wo_oth = bf16[256,512]{1,0:T(8,128)(2,1)} collective-permute-done((bf16[256,512]{1,0:T(8,128)(2,1)S(1)}, bf16[256,512]{1,0:T(8,128)(2,1)}, u32[]{:S(2)}, u32[]{:S(2)}) %collective-permute-start.2) | collective-permute-done | bytes 262176 | tf_op jit(solution)/shard_map/ppermute | solution.py:443
  47.0 3.6 %all-to-all-done.x_mine = bf16[16,64,1024]{2,1,0:T(8,128)(2,1)} async-done(((bf16[16,64,1024]{2,1,0:T(8,128)(2,1)}), bf16[16,64,1024]{2,1,0:T(8,128)(2,1)}, u32[]{:S(2)}, u32[]{:S(2)}) %all-to-all-start) | async-done | bytes 2097184 | tf_op jit(solution)/shard_map/all_to_all | solution.py:475
  50.6 1.3 copy.23.id_k
  52.0 0.7 pad_add_fusion.place
  52.6 2.5 %collective-permute-done.3.x_sib = bf16[16,64,1024]{2,1,0:T(8,128)(2,1)} collective-permute-done((bf16[16,64,1024]{2,1,0:T(8,128)(2,1)}, bf16[16,64,1024]{2,1,0:T(8,128)(2,1)}, u32[]{:S(2)}, u32[]{:S(2)}) %collective-permute-start.3) | collective-permute-done | bytes 2097184 | tf_op jit(solution)/shard_map/ppermute | solution.py:443
  55.8 10.4 %shard_map.203 = (bf16[128,256]{1,0:T(8,128)(2,1)}, bf16[16,2,64,256]{3,2,1,0:T(8,128)(2,1)}, bf16[16,2,64,256]{3,2,1,0:T(8,128)(2,1)}, f32[128,256]{1,0:T(8,128...) custom-call(s32[4]{0:T(128)} %pad_add_fusion.place, ...), custom_call_target="tpu_custom_call" | custom-call | flops 11000000512 | bytes 30000000 | tf_op jit(solution)/shard_map/pallas_call | solution.py:39
  66.3 1.4 collective-permute-done.4
  67.7 0.9 add_convert_fusion.2.chip
  68.7 3.1 %collective-permute-start.5 = (bf16[64,1024]{1,0:T(8,128)(2,1)S(1)}, bf16[64,1024]{1,0:T(8,128)(2,1)S(1)}, u32[]{:S(2)}, u32[]{:S(2)}) collective-permute-start(bf16[64,1024]{1,0:T(8,128)(2,1)S(1)} %add_convert_fusion.2.chip), channel_id=1, source_target_pairs={{0,2},{1,3},{2,0},{3,1},{4,6},{5,7},{6,4},{7,5},{8,10},{9,11},{10,... | collective-permute-start | bytes 393224 | tf_op jit(solution)/shard_map/ppermute | solution.py:443
  71.8 4.0 %collective-permute-done.5.recv = bf16[64,1024]{1,0:T(8,128)(2,1)S(1)} collective-permute-done((bf16[64,1024]{1,0:T(8,128)(2,1)S(1)}, bf16[64,1024]{1,0:T(8,128)(2,1)S(1)}, u32[]{:S(2)}, u32[]{:S(2)}) %collective-permute-start.5) | collective-permute-done | bytes 131104 | tf_op jit(solution)/shard_map/ppermute | solution.py:443
  75.8 0.8 shard_map.204
  76.6 0.7 copy-done.20
  77.3 1.3 collective-permute-done.6.hb_sib
  78.7 1.6 copy-done.7
  80.3 1.5 shard_map.205
  82.0 1.2 collective-permute-done.7
  83.2 3.1 %collective-permute-start.8 = (bf16[64,1024]{1,0:T(8,128)(2,1)S(1)}, bf16[64,1024]{1,0:T(8,128)(2,1)S(1)}, u32[]{:S(2)}, u32[]{:S(2)}) collective-permute-start(bf16[64,1024]{1,0:T(8,128)(2,1)S(1)} %add_convert_fusion.1.chip), channel_id=1, source_target_pairs={{0,2},{1,3},{2,0},{3,1},{4,6},{5,7},{6,4},{7,5},{8,10},{9,11},{10,... | collective-permute-start | bytes 393224 | tf_op jit(solution)/shard_map/ppermute | solution.py:443
  86.4 0.7 collective-permute-start.10
  87.0 4.1 %collective-permute-done.8.recv = bf16[64,1024]{1,0:T(8,128)(2,1)S(1)} collective-permute-done((bf16[64,1024]{1,0:T(8,128)(2,1)S(1)}, bf16[64,1024]{1,0:T(8,128)(2,1)S(1)}, u32[]{:S(2)}, u32[]{:S(2)}) %collective-permute-start.8) | collective-permute-done | bytes 131104 | tf_op jit(solution)/shard_map/ppermute | solution.py:443
  91.2 1.6 shard_map.206
  92.8 1.9 collective-permute-done.10.pair_ub
  94.7 2.1 shard_map.207
  96.9 1.3 collective-permute-done.11
  98.3 2.6 %collective-permute-start.12 = (bf16[64,1024]{1,0:T(8,128)(2,1)S(1)}, bf16[64,1024]{1,0:T(8,128)(2,1)S(1)}, u32[]{:S(2)}, u32[]{:S(2)}) collective-permute-start(bf16[64,1024]{1,0:T(8,128)(2,1)S(1)} %add_convert_fusion.chip), channel_id=1, source_target_pairs={{0,2},{1,3},{2,0},{3,1},{4,6},{5,7},{6,4},{7,5},{8,10},{9,11},{10,... | collective-permute-start | bytes 393224 | tf_op jit(solution)/shard_map/ppermute | solution.py:443
  100.8 4.6 %collective-permute-done.12.recv = bf16[64,1024]{1,0:T(8,128)(2,1)S(1)} collective-permute-done((bf16[64,1024]{1,0:T(8,128)(2,1)S(1)}, bf16[64,1024]{1,0:T(8,128)(2,1)S(1)}, u32[]{:S(2)}, u32[]{:S(2)}) %collective-permute-start.12) | collective-permute-done | bytes 131104 | tf_op jit(solution)/shard_map/ppermute | solution.py:443
  105.4 1.0 copy-done.23
  106.4 0.9 shard_map.208
  107.5 1.3 collective-permute-done.13.low_sib
  109.4 2.7 %shard_map.209 = (bf16[128,512]{1,0:T(8,128)(2,1)}, bf16[128,512]{1,0:T(8,128)(2,1)}, bf16[128,256]{1,0:T(8,128)(2,1)}, f32[1,512]{1,0:T(1,128)}, bf16[16,144,256]{2,1,0:T(8,128)(2,1)}) custom-call(s32[4]{0:T(128)} %pad_add_fusion.place, bf16[64,1024]{1,0:T(8,128)(2,1)} %copy-done.15, bf16[64,1024]{1,0:T(8,128)(2,1)} %copy-done.32, ...), custom_call_target="tpu_custom_call" | custom-call | flops 1650000000 | bytes 4500000 | tf_op jit(solution)/shard_map/pallas_call | solution.py:39
  112.1 4.0 %all-to-all-start.1 = ((bf16[16,144,256]{2,1,0:T(8,128)(2,1)}), bf16[16,144,256]{2,1,0:T(8,128)(2,1)S(1)}, u32[]{:S(2)}, u32[]{:S(2)}) async-start(bf16[16,144,256]{2,1,0:T(8,128)(2,1)} %get-tuple-element.93), calls=%async_computation.1 | async-start | bytes 2359296 | tf_op jit(solution)/shard_map/all_to_all | solution.py:546
  116.1 1.5 collective-permute-start.15
  118.3 1.5 collective-permute-start.14
  119.8 7.8 %shard_map.210.dq = bf16[128,256]{1,0:T(8,128)(2,1)} custom-call(s32[4]{0:T(128)} %pad_add_fusion.place, bf16[128,256]{1,0:T(8,128)(2,1)} %get-tuple-element.94.q, bf16[16,2,64,256]{3,2,1,0:T(8,128)(2,1)} %get-tuple-element.87.k, bf16[16,2,64,256]{3,2,1,0:T(8,128)(2,1)} %get-tuple-element.88.v, bf16[128,256]{1,0:T(8,128)(2,1)} %get-tuple-element.95.d_out, ...), custom_call_target="tpu_custom_call" | custom-call | flops 5500000256 | bytes 15000000 | tf_op jit(solution)/shard_map/pallas_call | solution.py:39
  128.2 3.3 %collective-permute-done.14.pair_late = bf16[128,768]{1,0:T(8,128)(2,1)S(1)} collective-permute-done((bf16[128,768]{1,0:T(8,128)(2,1)S(1)}, bf16[128,768]{1,0:T(8,128)(2,1)S(1)}, u32[]{:S(2)}, u32[]{:S(2)}) %collective-permute-start.14) | collective-permute-done | bytes 196640 | tf_op jit(solution)/shard_map/ppermute | solution.py:443
  131.5 2.6 %shard_map.211 = (bf16[16,256,256]{2,1,0:T(8,128)(2,1)}, f32[8,256]{1,0:T(8,128)S(1)}) custom-call(s32[4]{0:T(128)S(1)} %copy-done.5, bf16[64,1024]{1,0:T(8,128)(2,1)S(1)} %get-tuple-element.97.hb, bf16[64,1024]{1,0:T(8,128)(2,1)S(1)} %collective-permute-done.6.hb_sib, bf16[128,1024]{1,0:T(8,128)(2,1)S(1)} %copy-done.11, ...), custom_call_target="tpu_custom_call" | custom-call | flops 3300000000 | bytes 9000000 | tf_op jit(solution)/shard_map/pallas_call | solution.py:39
  134.1 1.9 all-to-all-done.1.recv
  136.0 1.0 copy-done.25
  137.0 4.9 %all-to-all-start.2 = ((bf16[16,256,256]{2,1,0:T(8,128)(2,1)}), bf16[16,256,256]{2,1,0:T(8,128)(2,1)S(1)}, u32[]{:S(2)}, u32[]{:S(2)}) async-start(bf16[16,256,256]{2,1,0:T(8,128)(2,1)} %get-tuple-element.113), calls=%async_computation.2 | async-start | bytes 4194304 | tf_op jit(solution)/shard_map/all_to_all | solution.py:561
  142.1 1.5 collective-permute-start.20
  143.6 13.6 %shard_map.212 = (bf16[128,768]{1,0:T(8,128)(2,1)}, bf16[64,1024]{1,0:T(8,128)(2,1)}, bf16[64,1024]{1,0:T(8,128)(2,1)}) custom-call(s32[4]{0:T(128)} %pad_add_fusion.place, bf16[16,64,1024]{2,1,0:T(8,128)(2,1)} %all-to-all-done.x_mine, bf16[16,64,1024]{2,1,0:T(8,128)(2,1)} %collective-permute-done.3.x_sib, bf16[2,256]{1,0:T(2,128)(2,1)} %bitcast.69, ...), custom_call_target="tpu_custom_call" | custom-call | flops 6600000000 | bytes 18000000 | tf_op jit(solution)/shard_map/pallas_call | solution.py:39
  157.8 1.5 collective-permute-start.21
  159.2 1.2 collective-permute-start.23
  160.4 5.6 %collective-permute-done.23 = f32[8,256]{1,0:T(8,128)S(1)} collective-permute-done((f32[8,256]{1,0:T(8,128)S(1)}, f32[8,256]{1,0:T(8,128)S(1)}, u32[]{:S(2)}, u32[]{:S(2)}) %collective-permute-start.23) | collective-permute-done | bytes 8224 | tf_op jit(solution)/shard_map/ppermute | solution.py:443
  166.1 0.9 copy-done.14
  167.0 2.0 shard_map.213
  169.1 2.4 %all-to-all-done.2.recv = bf16[16,256,256]{2,1,0:T(8,128)(2,1)S(1)} async-done(((bf16[16,256,256]{2,1,0:T(8,128)(2,1)}), bf16[16,256,256]{2,1,0:T(8,128)(2,1)S(1)}, u32[]{:S(2)}, u32[]{:S(2)}) %all-to-all-start.2) | async-done | bytes 2097184 | tf_op jit(solution)/shard_map/all_to_all | solution.py:561
  171.5 1.5 shard_map.214
  173.0 4.9 %all-to-all-start.3 = ((bf16[16,144,256]{2,1,0:T(8,128)(2,1)}), bf16[16,144,256]{2,1,0:T(8,128)(2,1)S(1)}, u32[]{:S(2)}, u32[]{:S(2)}) async-start(bf16[16,144,256]{2,1,0:T(8,128)(2,1)} %shard_map.213), calls=%async_computation.3 | async-start | bytes 2359296 | tf_op jit(solution)/shard_map/all_to_all | solution.py:581
  178.1 1.3 collective-permute-done.17
  179.4 2.3 collective-permute-start.18
  181.8 15.2 %all-to-all-done.3.recv = bf16[16,144,256]{2,1,0:T(8,128)(2,1)S(1)} async-done(((bf16[16,144,256]{2,1,0:T(8,128)(2,1)}), bf16[16,144,256]{2,1,0:T(8,128)(2,1)S(1)}, u32[]{:S(2)}, u32[]{:S(2)}) %all-to-all-start.3) | async-done | bytes 1179680 | tf_op jit(solution)/shard_map/all_to_all | solution.py:581
  197.0 1.7 shard_map.215
  198.7 3.7 %all-to-all-start.4 = ((bf16[16,128,256]{2,1,0:T(8,128)(2,1)}), bf16[16,128,256]{2,1,0:T(8,128)(2,1)S(1)}, u32[]{:S(2)}, u32[]{:S(2)}) async-start(bf16[16,128,256]{2,1,0:T(8,128)(2,1)} %get-tuple-element.117), calls=%async_computation.4 | async-start | bytes 2097152 | tf_op jit(solution)/shard_map/all_to_all | solution.py:588
  202.3 0.7 add_add_fusion
  204.8 16.2 %all-to-all-done.4.recv = bf16[16,128,256]{2,1,0:T(8,128)(2,1)S(1)} async-done(((bf16[16,128,256]{2,1,0:T(8,128)(2,1)}), bf16[16,128,256]{2,1,0:T(8,128)(2,1)S(1)}, u32[]{:S(2)}, u32[]{:S(2)}) %all-to-all-start.4) | async-done | bytes 1048608 | tf_op jit(solution)/shard_map/all_to_all | solution.py:588
  221.0 2.0 shard_map.216
  222.9 3.6 %all-gather.7.cloned.1.call-done = bf16[4096,256]{1,0:T(8,128)(2,1)} async-done(((bf16[256,256]{1,0:T(8,128)(2,1)}), bf16[4096,256]{1,0:T(8,128)(2,1)}) %all-gather.7.cloned.1.call-update) | async-done | bytes 2097168 | tf_op jit(solution)/shard_map/all_gather | solution.py:583
  226.5 3.8 %shard_map.217 = (f32[512,1024]{1,0:T(8,128)}, f32[1024,512]{1,0:T(8,128)}) custom-call(s32[4]{0:T(128)} %pad_add_fusion.place, bf16[16,256,256]{2,1,0:T(8,128)(2,1)} %bitcast.61), custom_call_target="tpu_custom_call" | custom-call | flops 2200000000 | bytes 6000000 | tf_op jit(solution)/shard_map/pallas_call | solution.py:39
  (113 shorter events, 6.5 us)
Async XLA Ops:
  9.8 8.5 %copy-start.2 = (bf16[1,512,1024]{2,1,0:T(8,128)(2,1)S(1)}, bf16[1,512,1024]{2,1,0:T(8,128)(2,1)}, u32[]{:S(2)}) copy-start(bf16[1,512,1024]{2,1,0:T(8,128)(2,1)} %param.17) | copy-start | bytes 3145732
  9.8 8.6 %copy-start.3 = (bf16[1,1024,512]{2,1,0:T(8,128)(2,1)S(1)}, bf16[1,1024,512]{2,1,0:T(8,128)(2,1)}, u32[]{:S(2)}) copy-start(bf16[1,1024,512]{2,1,0:T(8,128)(2,1)} %param.19) | copy-start | bytes 3145732
  9.8 13.7 %copy-start.29 = (bf16[1,512,3,256]{3,1,2,0:T(8,128)(2,1)S(1)}, bf16[1,512,3,256]{3,1,2,0:T(8,128)(2,1)}, u32[]{:S(2)}) copy-start(bf16[1,512,3,256]{3,1,2,0:T(8,128)(2,1)} %param.14) | copy-start | bytes 2359300
  9.8 15.2 %copy-start.30 = (bf16[1,256,512]{2,1,0:T(8,128)(2,1)S(1)}, bf16[1,256,512]{2,1,0:T(8,128)(2,1)}, u32[]{:S(2)}) copy-start(bf16[1,256,512]{2,1,0:T(8,128)(2,1)} %param.16) | copy-start | bytes 786436
  9.8 40.9 %copy-start.28 = (s32[2048]{0:T(1024)S(1)}, s32[2048]{0:T(1024)}, u32[]{:S(2)}) copy-start(s32[2048]{0:T(1024)} %param.13) | copy-start | bytes 24580
  9.8 40.8 %all-to-all-start = ((bf16[16,64,1024]{2,1,0:T(8,128)(2,1)}), bf16[16,64,1024]{2,1,0:T(8,128)(2,1)}, u32[]{:S(2)}, u32[]{:S(2)}) async-start(bf16[16,64,1024]{2,1,0:T(8,128)(2,1)} %broadcast_in_dim.30), calls=%async_computation | async-start | bytes 4194304 | tf_op jit(solution)/shard_map/all_to_all | solution.py:475
  18.3 59.1 %all-gather.5.cloned.1.call-start = ((), (), s32[]{:S(2)}) async-start(), calls=%async_computation.5 | async-start | bytes 2228224 | tf_op jit(solution)/shard_map/all_gather | solution.py:467
  18.4 5.0 %collective-permute-start = (bf16[128,512]{1,0:T(8,128)(2,1)S(1)}, bf16[128,512]{1,0:T(8,128)(2,1)S(1)}, u32[]{:S(2)}, u32[]{:S(2)}) collective-permute-start(bf16[128,512]{1,0:T(8,128)(2,1)S(1)} %pad_maximum_fusion.2), channel_id=1, source_target_pairs={{0,64},{64,0},{1,65},{65,1},{2,66},{66,2},{3,67},{67,3},{4,68},{68... | collective-permute-start | bytes 393224 | tf_op jit(solution)/shard_map/ppermute | solution.py:443
  23.4 2.0 copy-start.26
  23.5 23.6 %collective-permute-start.1 = (bf16[3,512,256]{2,1,0:T(8,128)(2,1)S(1)}, bf16[3,512,256]{2,1,0:T(8,128)(2,1)}, u32[]{:S(2)}, u32[]{:S(2)}) collective-permute-start(bf16[3,512,256]{2,1,0:T(8,128)(2,1)S(1)} %bitcast.64), channel_id=1, source_target_pairs={{0,64},{64,0},{1,65},{65,1},{2,66},{66,2},{3,67},{67,3},{4,68},{68... | collective-permute-start | bytes 2359304 | tf_op jit(solution)/shard_map/ppermute | solution.py:443
  24.9 22.1 %collective-permute-start.2 = (bf16[256,512]{1,0:T(8,128)(2,1)S(1)}, bf16[256,512]{1,0:T(8,128)(2,1)}, u32[]{:S(2)}, u32[]{:S(2)}) collective-permute-start(bf16[256,512]{1,0:T(8,128)(2,1)S(1)} %bitcast.67), channel_id=1, source_target_pairs={{0,64},{64,0},{1,65},{65,1},{2,66},{66,2},{3,67},{67,3},{4,68},{68... | collective-permute-start | bytes 786440 | tf_op jit(solution)/shard_map/ppermute | solution.py:443
  50.6 4.5 %collective-permute-start.3 = (bf16[16,64,1024]{2,1,0:T(8,128)(2,1)}, bf16[16,64,1024]{2,1,0:T(8,128)(2,1)}, u32[]{:S(2)}, u32[]{:S(2)}) collective-permute-start(bf16[16,64,1024]{2,1,0:T(8,128)(2,1)} %all-to-all-done.x_mine), channel_id=1, source_target_pairs={{0,1},{1,0},{2,3},{3,2},{4,5},{5,4},{6,7},{7,6},{8,9},{9,8},{10,11... | collective-permute-start | bytes 6291464 | tf_op jit(solution)/shard_map/ppermute | solution.py:443
  55.8 20.0 %copy-start = (bf16[128,1024]{1,0:T(8,128)(2,1)S(1)}, bf16[128,1024]{1,0:T(8,128)(2,1)}, u32[]{:S(2)}) copy-start(bf16[128,1024]{1,0:T(8,128)(2,1)} %tokens.5) | copy-start | bytes 786436
  55.8 20.0 %copy-start.4 = (s32[4]{0:T(128)S(1)}, s32[4]{0:T(128)}, u32[]{:S(2)}) copy-start(s32[4]{0:T(128)} %pad_add_fusion.place) | copy-start | bytes 52
  55.8 20.0 %copy-start.17 = (bf16[1,2,1024]{2,1,0:T(2,128)(2,1)S(1)}, bf16[1,2,1024]{2,1,0:T(2,128)(2,1)}, u32[]{:S(2)}) copy-start(bf16[1,2,1024]{2,1,0:T(2,128)(2,1)} %param.20) | copy-start | bytes 12292
  55.8 20.0 %copy-start.18 = (bf16[1,2,1024]{2,1,0:T(2,128)(2,1)S(1)}, bf16[1,2,1024]{2,1,0:T(2,128)(2,1)}, u32[]{:S(2)}) copy-start(bf16[1,2,1024]{2,1,0:T(2,128)(2,1)} %param.21) | copy-start | bytes 12292
  55.8 20.1 %copy-start.19 = (bf16[1,2,1024]{2,1,0:T(2,128)(2,1)S(1)}, bf16[1,2,1024]{2,1,0:T(2,128)(2,1)}, u32[]{:S(2)}) copy-start(bf16[1,2,1024]{2,1,0:T(2,128)(2,1)} %param.22) | copy-start | bytes 12292
  66.1 1.6 collective-permute-start.4
  68.6 10.0 %copy-start.16 = (bf16[1,1024]{1,0:T(2,128)(2,1)S(1)}, bf16[1,1024]{1,0:T(2,128)(2,1)}, u32[]{:S(2)}) copy-start(bf16[1,1024]{1,0:T(2,128)(2,1)} %b_up.1) | copy-start | bytes 6148
  68.7 7.1 %collective-permute-start.5 = (bf16[64,1024]{1,0:T(8,128)(2,1)S(1)}, bf16[64,1024]{1,0:T(8,128)(2,1)S(1)}, u32[]{:S(2)}, u32[]{:S(2)}) collective-permute-start(bf16[64,1024]{1,0:T(8,128)(2,1)S(1)} %add_convert_fusion.2.chip), channel_id=1, source_target_pairs={{0,2},{1,3},{2,0},{3,1},{4,6},{5,7},{6,4},{7,5},{8,10},{9,11},{10,... | collective-permute-start | bytes 393224 | tf_op jit(solution)/shard_map/ppermute | solution.py:443
  76.6 0.7 copy-start.20
  77.3 1.3 collective-permute-start.6
  78.7 1.6 copy-start.7
  80.3 10.9 %copy-start.9 = (f32[128,1024]{1,0:T(8,128)S(1)}, f32[128,1024]{1,0:T(8,128)}, u32[]{:S(2)}) copy-start(f32[128,1024]{1,0:T(8,128)} %cot.1) | copy-start | bytes 1572868
  80.3 10.9 %copy-start.21 = (f32[64,1024]{1,0:T(8,128)S(1)}, f32[64,1024]{1,0:T(8,128)}, u32[]{:S(2)}) copy-start(f32[64,1024]{1,0:T(8,128)} %copy-done.20) | copy-start | bytes 786436
  81.8 1.4 collective-permute-start.7
  83.2 7.9 %collective-permute-start.8 = (bf16[64,1024]{1,0:T(8,128)(2,1)S(1)}, bf16[64,1024]{1,0:T(8,128)(2,1)S(1)}, u32[]{:S(2)}, u32[]{:S(2)}) collective-permute-start(bf16[64,1024]{1,0:T(8,128)(2,1)S(1)} %add_convert_fusion.1.chip), channel_id=1, source_target_pairs={{0,2},{1,3},{2,0},{3,1},{4,6},{5,7},{6,4},{7,5},{8,10},{9,11},{10,... | collective-permute-start | bytes 393224 | tf_op jit(solution)/shard_map/ppermute | solution.py:443
  86.4 8.3 %collective-permute-start.10 = (bf16[128,768]{1,0:T(8,128)(2,1)S(1)}, bf16[128,768]{1,0:T(8,128)(2,1)S(1)}, u32[]{:S(2)}, u32[]{:S(2)}) collective-permute-start(bf16[128,768]{1,0:T(8,128)(2,1)S(1)} %slice.46), channel_id=1, source_target_pairs={{0,64},{64,0},{1,65},{65,1},{2,66},{66,2},{3,67},{67,3},{4,68},{68... | collective-permute-start | bytes 589832 | tf_op jit(solution)/shard_map/ppermute | solution.py:443
  91.2 3.5 %copy-start.8 = (bf16[2048,512]{1,0:T(8,128)(2,1)S(1)}, bf16[2048,512]{1,0:T(8,128)(2,1)}, u32[]{:S(2)}) copy-start(bf16[2048,512]{1,0:T(8,128)(2,1)} %all-gather.5.cloned.1.call-done) | copy-start | bytes 6291460
  92.8 4.0 %copy-start.22 = (f32[128,1024]{1,0:T(8,128)}, f32[128,1024]{1,0:T(8,128)S(1)}, u32[]{:S(2)}) copy-start(f32[128,1024]{1,0:T(8,128)S(1)} %get-tuple-element.78.dx) | copy-start | bytes 1572868
  92.8 1.9 collective-permute-start.9
  94.7 2.1 copy-start.12
  96.8 1.5 copy-start.10
  96.8 1.4 collective-permute-start.11
  98.3 7.1 %collective-permute-start.12 = (bf16[64,1024]{1,0:T(8,128)(2,1)S(1)}, bf16[64,1024]{1,0:T(8,128)(2,1)S(1)}, u32[]{:S(2)}, u32[]{:S(2)}) collective-permute-start(bf16[64,1024]{1,0:T(8,128)(2,1)S(1)} %add_convert_fusion.chip), channel_id=1, source_target_pairs={{0,2},{1,3},{2,0},{3,1},{4,6},{5,7},{6,4},{7,5},{8,10},{9,11},{10,... | collective-permute-start | bytes 393224 | tf_op jit(solution)/shard_map/ppermute | solution.py:443
  105.4 1.0 copy-start.23
  107.3 1.4 copy-start.15
  107.3 1.4 collective-permute-start.13
  108.8 0.7 copy-start.32
  112.1 5.5 %copy-start.11 = (bf16[128,1024]{1,0:T(8,128)(2,1)S(1)}, bf16[128,1024]{1,0:T(8,128)(2,1)}, u32[]{:S(2)}) copy-start(bf16[128,1024]{1,0:T(8,128)(2,1)} %copy-done.10) | copy-start | bytes 786436
  112.1 23.9 %all-to-all-start.1 = ((bf16[16,144,256]{2,1,0:T(8,128)(2,1)}), bf16[16,144,256]{2,1,0:T(8,128)(2,1)S(1)}, u32[]{:S(2)}, u32[]{:S(2)}) async-start(bf16[16,144,256]{2,1,0:T(8,128)(2,1)} %get-tuple-element.93), calls=%async_computation.1 | async-start | bytes 2359296 | tf_op jit(solution)/shard_map/all_to_all | solution.py:546
  116.1 11.5 %collective-permute-start.15 = (bf16[128,512]{1,0:T(8,128)(2,1)S(1)}, bf16[128,512]{1,0:T(8,128)(2,1)S(1)}, u32[]{:S(2)}, u32[]{:S(2)}) collective-permute-start(bf16[128,512]{1,0:T(8,128)(2,1)S(1)} %pad_maximum_fusion.3), channel_id=1, source_target_pairs={{0,64},{64,0},{1,65},{65,1},{2,66},{66,2},{3,67},{67,3},{4,68},{68... | collective-permute-start | bytes 393224 | tf_op jit(solution)/shard_map/ppermute | solution.py:443
  117.6 10.5 %collective-permute-start.16 = (bf16[128,1024]{1,0:T(8,128)(2,1)S(1)}, bf16[128,1024]{1,0:T(8,128)(2,1)S(1)}, u32[]{:S(2)}, u32[]{:S(2)}) collective-permute-start(bf16[128,1024]{1,0:T(8,128)(2,1)S(1)} %copy-done.11), channel_id=1, source_target_pairs={{0,64},{64,0},{1,65},{65,1},{2,66},{66,2},{3,67},{67,3},{4,68},{68... | collective-permute-start | bytes 786440 | tf_op jit(solution)/shard_map/ppermute | solution.py:443
  118.3 13.2 %collective-permute-start.14 = (bf16[128,768]{1,0:T(8,128)(2,1)S(1)}, bf16[128,768]{1,0:T(8,128)(2,1)S(1)}, u32[]{:S(2)}, u32[]{:S(2)}) collective-permute-start(bf16[128,768]{1,0:T(8,128)(2,1)S(1)} %pad_maximum_fusion), channel_id=1, source_target_pairs={{0,64},{64,0},{1,65},{65,1},{2,66},{66,2},{3,67},{67,3},{4,68},{68... | collective-permute-start | bytes 589832 | tf_op jit(solution)/shard_map/ppermute | solution.py:443
  119.8 11.7 %copy-start.5 = (s32[4]{0:T(128)S(1)}, s32[4]{0:T(128)}, u32[]{:S(2)}) copy-start(s32[4]{0:T(128)} %pad_add_fusion.place) | copy-start | bytes 52
  119.8 11.7 %copy-start.13 = (bf16[128,768]{1,0:T(8,128)(2,1)S(1)}, bf16[128,768]{1,0:T(8,128)(2,1)}, u32[]{:S(2)}) copy-start(bf16[128,768]{1,0:T(8,128)(2,1)} %copy-done.12) | copy-start | bytes 589828
  136.0 1.0 copy-start.25
  136.0 6.0 %copy-start.1 = (bf16[128,256]{1,0:T(8,128)(2,1)S(1)}, bf16[128,256]{1,0:T(8,128)(2,1)}, u32[]{:S(2)}) copy-start(bf16[128,256]{1,0:T(8,128)(2,1)} %get-tuple-element.108.ob) | copy-start | bytes 196612
  137.0 34.5 %all-to-all-start.2 = ((bf16[16,256,256]{2,1,0:T(8,128)(2,1)}), bf16[16,256,256]{2,1,0:T(8,128)(2,1)S(1)}, u32[]{:S(2)}, u32[]{:S(2)}) async-start(bf16[16,256,256]{2,1,0:T(8,128)(2,1)} %get-tuple-element.113), calls=%async_computation.2 | async-start | bytes 4194304 | tf_op jit(solution)/shard_map/all_to_all | solution.py:561
  142.0 84.6 %all-gather.7.cloned.1.call-start = ((), (), s32[]{:S(2)}) async-start(), calls=%async_computation.6 | async-start | bytes 2228224 | tf_op jit(solution)/shard_map/all_gather | solution.py:583
  142.1 24.0 %copy-start.6 = (s32[4]{0:T(128)S(1)}, s32[4]{0:T(128)}, u32[]{:S(2)}) copy-start(s32[4]{0:T(128)} %pad_add_fusion.place) | copy-start | bytes 52
  142.1 24.0 %copy-start.24 = (bf16[128,512]{1,0:T(8,128)(2,1)S(1)}, bf16[128,512]{1,0:T(8,128)(2,1)}, u32[]{:S(2)}) copy-start(bf16[128,512]{1,0:T(8,128)(2,1)} %get-tuple-element.109.low) | copy-start | bytes 393220
  142.1 24.0 %collective-permute-start.20 = (bf16[128,768]{1,0:T(8,128)(2,1)S(1)}, bf16[128,768]{1,0:T(8,128)(2,1)S(1)}, u32[]{:S(2)}, u32[]{:S(2)}) collective-permute-start(bf16[128,768]{1,0:T(8,128)(2,1)S(1)} %pad_maximum_fusion.1), channel_id=1, source_target_pairs={{0,64},{64,0},{1,65},{65,1},{2,66},{66,2},{3,67},{67,3},{4,68},{68... | collective-permute-start | bytes 589832 | tf_op jit(solution)/shard_map/ppermute | solution.py:443
  157.2 8.9 %collective-permute-start.19 = (bf16[128,768]{1,0:T(8,128)(2,1)}, bf16[128,768]{1,0:T(8,128)(2,1)S(1)}, u32[]{:S(2)}, u32[]{:S(2)}) collective-permute-start(bf16[128,768]{1,0:T(8,128)(2,1)} %get-tuple-element.107.d), channel_id=1, source_target_pairs={{0,64},{64,0},{1,65},{65,1},{2,66},{66,2},{3,67},{67,3},{4,68},{68... | collective-permute-start | bytes 589832 | tf_op jit(solution)/shard_map/ppermute | solution.py:443
  157.8 1.5 collective-permute-start.22
  157.8 8.3 %collective-permute-start.21 = (bf16[128,512]{1,0:T(8,128)(2,1)}, bf16[128,512]{1,0:T(8,128)(2,1)S(1)}, u32[]{:S(2)}, u32[]{:S(2)}) collective-permute-start(bf16[128,512]{1,0:T(8,128)(2,1)} %get-tuple-element.110), channel_id=1, source_target_pairs={{0,64},{64,0},{1,65},{65,1},{2,66},{66,2},{3,67},{67,3},{4,68},{68... | collective-permute-start | bytes 393224 | tf_op jit(solution)/shard_map/ppermute | solution.py:443
  159.2 6.8 %collective-permute-start.23 = (f32[8,256]{1,0:T(8,128)S(1)}, f32[8,256]{1,0:T(8,128)S(1)}, u32[]{:S(2)}, u32[]{:S(2)}) collective-permute-start(f32[8,256]{1,0:T(8,128)S(1)} %dynamic-slice_add_fusion), channel_id=1, source_target_pairs={{0,64},{64,0},{1,65},{65,1},{2,66},{66,2},{3,67},{67,3},{4,68},{68... | collective-permute-start | bytes 24584 | tf_op jit(solution)/shard_map/ppermute | solution.py:443
  166.1 0.9 copy-start.14
  173.0 5.0 %copy-start.31 = (bf16[64,1024]{1,0:T(8,128)(2,1)S(1)}, bf16[64,1024]{1,0:T(8,128)(2,1)}, u32[]{:S(2)}) copy-start(bf16[64,1024]{1,0:T(8,128)(2,1)} %get-tuple-element.106) | copy-start | bytes 393220
  173.0 6.4 %copy-start.27 = (bf16[64,1024]{1,0:T(8,128)(2,1)S(1)}, bf16[64,1024]{1,0:T(8,128)(2,1)}, u32[]{:S(2)}) copy-start(bf16[64,1024]{1,0:T(8,128)(2,1)} %get-tuple-element.105) | copy-start | bytes 393220
  173.0 24.0 %all-to-all-start.3 = ((bf16[16,144,256]{2,1,0:T(8,128)(2,1)}), bf16[16,144,256]{2,1,0:T(8,128)(2,1)S(1)}, u32[]{:S(2)}, u32[]{:S(2)}) async-start(bf16[16,144,256]{2,1,0:T(8,128)(2,1)} %shard_map.213), calls=%async_computation.3 | async-start | bytes 2359296 | tf_op jit(solution)/shard_map/all_to_all | solution.py:581
  177.9 1.4 collective-permute-start.17
  179.4 22.9 %collective-permute-start.18 = (bf16[32,1024]{1,0:T(8,128)(2,1)S(1)}, bf16[32,1024]{1,0:T(8,128)(2,1)S(1)}, u32[]{:S(2)}, u32[]{:S(2)}) collective-permute-start(bf16[32,1024]{1,0:T(8,128)(2,1)S(1)} %dynamic-slice_convert_fusion), channel_id=1, source_target_pairs={{0,2},{1,3},{2,0},{3,1},{4,6},{5,7},{6,4},{7,5},{8,10},{9,11},{10,... | collective-permute-start | bytes 196616 | tf_op jit(solution)/shard_map/ppermute | solution.py:443
  198.7 22.3 %all-to-all-start.4 = ((bf16[16,128,256]{2,1,0:T(8,128)(2,1)}), bf16[16,128,256]{2,1,0:T(8,128)(2,1)S(1)}, u32[]{:S(2)}, u32[]{:S(2)}) async-start(bf16[16,128,256]{2,1,0:T(8,128)(2,1)} %get-tuple-element.117), calls=%async_computation.4 | async-start | bytes 2097152 | tf_op jit(solution)/shard_map/all_to_all | solution.py:588
Sparse Core Ops, SparseCore 0:
  25.6 51.2 all-gather.4
  173.1 53.3 all-gather.6
